TPU v7x, 32 devices: a whole 2x2x4 slice. The times are simulated.
32 devices in a mesh: groups: 2 (over x), member: 2 (over core), tile: 8 (over z, y).
Axes of the slice: x: 2, y: 2, z: 4, core: 2. Of those that a mesh axis runs over, the one named last changes fastest.
Arguments:
- state: float32 [8, 4, 4, 512, 256], P(('groups', 'member'), None, None, 'tile'), parts along dimension 0, may hold values from -6 to 6
- perturbation: float32 [8, 4, 4, 512, 256], P(('groups', 'member'), None, None, 'tile'), parts along dimension 0, may hold values from -2 to 2
- ancestors: int32 [8], P('groups'), parts along dimension 0, may hold values from 0 to 3, as said below
Outputs:
- evolved: float32 [8, 4, 4, 512, 256], P(('groups', 'member'), None, None, 'tile'), parts along dimension 0
- observable: float32 [8], P(('groups', 'member')), parts along dimension 0
There are 2 independent parts, one for each index of `groups`. A program takes and returns all parts, laid end to end along the dimension named above; each array names one. Nothing has to cross between parts.
Inputs may be any that keep to these rules, and one draw needn't show every extreme that they name: `ancestors`: surviving slots name themselves; every other slot names a surviving slot; at least two slots survive and at least one does not.
All inputs are finite; a program needn't handle non-finite values.
Results may differ from a plain program's by a relative error of at most 0.00002.
Values sent between devices are 32-bit elements; how exact they have to be, the bound alone decides.
No kernel may reach another device: no remote copies, remote signals or barrier semaphores. Data moves between devices by JAX's collectives and lax.ppermute only.
A program may use at most 64 MiB of HBM per device.

v0:
```python
import jax
import jax.numpy as jnp
from jax import lax
from jax.sharding import PartitionSpec as P

STEPS_EACH = 2


TIME_STEP = 0.15
DIFFUSION = 0.2
MIXING = 0.1
CORIOLIS = 0.5
BUOYANCY_GAIN = 0.3
STRATIFICATION = 0.3
SATURATION = 0.5
LATENT = 0.5


def extended(cells, sides, width):
    for axis, dim in sides:
        count = lax.axis_size(axis)
        ends = count - 1
        head = lax.slice_in_dim(cells, 0, width, axis=dim)
        tail = lax.slice_in_dim(cells, cells.shape[dim] - width, cells.shape[dim], axis=dim)
        cells = jnp.concatenate(
            [
                lax.ppermute(tail, axis, [(i, (i + 1) % count) for i in range(ends)]),
                cells,
                lax.ppermute(head, axis, [((i + 1) % count, i) for i in range(ends)]),
            ],
            axis=dim,
        )
    return cells


def advance_core(padded):
    centre = padded[:, :, :, 2:-2, :]
    north_one = padded[:, :, :, 3:-1, :]
    south_one = padded[:, :, :, 1:-3, :]
    north_two = padded[:, :, :, 4:, :]
    south_two = padded[:, :, :, :-4, :]
    east_one = jnp.roll(centre, -1, axis=4)
    west_one = jnp.roll(centre, 1, axis=4)
    east_two = jnp.roll(centre, -2, axis=4)
    west_two = jnp.roll(centre, 2, axis=4)
    slope_y = (8.0 * (north_one - south_one) - (north_two - south_two)) / 12.0
    slope_x = (8.0 * (east_one - west_one) - (east_two - west_two)) / 12.0
    laplace = north_one + south_one + east_one + west_one - 4.0 * centre
    upper = jnp.concatenate([centre[:, :, 1:], centre[:, :, -1:]], axis=2)
    lower = jnp.concatenate([centre[:, :, :1], centre[:, :, :-1]], axis=2)
    vertical = upper + lower - 2.0 * centre
    east_wind = centre[:, 0:1]
    north_wind = centre[:, 1:2]
    buoyancy = centre[:, 2:3]
    tendency = (
        -(east_wind * slope_x + north_wind * slope_y) + DIFFUSION * laplace + MIXING * vertical
    )
    forcing = jnp.concatenate(
        [
            CORIOLIS * north_wind,
            -CORIOLIS * east_wind + BUOYANCY_GAIN * buoyancy,
            -STRATIFICATION * north_wind,
            jnp.zeros_like(north_wind),
        ],
        axis=1,
    )
    updated = centre + TIME_STEP * (tendency + forcing)
    buoyancy_new = updated[:, 2:3]
    moisture = updated[:, 3:4]
    excess = jnp.maximum(moisture - SATURATION * jnp.exp(0.1 * buoyancy_new), 0.0)
    return jnp.concatenate(
        [updated[:, 0:2], buoyancy_new + LATENT * excess, moisture - excess], axis=1
    )


def advance_all(fields):
    for number in range(STEPS_EACH):
        padded = extended(fields, (("tile", 3),), 2)
        fields = advance_core(padded)
    return fields


def body(state, perturbation, ancestors):
    count_dev = state.shape[0]
    owner = lax.axis_index("member")
    fields = advance_all(state)
    member_count = lax.axis_size("member")
    slot_source = ancestors - owner * count_dev
    mine = (slot_source >= 0) & (slot_source < count_dev)
    outgoing = jnp.take(fields, jnp.clip(slot_source, 0, count_dev - 1), axis=0)
    outgoing = jnp.where(mine[:, None, None, None, None], outgoing, 0.0)
    incoming = lax.all_to_all(outgoing, "member", split_axis=0, concat_axis=0, tiled=True)
    cloned = jnp.sum(incoming.reshape((member_count, count_dev) + fields.shape[1:]), axis=0)
    fields = advance_all(cloned + perturbation)
    rows_here = fields.shape[3]
    total_rows = rows_here * lax.axis_size("tile")
    latitude = (lax.axis_index("tile") * rows_here + jnp.arange(rows_here, dtype=jnp.int32)).astype(
        jnp.float32
    )
    weight = 1.0 + 2.0 * latitude / (total_rows - 1)
    buoyancy = fields[:, 2]
    partial_total = jnp.sum(weight[:, None] * buoyancy * buoyancy, axis=(1, 2, 3))
    total = lax.psum(partial_total, "tile")
    observable = total / (fields.shape[2] * total_rows * fields.shape[4])
    return (fields, observable)


def solution(mesh):
    return jax.shard_map(
        body,
        mesh=mesh,
        in_specs=(
            P(("groups", "member"), None, None, "tile", None),
            P(("groups", "member"), None, None, "tile", None),
            P("groups"),
        ),
        out_specs=(P(("groups", "member"), None, None, "tile", None), P(("groups", "member"))),
        check_vma=False,
    )
```

profile of v0, /device:TPU:0, one launch (start us, length us, event | category | flops | bytes accessed | tf_op | source)
XLA Modules:
  0.0 146.0 jit_solution(2485772114257159055)
XLA Ops:
  1.7 1.3 collective-permute-start
  3.0 5.6 %collective-permute-start.1 = (f32[2,4,4,2,256]{4,3,2,1,0:T(2,128)S(1)}, f32[2,4,4,2,256]{4,3,2,1,0:T(2,128)S(1)}, u32[]{:S(2)}, u32[]{:S(2)}) collective-permute-start(f32[2,4,4,2,256]{4,3,2,1,0:T(2,128)S(1)} %get-tuple-element.95), channel_id=1, source_target_pairs={{0,1},{1,2},{2,3},{3,4},{4,5},{5,6},{6,7},{8,9},{9,10},{10,11},{11... | collective-permute-start | bytes 196616 | tf_op jit(solution)/shard_map/ppermute | solution.py:27
  8.7 2.9 %multiply_bitcast_fusion.7 = (f32[2,4,64,256]{3,2,1,0:T(8,128)}, f32[2,1,4,64,256]{4,3,2,1,0:T(8,128)}, f32[2,1,4,64,256]{4,3,2,1,0:T(8,128)}, f32[2,4,64,256]{3,2,1,0:T(8,128)}, f32[2,1,4,64,256]{4,3,2,1,0:T(8,128)}) fusion(f32[2,4,4,64,256]{4,3,2,1,0:T(8,128)} %param.3), kind=kLoop, calls=%fused_computation.124 | loop fusion | flops 917504 | bytes 4194304 | tf_op jit(solution)/shard_map/mul | solution.py:56
  11.6 1.5 %constant_dynamic-update-slice_fusion.1 = f32[2,4,4,66,256]{4,3,2,1,0:T(8,128)} fusion(f32[2,4,4,64,256]{4,3,2,1,0:T(8,128)S(1)} %copy-done), kind=kLoop, calls=%fused_computation.135 | loop fusion | bytes 4194304
  13.2 2.8 %fusion.84 = (f32[2,4,4,64,255]{4,3,2,1,0:T(8,128)}, f32[2,4,4,64,255]{4,3,2,1,0:T(8,128)}) fusion(f32[2,4,4,64,256]{4,3,2,1,0:T(8,128)S(1)} %copy-done), kind=kLoop, calls=%fused_computation.162 | loop fusion | bytes 8355840 | tf_op jit(solution)/shard_map/jit(_roll_static)/slice | solution.py:42
  16.0 2.8 %fusion.89 = (f32[2,4,4,64,254]{4,3,2,1,0:T(8,128)}, f32[2,4,4,64,254]{4,3,2,1,0:T(8,128)}) fusion(f32[2,4,4,64,256]{4,3,2,1,0:T(8,128)S(1)} %copy-done), kind=kLoop, calls=%fused_computation.167 | loop fusion | bytes 8323072 | tf_op jit(solution)/shard_map/jit(_roll_static)/slice | solution.py:45
  18.7 2.1 %fusion.87 = (f32[2,4,3,64,256]{4,3,2,1,0:T(8,128)}, f32[2,4,3,64,256]{4,3,2,1,0:T(8,128)}) fusion(f32[2,4,4,64,256]{4,3,2,1,0:T(8,128)S(1)} %copy-done), kind=kLoop, calls=%fused_computation.165 | loop fusion | bytes 6291456 | tf_op jit(solution)/shard_map/slice | solution.py:50
  20.8 1.7 %fusion.85 = (f32[2,4,4,64,1]{4,3,2,1,0:T(8,128)}, f32[2,4,4,64,1]{4,3,2,1,0:T(8,128)}) fusion(f32[2,4,4,64,256]{4,3,2,1,0:T(8,128)S(1)} %copy-done), kind=kLoop, calls=%fused_computation.163 | loop fusion | bytes 32768 | tf_op jit(solution)/shard_map/jit(_roll_static)/slice | solution.py:42
  22.5 1.7 %fusion.88 = (f32[2,4,4,64,2]{4,3,2,1,0:T(8,128)}, f32[2,4,4,64,2]{4,3,2,1,0:T(8,128)}) fusion(f32[2,4,4,64,256]{4,3,2,1,0:T(8,128)S(1)} %copy-done), kind=kLoop, calls=%fused_computation.166 | loop fusion | bytes 65536 | tf_op jit(solution)/shard_map/jit(_roll_static)/slice | solution.py:45
  25.9 9.7 %fusion.5 = f32[2,4,4,64,256]{4,3,2,1,0:T(8,128)S(1)} fusion(f32[2,4,4,64,256]{4,3,2,1,0:T(8,128)S(1)} %copy-done, f32[2,1,4,64,256]{4,3,2,1,0:T(8,128)S(1)} %broadcast.118, f32[2,4,4,2,256]{4,3,2,1,0:T(2,128)S(1)} %collective-permute-done.1, f32[2,4,4,66,256]{4,3,2,1,0:T(8,128)} %constant_dynamic-update-slice_fusion, ...), kind=kLoop, calls=%fused_computation.21 | loop fusion | flops 19922944 | bytes 24182784 | tf_op jit(solution)/shard_map/add | solution.py:67
  35.6 1.6 %multiply_bitcast_fusion.5 = (f32[2,4,64,256]{3,2,1,0:T(8,128)}, f32[2,1,4,64,256]{4,3,2,1,0:T(8,128)}, f32[2,1,4,64,256]{4,3,2,1,0:T(8,128)}, f32[2,1,4,64,256]...) fusion(f32[2,4,4,64,256]{4,3,2,1,0:T(8,128)S(1)} %fusion.5), kind=kLoop, calls=%fused_computation.118 | loop fusion | flops 1835008 | bytes 5767168 | tf_op jit(solution)/shard_map/mul | solution.py:56
  39.6 1.7 %fusion.78 = (f32[2,4,4,64,1]{4,3,2,1,0:T(8,128)}, f32[2,4,4,64,1]{4,3,2,1,0:T(8,128)}) fusion(f32[2,4,4,64,256]{4,3,2,1,0:T(8,128)S(1)} %pad_maximum_fusion.11), kind=kLoop, calls=%fused_computation.156 | loop fusion | bytes 32768 | tf_op jit(solution)/shard_map/jit(_roll_static)/slice | solution.py:42
  41.3 1.7 %fusion.81 = (f32[2,4,4,64,2]{4,3,2,1,0:T(8,128)}, f32[2,4,4,64,2]{4,3,2,1,0:T(8,128)}) fusion(f32[2,4,4,64,256]{4,3,2,1,0:T(8,128)S(1)} %pad_maximum_fusion.11), kind=kLoop, calls=%fused_computation.159 | loop fusion | bytes 65536 | tf_op jit(solution)/shard_map/jit(_roll_static)/slice | solution.py:45
  44.2 5.4 %collective-permute-start.3 = (f32[2,4,4,2,256]{4,3,2,1,0:T(2,128)S(1)}, f32[2,4,4,2,256]{4,3,2,1,0:T(2,128)S(1)}, u32[]{:S(2)}, u32[]{:S(2)}) collective-permute-start(f32[2,4,4,2,256]{4,3,2,1,0:T(2,128)S(1)} %get-tuple-element.76), channel_id=1, source_target_pairs={{0,1},{1,2},{2,3},{3,4},{4,5},{5,6},{6,7},{8,9},{9,10},{10,11},{11... | collective-permute-start | bytes 196616 | tf_op jit(solution)/shard_map/ppermute | solution.py:27
  52.1 5.7 %fusion.8 = f32[2,4,4,64,256]{4,3,2,1,0:T(8,128)S(1)} fusion(f32[2,1,4,64,256]{4,3,2,1,0:T(8,128)S(1)} %broadcast.118, f32[2,4,4,66,256]{4,3,2,1,0:T(8,128)S(1)} %get-tuple-element.74, f32[2,4,4,66,256]{4,3,2,1,0:T(8,128)S(1)} %get-tuple-element.73, f32[2,4,4,64,2]{4,3,2,1,0:T(8,128)} %get-tuple-element.70, f32[2,4,4,64,254]{4,3,2,1,0:T(8,128)S(1)} %get-tuple-element.72, ...), kind=kLoop, calls=%fused_computation.24 | loop fusion | flops 19922944 | bytes 28311552 | tf_op jit(solution)/shard_map/add | solution.py:67
  58.4 2.8 %gather_fusion = f32[4,4,4,64,256]{4,3,2,1,0:T(8,128)} fusion(f32[2,4,4,64,256]{4,3,2,1,0:T(8,128)S(1)} %pad_maximum_fusion.14, s32[1024]{0:T(1024)S(1)} %pad_clamp_fusion), kind=kCustom, calls=%fused_computation | custom fusion | bytes 8388624 | tf_op jit(solution)/shard_map/jit(_take)/gather | solution.py:90
  61.2 2.7 %select_select_fusion = f32[4,4,4,64,256]{4,3,2,1,0:T(8,128)S(1)} fusion(f32[4,4,4,64,256]{4,3,2,1,0:T(8,128)} %gather_fusion, pred[4]{0:T(512)(128)(4,1)S(1)} %get-tuple-element.6, pred[4]{0:T(512)(128)(4,1)S(1)} %get-tuple-element.96), kind=kLoop, calls=%fused_computation.5 | loop fusion | flops 2097152 | bytes 8388616 | tf_op jit(solution)/shard_map/jit(_where)/select_n | solution.py:91
  63.9 8.2 %all_to_all.5 = f32[4,4,4,64,256]{4,3,2,1,0:T(8,128)} all-to-all(f32[4,4,4,64,256]{4,3,2,1,0:T(8,128)S(1)} %select_select_fusion), channel_id=1, replica_groups=mesh['groups'=2,'member'=2,'tile'=8] {'member'}, dimensions={0} | all-to-all | bytes 8388608 | tf_op jit(solution)/shard_map/all_to_all | solution.py:92
  72.1 2.7 %reduce_sum.18 = f32[2,4,4,64,256]{4,3,2,1,0:T(8,128)S(1)} reduce(f32[2,2,4,4,64,256]{5,4,3,2,1,0:T(8,128)} %bitcast.19, f32[]{:T(128)} %constant.68.clone.1), dimensions={0}, to_apply=%region_0.1 | reduce | flops 524288 | bytes 6291460 | tf_op jit(solution)/shard_map/reduce_sum | solution.py:93
  74.8 1.9 %add.184 = f32[2,4,4,64,256]{4,3,2,1,0:T(8,128)S(1)} add(f32[2,4,4,64,256]{4,3,2,1,0:T(8,128)S(1)} %reduce_sum.18, f32[2,4,4,64,256]{4,3,2,1,0:T(8,128)} %param.4) | non-fusion elementwise | flops 524288 | bytes 6291456 | tf_op jit(solution)/shard_map/add | solution.py:94
  78.6 1.5 %multiply_bitcast_fusion.3 = (f32[2,4,64,256]{3,2,1,0:T(8,128)}, f32[2,1,4,64,256]{4,3,2,1,0:T(8,128)}, f32[2,1,4,64,256]{4,3,2,1,0:T(8,128)}, f32[2,1,4,64,256]{4,3,2,1,0:T(8,128)}, f32[2,4,64,256]{3,2,1,0:T(8,128)}) fusion(f32[2,4,4,64,256]{4,3,2,1,0:T(8,128)S(1)} %add.184), kind=kLoop, calls=%fused_computation.112 | loop fusion | flops 917504 | bytes 4194304 | tf_op jit(solution)/shard_map/mul | solution.py:56
  80.9 1.3 collective-permute-start.4
  82.2 5.4 %collective-permute-start.5 = (f32[2,4,4,2,256]{4,3,2,1,0:T(2,128)S(1)}, f32[2,4,4,2,256]{4,3,2,1,0:T(2,128)S(1)}, u32[]{:S(2)}, u32[]{:S(2)}) collective-permute-start(f32[2,4,4,2,256]{4,3,2,1,0:T(2,128)S(1)} %get-tuple-element.51), channel_id=1, source_target_pairs={{0,1},{1,2},{2,3},{3,4},{4,5},{5,6},{6,7},{8,9},{9,10},{10,11},{11... | collective-permute-start | bytes 196616 | tf_op jit(solution)/shard_map/ppermute | solution.py:27
  88.6 1.8 %collective-permute-done.5 = f32[2,4,4,2,256]{4,3,2,1,0:T(2,128)S(1)} collective-permute-done((f32[2,4,4,2,256]{4,3,2,1,0:T(2,128)S(1)}, f32[2,4,4,2,256]{4,3,2,1,0:T(2,128)S(1)}, u32[]{:S(2)}, u32[]{:S(2)}) %collective-permute-start.5) | collective-permute-done | bytes 65568 | tf_op jit(solution)/shard_map/ppermute | solution.py:27
  91.0 5.9 %fusion.11 = f32[2,4,4,64,256]{4,3,2,1,0:T(8,128)S(1)} fusion(f32[2,4,4,64,256]{4,3,2,1,0:T(8,128)S(1)} %add.184, f32[2,1,4,64,256]{4,3,2,1,0:T(8,128)S(1)} %broadcast.118, f32[2,4,4,2,256]{4,3,2,1,0:T(2,128)} %copy-done.2, f32[2,4,4,2,256]{4,3,2,1,0:T(2,128)} %copy-done.1, f32[2,4,4,64,2]{4,3,2,1,0:T(8,128)S(1)} %get-tuple-element.47, ...), kind=kLoop, calls=%fused_computation.27 | loop fusion | flops 20971520 | bytes 20054016 | tf_op jit(solution)/shard_map/add | solution.py:67
  96.9 1.6 %multiply_bitcast_fusion.1 = (f32[2,4,64,256]{3,2,1,0:T(8,128)}, f32[2,1,4,64,256]{4,3,2,1,0:T(8,128)}, f32[2,1,4,64,256]{4,3,2,1,0:T(8,128)}, f32[2,1,4,64,256]...) fusion(f32[2,4,4,64,256]{4,3,2,1,0:T(8,128)S(1)} %fusion.11), kind=kLoop, calls=%fused_computation.107 | loop fusion | flops 1835008 | bytes 5767168 | tf_op jit(solution)/shard_map/mul | solution.py:56
  100.9 1.7 %fusion.64 = (f32[2,4,4,64,1]{4,3,2,1,0:T(8,128)}, f32[2,4,4,64,1]{4,3,2,1,0:T(8,128)}) fusion(f32[2,4,4,64,256]{4,3,2,1,0:T(8,128)S(1)} %pad_maximum_fusion.17), kind=kLoop, calls=%fused_computation.142 | loop fusion | bytes 32768 | tf_op jit(solution)/shard_map/jit(_roll_static)/slice | solution.py:42
  102.6 1.7 %fusion.67 = (f32[2,4,4,64,2]{4,3,2,1,0:T(8,128)}, f32[2,4,4,64,2]{4,3,2,1,0:T(8,128)}) fusion(f32[2,4,4,64,256]{4,3,2,1,0:T(8,128)S(1)} %pad_maximum_fusion.17), kind=kLoop, calls=%fused_computation.145 | loop fusion | bytes 65536 | tf_op jit(solution)/shard_map/jit(_roll_static)/slice | solution.py:45
  105.5 5.0 %collective-permute-start.7 = (f32[2,4,4,2,256]{4,3,2,1,0:T(2,128)S(1)}, f32[2,4,4,2,256]{4,3,2,1,0:T(2,128)S(1)}, u32[]{:S(2)}, u32[]{:S(2)}) collective-permute-start(f32[2,4,4,2,256]{4,3,2,1,0:T(2,128)S(1)} %get-tuple-element.32), channel_id=1, source_target_pairs={{0,1},{1,2},{2,3},{3,4},{4,5},{5,6},{6,7},{8,9},{9,10},{10,11},{11... | collective-permute-start | bytes 196616 | tf_op jit(solution)/shard_map/ppermute | solution.py:27
  113.3 5.7 %fusion.14 = f32[2,4,4,64,256]{4,3,2,1,0:T(8,128)S(1)} fusion(f32[2,1,4,64,256]{4,3,2,1,0:T(8,128)S(1)} %broadcast.118, f32[2,4,4,66,256]{4,3,2,1,0:T(8,128)S(1)} %get-tuple-element.30, f32[2,4,4,66,256]{4,3,2,1,0:T(8,128)S(1)} %get-tuple-element.29, f32[2,4,4,64,2]{4,3,2,1,0:T(8,128)} %get-tuple-element.26, f32[2,4,4,64,254]{4,3,2,1,0:T(8,128)S(1)} %get-tuple-element.28, ...), kind=kLoop, calls=%fused_computation.30 | loop fusion | flops 19922944 | bytes 28311552 | tf_op jit(solution)/shard_map/add | solution.py:67
  119.6 24.4 %psum.7 = f32[2]{0:T(128)S(1)} all-reduce(f32[2]{0:T(128)S(1)} %get-tuple-element.2), channel_id=1, replica_groups=mesh['groups'=2,'member'=2,'tile'=8] {'tile'}, use_global_device_ids=true, to_apply=%region_2.3 | all-reduce | flops 2 | bytes 16 | tf_op jit(solution)/shard_map/psum | solution.py:103
  144.5 1.5 %pad_maximum_fusion.20 = f32[2,4,4,64,256]{4,3,2,1,0:T(8,128)} fusion(f32[2,1,4,64,256]{4,3,2,1,0:T(8,128)S(1)} %fusion.59, f32[2,1,4,64,256]{4,3,2,1,0:T(8,128)S(1)} %get-tuple-element.3, f32[2,2,4,64,256]{4,3,2,1,0:T(8,128)S(1)} %slice.480), kind=kLoop, calls=%fused_computation.97 | loop fusion | flops 1048576 | bytes 4194304 | tf_op jit(solution)/shard_map/concatenate | solution.py:71
  (54 shorter events, 20.9 us)
Async XLA Ops:
  1.7 23.4 %collective-permute-start = (f32[2,4,4,2,256]{4,3,2,1,0:T(2,128)S(1)}, f32[2,4,4,2,256]{4,3,2,1,0:T(2,128)S(1)}, u32[]{:S(2)}, u32[]{:S(2)}) collective-permute-start(f32[2,4,4,2,256]{4,3,2,1,0:T(2,128)S(1)} %get-tuple-element.94), channel_id=1, source_target_pairs={{1,0},{2,1},{3,2},{4,3},{5,4},{6,5},{7,6},{9,8},{10,9},{11,10},{12... | collective-permute-start | bytes 196616 | tf_op jit(solution)/shard_map/ppermute | solution.py:29
  3.0 8.6 %copy-start = (f32[2,4,4,64,256]{4,3,2,1,0:T(8,128)S(1)}, f32[2,4,4,64,256]{4,3,2,1,0:T(8,128)}, u32[]{:S(2)}) copy-start(f32[2,4,4,64,256]{4,3,2,1,0:T(8,128)} %param.3) | copy-start | bytes 6291460
  3.0 22.8 %collective-permute-start.1 = (f32[2,4,4,2,256]{4,3,2,1,0:T(2,128)S(1)}, f32[2,4,4,2,256]{4,3,2,1,0:T(2,128)S(1)}, u32[]{:S(2)}, u32[]{:S(2)}) collective-permute-start(f32[2,4,4,2,256]{4,3,2,1,0:T(2,128)S(1)} %get-tuple-element.95), channel_id=1, source_target_pairs={{0,1},{1,2},{2,3},{3,4},{4,5},{5,6},{6,7},{8,9},{9,10},{10,11},{11... | collective-permute-start | bytes 196616 | tf_op jit(solution)/shard_map/ppermute | solution.py:27
  24.2 0.9 copy-start.3
  42.9 7.8 %collective-permute-start.2 = (f32[2,4,4,2,256]{4,3,2,1,0:T(2,128)S(1)}, f32[2,4,4,2,256]{4,3,2,1,0:T(2,128)S(1)}, u32[]{:S(2)}, u32[]{:S(2)}) collective-permute-start(f32[2,4,4,2,256]{4,3,2,1,0:T(2,128)S(1)} %get-tuple-element.75), channel_id=1, source_target_pairs={{1,0},{2,1},{3,2},{4,3},{5,4},{6,5},{7,6},{9,8},{10,9},{11,10},{12... | collective-permute-start | bytes 196616 | tf_op jit(solution)/shard_map/ppermute | solution.py:29
  44.2 7.3 %collective-permute-start.3 = (f32[2,4,4,2,256]{4,3,2,1,0:T(2,128)S(1)}, f32[2,4,4,2,256]{4,3,2,1,0:T(2,128)S(1)}, u32[]{:S(2)}, u32[]{:S(2)}) collective-permute-start(f32[2,4,4,2,256]{4,3,2,1,0:T(2,128)S(1)} %get-tuple-element.76), channel_id=1, source_target_pairs={{0,1},{1,2},{2,3},{3,4},{4,5},{5,6},{6,7},{8,9},{9,10},{10,11},{11... | collective-permute-start | bytes 196616 | tf_op jit(solution)/shard_map/ppermute | solution.py:27
  80.9 7.7 %collective-permute-start.4 = (f32[2,4,4,2,256]{4,3,2,1,0:T(2,128)S(1)}, f32[2,4,4,2,256]{4,3,2,1,0:T(2,128)S(1)}, u32[]{:S(2)}, u32[]{:S(2)}) collective-permute-start(f32[2,4,4,2,256]{4,3,2,1,0:T(2,128)S(1)} %get-tuple-element.50), channel_id=1, source_target_pairs={{1,0},{2,1},{3,2},{4,3},{5,4},{6,5},{7,6},{9,8},{10,9},{11,10},{12... | collective-permute-start | bytes 196616 | tf_op jit(solution)/shard_map/ppermute | solution.py:29
  82.2 8.2 %collective-permute-start.5 = (f32[2,4,4,2,256]{4,3,2,1,0:T(2,128)S(1)}, f32[2,4,4,2,256]{4,3,2,1,0:T(2,128)S(1)}, u32[]{:S(2)}, u32[]{:S(2)}) collective-permute-start(f32[2,4,4,2,256]{4,3,2,1,0:T(2,128)S(1)} %get-tuple-element.51), channel_id=1, source_target_pairs={{0,1},{1,2},{2,3},{3,4},{4,5},{5,6},{6,7},{8,9},{9,10},{10,11},{11... | collective-permute-start | bytes 196616 | tf_op jit(solution)/shard_map/ppermute | solution.py:27
  88.6 1.8 %copy-start.1 = (f32[2,4,4,2,256]{4,3,2,1,0:T(2,128)}, f32[2,4,4,2,256]{4,3,2,1,0:T(2,128)S(1)}, u32[]{:S(2)}) copy-start(f32[2,4,4,2,256]{4,3,2,1,0:T(2,128)S(1)} %collective-permute-done.4) | copy-start | bytes 196612
  90.4 0.6 copy-start.2
  104.3 7.4 %collective-permute-start.6 = (f32[2,4,4,2,256]{4,3,2,1,0:T(2,128)S(1)}, f32[2,4,4,2,256]{4,3,2,1,0:T(2,128)S(1)}, u32[]{:S(2)}, u32[]{:S(2)}) collective-permute-start(f32[2,4,4,2,256]{4,3,2,1,0:T(2,128)S(1)} %get-tuple-element.31), channel_id=1, source_target_pairs={{1,0},{2,1},{3,2},{4,3},{5,4},{6,5},{7,6},{9,8},{10,9},{11,10},{12... | collective-permute-start | bytes 196616 | tf_op jit(solution)/shard_map/ppermute | solution.py:29
  105.5 7.2 %collective-permute-start.7 = (f32[2,4,4,2,256]{4,3,2,1,0:T(2,128)S(1)}, f32[2,4,4,2,256]{4,3,2,1,0:T(2,128)S(1)}, u32[]{:S(2)}, u32[]{:S(2)}) collective-permute-start(f32[2,4,4,2,256]{4,3,2,1,0:T(2,128)S(1)} %get-tuple-element.32), channel_id=1, source_target_pairs={{0,1},{1,2},{2,3},{3,4},{4,5},{5,6},{6,7},{8,9},{9,10},{10,11},{11... | collective-permute-start | bytes 196616 | tf_op jit(solution)/shard_map/ppermute | solution.py:27
where the time goes:
time: 147 us; the launch traced here: 146 us
  other arithmetic  46.4 us (32%)
  local copies, waits for them, and re-layouts  35.6 us (24%)
  blocking collectives  32.5 us (22%)
  starting transfers between devices  26.7 us (18%)
  waiting for transfers between devices  3.75 us (3%)
    add x4, other arithmetic, advance_core(): updated = centre + TIME_STEP * (tendency + forcing)  27.1 us
    psum x1, blocking collectives, body(): total = lax.psum(partial_total, 'tile')  24.4 us
    ppermute x4, starting transfers between devices, extended(): lax.ppermute(tail, axis, [(i, (i + 1) % count) for i in range(ends)])  21.5 us
    slice x8, local copies, waits for them, and re-layouts, advance_core(): west_two = jnp.roll(centre, 2, axis=4)  10.6 us
    slice x8, local copies, waits for them, and re-layouts, advance_core(): east_one = jnp.roll(centre, -1, axis=4)  10.5 us
    all_to_all x1, blocking collectives, body(): lax.all_to_all(outgoing, 'member', split_axis=0, concat_axis=0, tiled=True)  8.18 us
    mul x4, other arithmetic, advance_core(): east_wind * slope_x + north_wind * slope_y  7.68 us
    slice x8, local copies, waits for them, and re-layouts, advance_core(): lower = jnp.concatenate([centre[:, :, :1], centre[:, :, :-1]], axis=2)  7.26 us
  transfers between devices with their start and end apart: 8, of which 3 were waited for; matrix products, arithmetic and copies ran while one was open for 14% of the time, Pallas kernels for 0%

commit v1 on v0

v1 whole, which is shorter than its diff:
```python
import functools

import jax
import jax.numpy as jnp
from jax import lax
from jax.experimental import pallas as pl
from jax.experimental.pallas import tpu as pltpu
from jax.sharding import PartitionSpec as P

STEPS_EACH = 2
TIME_STEP = 0.15
DIFFUSION = 0.2
MIXING = 0.1
CORIOLIS = 0.5
BUOYANCY_GAIN = 0.3
STRATIFICATION = 0.3
SATURATION = 0.5
LATENT = 0.5

LANES = 128
TILE = 8
REACH = 2
DEEP = 4 * REACH
SHALLOW = 2 * REACH
STRIP = 24
BAND = 16

KEEP = 1.0 - TIME_STEP * (4.0 * DIFFUSION + 2.0 * MIXING)
SPREAD = TIME_STEP * DIFFUSION
LIFT = TIME_STEP * MIXING
NEAR = TIME_STEP * 8.0 / 12.0
FAR = TIME_STEP / 12.0


def shifted(parts, by):
    lane = lax.broadcasted_iota(jnp.int32, parts[0].shape, 1)
    turned = [pltpu.roll(part, (-by) % LANES, 1) for part in parts]
    count = len(parts)
    if by > 0:
        return [jnp.where(lane >= LANES - by, turned[(h + 1) % count], turned[h]) for h in range(count)]
    return [jnp.where(lane < -by, turned[(h - 1) % count], turned[h]) for h in range(count)]


def advance_tile(load, levels, halves, store):
    for l in range(levels):
        up, down = min(l + 1, levels - 1), max(l - 1, 0)
        centre = [[load(f, l, h, 0) for h in range(halves)] for f in range(4)]
        winds = []
        for h in range(halves):
            e, n = centre[0][h], centre[1][h]
            en, nn = NEAR * e, NEAR * n
            winds.append((SPREAD - en, SPREAD + en, FAR * e, SPREAD - nn, SPREAD + nn, FAR * n))
        updated = []
        for f in range(4):
            c = centre[f]
            e1, w1, e2, w2 = shifted(c, 1), shifted(c, -1), shifted(c, 2), shifted(c, -2)
            row = []
            for h in range(halves):
                ae, aw, ax, an, as_, ay = winds[h]
                new = KEEP * c[h] + LIFT * (load(f, up, h, 0) + load(f, down, h, 0))
                new += ae * e1[h] + aw * w1[h] + ax * (e2[h] - w2[h])
                new += an * load(f, l, h, 1) + as_ * load(f, l, h, -1)
                new += ay * (load(f, l, h, 2) - load(f, l, h, -2))
                row.append(new)
            updated.append(row)
        for h in range(halves):
            e, n, b = centre[0][h], centre[1][h], centre[2][h]
            turn = (TIME_STEP * CORIOLIS) * n
            store(0, l, h, updated[0][h] + turn)
            store(1, l, h, updated[1][h] - (TIME_STEP * CORIOLIS) * e + (TIME_STEP * BUOYANCY_GAIN) * b)
            b_new = updated[2][h] - (TIME_STEP * STRATIFICATION) * n
            q_new = updated[3][h]
            excess = jnp.maximum(q_new - SATURATION * jnp.exp(0.1 * b_new), 0.0)
            store(2, l, h, b_new + LATENT * excess)
            store(3, l, h, q_new - excess)


def loader(ref, lead, start):
    def load(f, l, h, shift):
        return ref[(*lead, f, l, h, pl.ds(start + shift, TILE), slice(None))]

    return load


def latitude(first_row, total_rows):
    rows = first_row + lax.broadcasted_iota(jnp.int32, (TILE, LANES), 0)
    return 1.0 + (2.0 / (total_rows - 1)) * rows.astype(jnp.float32)


def half(h):
    return pl.ds(h * LANES, LANES)


def interior_kernel(dims, ancestors, own, other, pert, fields, sums, kept, late, first, second, noise, sems):
    members, levels, rows, halves, total_rows = dims
    owner = lax.axis_index("member")
    tile = lax.axis_index("tile")
    top = rows + TILE

    def state_copy(source, number, m, h):
        return pltpu.make_async_copy(
            source.at[number, :, :, :, half(h)],
            first.at[m, :, :, h, pl.ds(TILE, rows), :],
            sems.at[m, h],
        )

    def pert_copy(m, h):
        return pltpu.make_async_copy(
            pert.at[m, :, :, :, half(h)], noise.at[m, :, :, h, pl.ds(TILE, rows), :], sems.at[members + m, h]
        )

    def out_copy(m, h):
        return pltpu.make_async_copy(
            first.at[m, :, :, h, pl.ds(2 * TILE, rows - 2 * TILE), :],
            fields.at[m, :, :, pl.ds(TILE, rows - 2 * TILE), half(h)],
            sems.at[2 * members + m, h],
        )

    for m in range(members):
        source = ancestors[owner * members + m]
        here = lax.div(source, members) == owner
        number = lax.rem(source, members)

        @pl.when(here)
        def _():
            for h in range(halves):
                state_copy(own, number, m, h).start()

        @pl.when(jnp.logical_not(here))
        def _():
            for h in range(halves):
                state_copy(other, number, m, h).start()

    for m in range(members):
        for h in range(halves):
            pert_copy(m, h).start()

    def sweep(source, target, m, start, tiles, post=None):
        def one(i, carry):
            r = start + i * TILE

            def store(f, l, h, value):
                if post is not None:
                    value = post(f, l, h, r, value)
                target[m, f, l, h, pl.ds(r, TILE), :] = value

            advance_tile(loader(source, (m,), r), levels, halves, store)
            return carry

        lax.fori_loop(0, tiles, one, 0)

    for m in range(members):
        for h in range(halves):
            state_copy(own, 0, m, h).wait()
        sweep(first, second, m, TILE + REACH, rows // TILE)
        for h in range(halves):
            pert_copy(m, h).wait()
        sweep(
            second,
            first,
            m,
            TILE + 2 * REACH,
            rows // TILE - 1,
            post=lambda f, l, h, r, value: value + noise[m, f, l, h, pl.ds(r, TILE), :],
        )
        for f in range(4):
            for l in range(levels):
                for h in range(halves):
                    kept[m, f, l, 0, h] = first[m, f, l, h, pl.ds(TILE + 4, 8), :]
                    kept[m, f, l, 1, h] = first[m, f, l, h, pl.ds(top - 8 - 4, 8), :]
        sweep(first, second, m, TILE + 3 * REACH, rows // TILE - 1)
        for f in range(4):
            for l in range(levels):
                for h in range(halves):
                    late[m, f, l, 0, h] = second[m, f, l, h, pl.ds(TILE + 6, 8), :]
                    late[m, f, l, 1, h] = second[m, f, l, h, pl.ds(top - 8 - 6, 8), :]

        def last(i, total):
            r = 2 * TILE + i * TILE
            weight = latitude(tile * rows + r - TILE, total_rows)
            squares = []

            def store(f, l, h, value):
                first[m, f, l, h, pl.ds(r, TILE), :] = value
                if f == 2:
                    squares.append(value * value)

            advance_tile(loader(second, (m,), r), levels, halves, store)
            return total + weight * sum(squares)

        sums[m] = lax.fori_loop(0, rows // TILE - 2, last, jnp.zeros((TILE, LANES), jnp.float32))
        for h in range(halves):
            out_copy(m, h).start()
    for m in range(members):
        for h in range(halves):
            out_copy(m, h).wait()


def early_edge_kernel(dims, ancestors, own, other, own_pair, own_cross, other_pair, other_cross, early, first, second, sems):
    members, levels, rows, halves, total_rows = dims
    owner = lax.axis_index("member")
    tile = lax.axis_index("tile")
    last_tile = lax.axis_size("tile") - 1
    odd = lax.rem(tile, 2) == 1

    def place(source, number, m, side, begin, h, local):
        return pltpu.make_async_copy(
            source.at[number, :, :, pl.ds(begin, TILE), half(h)],
            first.at[m, :, :, side, h, pl.ds(local, TILE), :],
            sems.at[m, side, local // TILE, h],
        )

    for m in range(members):
        source = ancestors[owner * members + m]
        here = lax.div(source, members) == owner
        number = lax.rem(source, members)

        def bring(state, low, high):
            for h in range(halves):
                place(low, number, m, 0, 0, h, 0).start()
                place(state, number, m, 0, 0, h, TILE).start()
                place(state, number, m, 1, rows - TILE, h, 0).start()
                place(high, number, m, 1, 0, h, TILE).start()

        for chosen, state, pair, cross in (
            (here, own, own_pair, own_cross),
            (jnp.logical_not(here), other, other_pair, other_cross),
        ):
            for parity, low, high in ((odd, pair, cross), (jnp.logical_not(odd), cross, pair)):

                @pl.when(jnp.logical_and(chosen, parity))
                def _():
                    bring(state, low, high)

    for m in range(members):
        for side in range(2):
            for h in range(halves):
                for local in (0, TILE):
                    place(own_pair, 0, m, side, 0, h, local).wait()

    outside = (tile == 0, tile == last_tile)

    def blank(ref, begin):
        def clear(side, start):
            for m in range(members):
                for f in range(4):
                    for l in range(levels):
                        for h in range(halves):
                            ref[m, f, l, side, h, pl.ds(start, TILE), :] = jnp.zeros((TILE, LANES), jnp.float32)

        @pl.when(outside[0])
        def _():
            clear(0, begin[0])

        @pl.when(outside[1])
        def _():
            clear(1, begin[1])

    blank(first, (0, TILE))

    def step(source, write, starts):
        def one(index, carry):
            m, side = lax.div(index, 2), lax.rem(index, 2)
            for start in starts:
                advance_tile(
                    loader_side(source, m, side, start),
                    levels,
                    halves,
                    functools.partial(write, m, side, start),
                )
            return carry

        lax.fori_loop(0, members * 2, one, 0)

    def write_second(m, side, start, f, l, h, value):
        second[m, f, l, side, h, pl.ds(start, TILE), :] = value

    step(first, write_second, (REACH, REACH + 4))
    blank(second, (0, TILE))

    row = lax.broadcasted_iota(jnp.int32, (TILE, LANES), 0)

    def write_early(m, side, start, f, l, h, value):
        low = jnp.logical_and(jnp.logical_and(side == 0, outside[0]), row < 4)
        high = jnp.logical_and(jnp.logical_and(side == 1, outside[1]), row >= 4)
        early[m, f, l, side, h] = jnp.where(jnp.logical_or(low, high), 0.0, value)

    step(second, write_early, (2 * REACH,))


def loader_side(ref, m, side, start):
    def load(f, l, h, shift):
        return ref[m, f, l, side, h, pl.ds(start + shift, TILE), :]

    return load


def late_edge_kernel(dims, early, kept, late, pert_low, pert_high, pair, cross, sums, done, fields, total, first, second, third, sems):
    members, levels, rows, halves, total_rows = dims
    tile = lax.axis_index("tile")
    last_tile = lax.axis_size("tile") - 1
    odd = lax.rem(tile, 2) == 1
    outside = (tile == 0, tile == last_tile)
    row = lax.broadcasted_iota(jnp.int32, (TILE, LANES), 0)

    def fill(m, carry):
        for f in range(4):
            for l in range(levels):
                for h in range(halves):
                    cols = slice(h * LANES, (h + 1) * LANES)
                    from_pair = pair[m, f, l, :, cols]
                    from_cross = cross[m, f, l, :, cols]
                    below = jnp.where(odd, from_pair, from_cross)
                    above = jnp.where(odd, from_cross, from_pair)
                    below = jnp.where(outside[0], 0.0, below)
                    above = jnp.where(outside[1], 0.0, above)
                    first[m, f, l, 0, h, 4:8, :] = early[m, f, l, 0, h, 0:4, :] + below
                    first[m, f, l, 0, h, 8:12, :] = early[m, f, l, 0, h, 4:8, :] + pert_low[m, f, l, 0:4, cols]
                    first[m, f, l, 0, h, 12:20, :] = kept[m, f, l, 0, h]
                    first[m, f, l, 1, h, 4:12, :] = kept[m, f, l, 1, h]
                    first[m, f, l, 1, h, 12:16, :] = early[m, f, l, 1, h, 0:4, :] + pert_high[m, f, l, 4:8, cols]
                    first[m, f, l, 1, h, 16:20, :] = early[m, f, l, 1, h, 4:8, :] + above
                    second[m, f, l, 0, h, 14:22, :] = late[m, f, l, 0, h]
                    second[m, f, l, 1, h, 2:10, :] = late[m, f, l, 1, h]
        return carry

    lax.fori_loop(0, members, fill, 0)

    def third_step(m, carry):
        for side, start in ((0, 6), (1, 10)):
            beyond = jnp.logical_and(outside[side], (row < 2) if side == 0 else (row >= 6))

            def store(f, l, h, value):
                second[m, f, l, side, h, start : start + TILE, :] = jnp.where(beyond, 0.0, value)

            advance_tile(loader_side(first, m, side, start), levels, halves, store)
        return carry

    lax.fori_loop(0, members, third_step, 0)

    def copy(m, side, h):
        return pltpu.make_async_copy(
            third.at[m, :, :, side, h],
            fields.at[m, :, :, pl.ds(side * (rows - TILE), TILE), half(h)],
            sems.at[m, side, h],
        )

    def fourth_step(m, carry):
        acc = sums[m]
        for side in range(2):
            squares = []

            def store(f, l, h, value):
                third[m, f, l, side, h] = value
                if f == 2:
                    squares.append(value * value)

            advance_tile(loader_side(second, m, side, 8), levels, halves, store)
            acc += latitude(tile * rows + side * (rows - TILE), total_rows) * sum(squares)
            for h in range(halves):
                copy(m, side, h).start()
        total[m] = jnp.full((TILE, LANES), jnp.sum(acc) / (levels * total_rows * halves * LANES), jnp.float32)
        return carry

    lax.fori_loop(0, members, fourth_step, 0)
    for m in range(members):
        for side in range(2):
            for h in range(halves):
                copy(m, side, h).wait()


def tile_sum(value, count):
    if count & (count - 1):
        return lax.psum(value, "tile")
    reach = 1
    while reach < count:
        value = value + lax.ppermute(value, "tile", [(i, i ^ reach) for i in range(count)])
        reach *= 2
    return value


def body(state, perturbation, ancestors):
    members, fields_n, levels, rows, columns = state.shape
    halves = columns // LANES
    count = lax.axis_size("tile")
    tile = lax.axis_index("tile")
    total_rows = rows * count
    dims = (members, levels, rows, halves, total_rows)
    odd = lax.rem(tile, 2) == 1
    pair_pairs = [(i, i ^ 1) for i in range(count)]
    cross_pairs = [(i, i + 1 if i % 2 else i - 1) for i in range(1, count - 1)]

    other = lax.ppermute(state, "member", [(0, 1), (1, 0)])

    def edge(array, width, low):
        start = jnp.where(low, 0, rows - width)
        return lax.dynamic_slice_in_dim(array, start, width, axis=3)

    pair = lax.ppermute(edge(state, DEEP, odd), "tile", pair_pairs)
    cross = lax.ppermute(edge(state, DEEP, ~odd), "tile", cross_pairs)
    pert_pair = lax.ppermute(edge(perturbation, SHALLOW, odd), "tile", pair_pairs)
    pert_cross = lax.ppermute(edge(perturbation, SHALLOW, ~odd), "tile", cross_pairs)

    def vmem():
        return pl.BlockSpec(memory_space=pltpu.VMEM)

    def anywhere():
        return pl.BlockSpec(memory_space=pl.ANY)

    def smem():
        return pl.BlockSpec(memory_space=pltpu.SMEM)

    f32 = jnp.float32
    grid = (members, 4, levels, halves, rows + 2 * TILE, LANES)
    edges = (members, 4, levels, 2, halves, TILE, LANES)
    cells = members * 4 * levels * rows * columns
    done, sums, kept, late = pl.pallas_call(
        functools.partial(interior_kernel, dims),
        out_shape=(
            jax.ShapeDtypeStruct(state.shape, f32),
            jax.ShapeDtypeStruct((members, TILE, LANES), f32),
            jax.ShapeDtypeStruct(edges, f32),
            jax.ShapeDtypeStruct(edges, f32),
        ),
        in_specs=[smem(), anywhere(), anywhere(), anywhere()],
        out_specs=(anywhere(), vmem(), vmem(), vmem()),
        scratch_shapes=[
            pltpu.VMEM(grid, f32),
            pltpu.VMEM(grid, f32),
            pltpu.VMEM(grid, f32),
            pltpu.SemaphoreType.DMA((3 * members, halves)),
        ],
        compiler_params=pltpu.CompilerParams(vmem_limit_bytes=24 * 1024 * 1024),
        cost_estimate=pl.CostEstimate(flops=cells * 100, bytes_accessed=cells * 16, transcendentals=cells),
        name="interior",
    )(ancestors, state, other, perturbation)

    other_pair = lax.ppermute(pair, "member", [(0, 1), (1, 0)])
    other_cross = lax.ppermute(cross, "member", [(0, 1), (1, 0)])
    early = pl.pallas_call(
        functools.partial(early_edge_kernel, dims),
        out_shape=jax.ShapeDtypeStruct(edges, f32),
        in_specs=[smem()] + [anywhere()] * 6,
        out_specs=vmem(),
        scratch_shapes=[
            pltpu.VMEM((members, 4, levels, 2, halves, BAND, LANES), f32),
            pltpu.VMEM((members, 4, levels, 2, halves, BAND, LANES), f32),
            pltpu.SemaphoreType.DMA((members, 2, 2, halves)),
        ],
        compiler_params=pltpu.CompilerParams(vmem_limit_bytes=16 * 1024 * 1024),
        cost_estimate=pl.CostEstimate(flops=cells * 20, bytes_accessed=cells * 4, transcendentals=cells),
        name="early_edge",
    )(ancestors, state, other, pair, cross, other_pair, other_cross)

    pert_low = perturbation[:, :, :, :TILE]
    pert_high = perturbation[:, :, :, rows - TILE :]
    evolved, total = pl.pallas_call(
        functools.partial(late_edge_kernel, dims),
        out_shape=(
            jax.ShapeDtypeStruct(state.shape, f32),
            jax.ShapeDtypeStruct((members, TILE, LANES), f32),
        ),
        in_specs=[vmem()] * 8 + [anywhere()],
        out_specs=(anywhere(), vmem()),
        scratch_shapes=[
            pltpu.VMEM((members, 4, levels, 2, halves, STRIP, LANES), f32),
            pltpu.VMEM((members, 4, levels, 2, halves, STRIP, LANES), f32),
            pltpu.VMEM(edges, f32),
            pltpu.SemaphoreType.DMA((members, 2, halves)),
        ],
        input_output_aliases={8: 0},
        compiler_params=pltpu.CompilerParams(vmem_limit_bytes=24 * 1024 * 1024),
        cost_estimate=pl.CostEstimate(flops=cells * 20, bytes_accessed=cells * 4, transcendentals=cells),
        name="late_edge",
    )(early, kept, late, pert_low, pert_high, pert_pair, pert_cross, sums, done)

    observable = tile_sum(total, count)[:, 0, 0]
    return evolved, observable


def solution(mesh):
    return jax.shard_map(
        body,
        mesh=mesh,
        in_specs=(
            P(("groups", "member"), None, None, "tile", None),
            P(("groups", "member"), None, None, "tile", None),
            P("groups"),
        ),
        out_specs=(P(("groups", "member"), None, None, "tile", None), P(("groups", "member"))),
        check_vma=False,
    )
```

time: 147 us -> 60 us (0.41)
  other arithmetic: 46.4 us -> 0.62 us
  blocking collectives: 32.5 us -> 0 us
  local copies, waits for them, and re-layouts: 35.6 us -> 3.34 us
  Pallas kernels: 0 us -> 19.5 us
  waiting for transfers between devices: 3.75 us -> 18.7 us
  starting transfers between devices: 26.7 us -> 16.8 us
    add x7 -> x2, other arithmetic: 29.1 us -> 0.01 us  [tile_sum(): value + lax.ppermute(value, 'tile', [(i, i ^ reach) for i in range(count)])]
    slice x32 -> x1, local copies, waits for them, and re-layouts: 29.9 us -> 1.07 us  [body(): pert_high = perturbation[:, :, :, rows - TILE:]]
    psum x1 -> x0, blocking collectives: 24.4 us -> none  [body(): total = lax.psum(partial_total, 'tile')]
    pallas_call x0 -> x3, Pallas kernels: none -> 19.5 us  [the longest x1 13.8 us: body(): pl.pallas_call(functools.partial(interior_kernel, dims), out_shape=(jax.S...]
    ppermute x8 -> x10, waiting for transfers between devices: 3.75 us -> 18.7 us  [the longest x1 11 us: body(): pair = lax.ppermute(edge(state, DEEP, odd), 'tile', pair_pairs)]
    ppermute x8 -> x10, starting transfers between devices: 26.7 us -> 16.8 us  [the longest x1 5.38 us: body(): pair = lax.ppermute(edge(state, DEEP, odd), 'tile', pair_pairs)]
    all_to_all x1 -> x0, blocking collectives: 8.18 us -> none  [body(): lax.all_to_all(outgoing, 'member', split_axis=0, concat_axis=0, tiled=True)]
    mul x4 -> x0, other arithmetic: 7.68 us -> none  [advance_core(): east_wind * slope_x + north_wind * slope_y]
  transfers between devices with their start and end apart: 8 -> 10, of which waited for: 3 -> 4; matrix products, arithmetic and copies ran while one was open for 14% -> 6% of each run, Pallas kernels for 0% -> 28%
where the time goes in v1:
time: 60 us; the launch traced here: 59.8 us
  Pallas kernels  19.5 us (32%)
  waiting for transfers between devices  18.7 us (31%)
  starting transfers between devices  16.8 us (28%)
  local copies, waits for them, and re-layouts  3.34 us (6%)
  between operations  0.79 us (1%)
  other arithmetic  0.62 us (1%)
    pallas_call x1, Pallas kernels, body(): pl.pallas_call(functools.partial(interior_kernel, dims), out_shape=(jax.S...  13.8 us
    ppermute x1, waiting for transfers between devices, body(): pair = lax.ppermute(edge(state, DEEP, odd), 'tile', pair_pairs)  11 us
    ppermute x3, waiting for transfers between devices, tile_sum(): lax.ppermute(value, 'tile', [(i, i ^ reach) for i in range(count)])  7.74 us
    ppermute x1, starting transfers between devices, body(): pair = lax.ppermute(edge(state, DEEP, odd), 'tile', pair_pairs)  5.38 us
    ppermute x1, starting transfers between devices, body(): lax.ppermute(edge(perturbation, SHALLOW, odd), 'tile', pair_pairs)  5.31 us
    ppermute x3, starting transfers between devices, tile_sum(): lax.ppermute(value, 'tile', [(i, i ^ reach) for i in range(count)])  4.17 us
    pallas_call x1, Pallas kernels, body(): pl.pallas_call(functools.partial(early_edge_kernel, dims), out_shape=jax....  3.18 us
    pallas_call x1, Pallas kernels, body(): pl.pallas_call(functools.partial(late_edge_kernel, dims), out_shape=(jax....  2.54 us
  transfers between devices with their start and end apart: 10, of which 4 were waited for; matrix products, arithmetic and copies ran while one was open for 6% of the time, Pallas kernels for 28%

profile of v1, /device:TPU:0, one launch (start us, length us, event | category | flops | bytes accessed | tf_op | source)
XLA Modules:
  0.0 59.8 jit_solution(7734876946295755612)
XLA Ops:
  0.6 0.0 copy-start
  0.6 0.0 copy-start.2
  0.6 0.5 collective-permute-start
  1.2 1.2 %constant_dynamic-slice_fusion.2 = (f32[2,4,4,8,256]{4,3,2,1,0:T(8,128)S(1)}, f32[2,4,4,8,256]{4,3,2,1,0:T(8,128)S(1)}) fusion(f32[2,4,4,64,256]{4,3,2,1,0:T(8,128)} %own.3, s32[]{:T(128)S(6)} %select_n.18, s32[]{:T(128)S(6)} %select_n.17), kind=kLoop, calls=%fused_computation.3 | loop fusion | bytes 1048584 | tf_op jit(solution)/shard_map/dynamic_slice | solution.py:397
  2.3 0.7 %collective-permute-start.2 = (f32[2,4,4,8,256]{4,3,2,1,0:T(8,128)S(1)}, f32[2,4,4,8,256]{4,3,2,1,0:T(8,128)S(1)}, u32[]{:S(2)}, u32[]{:S(2)}) collective-permute-start(f32[2,4,4,8,256]{4,3,2,1,0:T(8,128)S(1)} %get-tuple-element.18), channel_id=1, source_target_pairs={{1,2},{2,1},{3,4},{4,3},{5,6},{6,5},{9,10},{10,9},{11,12},{12,11},... | collective-permute-start | bytes 786440 | tf_op jit(solution)/shard_map/ppermute | solution.py:400
  3.0 5.4 %collective-permute-start.1 = (f32[2,4,4,8,256]{4,3,2,1,0:T(8,128)S(1)}, f32[2,4,4,8,256]{4,3,2,1,0:T(8,128)S(1)}, u32[]{:S(2)}, u32[]{:S(2)}) collective-permute-start(f32[2,4,4,8,256]{4,3,2,1,0:T(8,128)S(1)} %get-tuple-element.19), channel_id=1, source_target_pairs={{0,1},{1,0},{2,3},{3,2},{4,5},{5,4},{6,7},{7,6},{8,9},{9,8},{10,11... | collective-permute-start | bytes 786440 | tf_op jit(solution)/shard_map/ppermute | solution.py:399
  8.4 0.0 collective-permute-done.2.own_cross
  8.4 0.0 collective-permute-start.4
  8.4 11.0 %collective-permute-done.1.own_pair = f32[2,4,4,8,256]{4,3,2,1,0:T(8,128)S(1)} collective-permute-done((f32[2,4,4,8,256]{4,3,2,1,0:T(8,128)S(1)}, f32[2,4,4,8,256]{4,3,2,1,0:T(8,128)S(1)}, u32[]{:S(2)}, u32[]{:S(2)}) %collective-permute-start.1) | collective-permute-done | bytes 262176 | tf_op jit(solution)/shard_map/ppermute | solution.py:399
  19.4 0.0 collective-permute-start.3
  19.4 1.1 %constant_dynamic-slice_fusion = (f32[2,4,4,4,256]{4,3,2,1,0:T(4,128)S(1)}, f32[2,4,4,4,256]{4,3,2,1,0:T(4,128)S(1)}) fusion(f32[2,4,4,64,256]{4,3,2,1,0:T(8,128)} %pert.1, s32[]{:T(128)S(6)} %select_n.20, s32[]{:T(128)S(6)} %select_n.19), kind=kLoop, calls=%fused_computation.1 | loop fusion | bytes 524296 | tf_op jit(solution)/shard_map/dynamic_slice | solution.py:397
  20.5 0.7 %collective-permute-start.6 = (f32[2,4,4,4,256]{4,3,2,1,0:T(4,128)S(1)}, f32[2,4,4,4,256]{4,3,2,1,0:T(4,128)S(1)}, u32[]{:S(2)}, u32[]{:S(2)}) collective-permute-start(f32[2,4,4,4,256]{4,3,2,1,0:T(4,128)S(1)} %get-tuple-element.14), channel_id=1, source_target_pairs={{1,2},{2,1},{3,4},{4,3},{5,6},{6,5},{9,10},{10,9},{11,12},{12,11},... | collective-permute-start | bytes 393224 | tf_op jit(solution)/shard_map/ppermute | solution.py:402
  21.2 5.3 %collective-permute-start.5 = (f32[2,4,4,4,256]{4,3,2,1,0:T(4,128)S(1)}, f32[2,4,4,4,256]{4,3,2,1,0:T(4,128)S(1)}, u32[]{:S(2)}, u32[]{:S(2)}) collective-permute-start(f32[2,4,4,4,256]{4,3,2,1,0:T(4,128)S(1)} %get-tuple-element.15), channel_id=1, source_target_pairs={{0,1},{1,0},{2,3},{3,2},{4,5},{5,4},{6,7},{7,6},{8,9},{9,8},{10,11... | collective-permute-start | bytes 393224 | tf_op jit(solution)/shard_map/ppermute | solution.py:401
  26.5 1.1 %fusion.1 = (f32[2,4,4,8,256]{4,3,2,1,0:T(8,128)S(1)}, f32[2,4,4,8,256]{4,3,2,1,0:T(8,128)S(1)}) fusion(f32[2,4,4,64,256]{4,3,2,1,0:T(8,128)} %pert.1), kind=kLoop, calls=%fused_computation.6 | loop fusion | bytes 1048576 | tf_op jit(solution)/shard_map/slice | solution.py:456
  27.6 0.0 copy-start.1
  27.6 0.0 collective-permute-done.4.other_cross
  27.6 0.0 collective-permute-done.3.other_pair
  27.6 0.0 collective-permute-done.other
  27.6 0.0 copy-done
  27.6 3.2 %early_edge.1.early = f32[2,4,4,2,2,8,128]{6,5,4,3,2,1,0:T(8,128)S(1)} custom-call(s32[4]{0:T(128)S(1)} %copy-done.2, f32[2,4,4,64,256]{4,3,2,1,0:T(8,128)S(1)} %copy-done, f32[2,4,4,64,256]{4,3,2,1,0:T(8,128)} %collective-permute-done.other, f32[2,4,4,8,256]{4,3,2,1,0:T(8,128)S(1)} %collective-permute-done.1.own_pair, ...), custom_call_target="tpu_custom_call" | custom-call | flops 10485760 | bytes 2097152 | tf_op jit(solution)/shard_map/early_edge/pallas_call | solution.py:440
  30.8 0.0 copy-done.1
  30.8 13.8 %interior.1 = (f32[2,4,4,64,256]{4,3,2,1,0:T(8,128)}, f32[2,8,128]{2,1,0:T(8,128)S(1)}, f32[2,4,4,2,2,8,128]{6,5,4,3,2,1,0:T(8,128)S(1)}, f32[2,4,4,2,2,8,128]{6,5,4,3,2,1,0:T(8,128)S(1)}) custom-call(s32[4]{0:T(128)S(1)} %copy-done.2, f32[2,4,4,64,256]{4,3,2,1,0:T(8,128)S(1)} %copy-done, f32[2,4,4,64,256]{4,3,2,1,0:T(8,128)} %collective-permute-done.other, ...), custom_call_target="tpu_custom_call" | custom-call | flops 52428800 | bytes 8388608 | tf_op jit(solution)/shard_map/interior/pallas_call | solution.py:417
  44.6 0.0 collective-permute-done.6.cross
  44.7 0.0 collective-permute-done.5.pair
  44.7 2.5 %late_edge.1 = (f32[2,4,4,64,256]{4,3,2,1,0:T(8,128)}, f32[2,8,128]{2,1,0:T(8,128)S(1)}) custom-call(f32[2,4,4,2,2,8,128]{6,5,4,3,2,1,0:T(8,128)S(1)} %early_edge.1.early, f32[2,4,4,2,2,8,128]{6,5,4,3,2,1,0:T(8,128)S(1)} %get-tuple-element.8.kept, f32[2,4,4,2,2,8,128]{6,5,4,3,2,1,0:T(8,128)S(1)} %get-tuple-element.9.late, ...), custom_call_target="tpu_custom_call", output_to_operand_aliasing={{0}: (8, {})} | custom-call | flops 10485760 | bytes 2097152 | tf_op jit(solution)/shard_map/late_edge/pallas_call | solution.py:457
  47.2 0.1 collective-permute-start.7
  47.3 3.6 %collective-permute-done.7 = f32[2,8,128]{2,1,0:T(8,128)S(1)} collective-permute-done((f32[2,8,128]{2,1,0:T(8,128)S(1)}, f32[2,8,128]{2,1,0:T(8,128)S(1)}, u32[]{:S(2)}, u32[]{:S(2)}) %collective-permute-start.7) | collective-permute-done | bytes 8224 | tf_op jit(solution)/shard_map/ppermute | solution.py:377
  50.9 1.5 %collective-permute-start.8 = (f32[2,8,128]{2,1,0:T(8,128)S(1)}, f32[2,8,128]{2,1,0:T(8,128)S(1)}, u32[]{:S(2)}, u32[]{:S(2)}) collective-permute-start(f32[2,8,128]{2,1,0:T(8,128)S(1)} %add.6), channel_id=1, source_target_pairs={{0,2},{1,3},{2,0},{3,1},{4,6},{5,7},{6,4},{7,5},{8,10},{9,11},{10,... | collective-permute-start | bytes 24584 | tf_op jit(solution)/shard_map/ppermute | solution.py:377
  52.5 2.1 %collective-permute-done.8 = f32[2,8,128]{2,1,0:T(8,128)S(1)} collective-permute-done((f32[2,8,128]{2,1,0:T(8,128)S(1)}, f32[2,8,128]{2,1,0:T(8,128)S(1)}, u32[]{:S(2)}, u32[]{:S(2)}) %collective-permute-start.8) | collective-permute-done | bytes 8224 | tf_op jit(solution)/shard_map/ppermute | solution.py:377
  54.6 2.6 %collective-permute-start.9 = (f32[2,8,128]{2,1,0:T(8,128)S(1)}, f32[2,8,128]{2,1,0:T(8,128)S(1)}, u32[]{:S(2)}, u32[]{:S(2)}) collective-permute-start(f32[2,8,128]{2,1,0:T(8,128)S(1)} %add.14), channel_id=1, source_target_pairs={{0,4},{1,5},{2,6},{3,7},{4,0},{5,1},{6,2},{7,3},{8,12},{9,13},{10,... | collective-permute-start | bytes 24584 | tf_op jit(solution)/shard_map/ppermute | solution.py:377
  57.2 2.0 %collective-permute-done.9 = f32[2,8,128]{2,1,0:T(8,128)S(1)} collective-permute-done((f32[2,8,128]{2,1,0:T(8,128)S(1)}, f32[2,8,128]{2,1,0:T(8,128)S(1)}, u32[]{:S(2)}, u32[]{:S(2)}) %collective-permute-start.9) | collective-permute-done | bytes 8224 | tf_op jit(solution)/shard_map/ppermute | solution.py:377
  59.1 0.6 %fusion = f32[2]{0:T(128)} fusion(f32[2,8,128]{2,1,0:T(8,128)S(1)} %collective-permute-done.9, f32[2,8,128]{2,1,0:T(8,128)S(1)} %add.14), kind=kLoop, calls=%fused_computation.5 | loop fusion | flops 2 | bytes 24 | tf_op jit(solution)/shard_map/slice | solution.py:477
  (3 shorter events, 0.0 us)
Async XLA Ops:
  0.6 27.0 %copy-start = (f32[2,4,4,64,256]{4,3,2,1,0:T(8,128)S(1)}, f32[2,4,4,64,256]{4,3,2,1,0:T(8,128)}, u32[]{:S(2)}) copy-start(f32[2,4,4,64,256]{4,3,2,1,0:T(8,128)} %own.3) | copy-start | bytes 6291460
  0.6 27.0 %copy-start.2 = (s32[4]{0:T(128)S(1)}, s32[4]{0:T(128)}, u32[]{:S(2)}) copy-start(s32[4]{0:T(128)} %ancestors.3) | copy-start | bytes 52
  0.6 27.0 %collective-permute-start = (f32[2,4,4,64,256]{4,3,2,1,0:T(8,128)}, f32[2,4,4,64,256]{4,3,2,1,0:T(8,128)}, u32[]{:S(2)}, u32[]{:S(2)}) collective-permute-start(f32[2,4,4,64,256]{4,3,2,1,0:T(8,128)} %own.3), channel_id=1, source_target_pairs={{0,8},{8,0},{1,9},{9,1},{2,10},{10,2},{3,11},{11,3},{4,12},{12,4},... | collective-permute-start | bytes 6291464 | tf_op jit(solution)/shard_map/ppermute | solution.py:393
  2.3 6.1 %collective-permute-start.2 = (f32[2,4,4,8,256]{4,3,2,1,0:T(8,128)S(1)}, f32[2,4,4,8,256]{4,3,2,1,0:T(8,128)S(1)}, u32[]{:S(2)}, u32[]{:S(2)}) collective-permute-start(f32[2,4,4,8,256]{4,3,2,1,0:T(8,128)S(1)} %get-tuple-element.18), channel_id=1, source_target_pairs={{1,2},{2,1},{3,4},{4,3},{5,6},{6,5},{9,10},{10,9},{11,12},{12,11},... | collective-permute-start | bytes 786440 | tf_op jit(solution)/shard_map/ppermute | solution.py:400
  3.0 16.4 %collective-permute-start.1 = (f32[2,4,4,8,256]{4,3,2,1,0:T(8,128)S(1)}, f32[2,4,4,8,256]{4,3,2,1,0:T(8,128)S(1)}, u32[]{:S(2)}, u32[]{:S(2)}) collective-permute-start(f32[2,4,4,8,256]{4,3,2,1,0:T(8,128)S(1)} %get-tuple-element.19), channel_id=1, source_target_pairs={{0,1},{1,0},{2,3},{3,2},{4,5},{5,4},{6,7},{7,6},{8,9},{9,8},{10,11... | collective-permute-start | bytes 786440 | tf_op jit(solution)/shard_map/ppermute | solution.py:399
  8.4 19.2 %collective-permute-start.4 = (f32[2,4,4,8,256]{4,3,2,1,0:T(8,128)S(1)}, f32[2,4,4,8,256]{4,3,2,1,0:T(8,128)S(1)}, u32[]{:S(2)}, u32[]{:S(2)}) collective-permute-start(f32[2,4,4,8,256]{4,3,2,1,0:T(8,128)S(1)} %collective-permute-done.2.own_cross), channel_id=1, source_target_pairs={{0,8},{8,0},{1,9},{9,1},{2,10},{10,2},{3,11},{11,3},{4,12},{12,4},... | collective-permute-start | bytes 786440 | tf_op jit(solution)/shard_map/ppermute | solution.py:439
  19.4 8.2 %collective-permute-start.3 = (f32[2,4,4,8,256]{4,3,2,1,0:T(8,128)S(1)}, f32[2,4,4,8,256]{4,3,2,1,0:T(8,128)S(1)}, u32[]{:S(2)}, u32[]{:S(2)}) collective-permute-start(f32[2,4,4,8,256]{4,3,2,1,0:T(8,128)S(1)} %collective-permute-done.1.own_pair), channel_id=1, source_target_pairs={{0,8},{8,0},{1,9},{9,1},{2,10},{10,2},{3,11},{11,3},{4,12},{12,4},... | collective-permute-start | bytes 786440 | tf_op jit(solution)/shard_map/ppermute | solution.py:438
  20.5 24.1 %collective-permute-start.6 = (f32[2,4,4,4,256]{4,3,2,1,0:T(4,128)S(1)}, f32[2,4,4,4,256]{4,3,2,1,0:T(4,128)S(1)}, u32[]{:S(2)}, u32[]{:S(2)}) collective-permute-start(f32[2,4,4,4,256]{4,3,2,1,0:T(4,128)S(1)} %get-tuple-element.14), channel_id=1, source_target_pairs={{1,2},{2,1},{3,4},{4,3},{5,6},{6,5},{9,10},{10,9},{11,12},{12,11},... | collective-permute-start | bytes 393224 | tf_op jit(solution)/shard_map/ppermute | solution.py:402
  21.2 23.5 %collective-permute-start.5 = (f32[2,4,4,4,256]{4,3,2,1,0:T(4,128)S(1)}, f32[2,4,4,4,256]{4,3,2,1,0:T(4,128)S(1)}, u32[]{:S(2)}, u32[]{:S(2)}) collective-permute-start(f32[2,4,4,4,256]{4,3,2,1,0:T(4,128)S(1)} %get-tuple-element.15), channel_id=1, source_target_pairs={{0,1},{1,0},{2,3},{3,2},{4,5},{5,4},{6,7},{7,6},{8,9},{9,8},{10,11... | collective-permute-start | bytes 393224 | tf_op jit(solution)/shard_map/ppermute | solution.py:401
  27.6 3.3 %copy-start.1 = (f32[2,4,4,64,256]{4,3,2,1,0:T(8,128)S(1)}, f32[2,4,4,64,256]{4,3,2,1,0:T(8,128)}, u32[]{:S(2)}) copy-start(f32[2,4,4,64,256]{4,3,2,1,0:T(8,128)} %pert.1) | copy-start | bytes 6291460
  47.2 3.7 %collective-permute-start.7 = (f32[2,8,128]{2,1,0:T(8,128)S(1)}, f32[2,8,128]{2,1,0:T(8,128)S(1)}, u32[]{:S(2)}, u32[]{:S(2)}) collective-permute-start(f32[2,8,128]{2,1,0:T(8,128)S(1)} %get-tuple-element.13), channel_id=1, source_target_pairs={{0,1},{1,0},{2,3},{3,2},{4,5},{5,4},{6,7},{7,6},{8,9},{9,8},{10,11... | collective-permute-start | bytes 24584 | tf_op jit(solution)/shard_map/ppermute | solution.py:377
  50.9 3.7 %collective-permute-start.8 = (f32[2,8,128]{2,1,0:T(8,128)S(1)}, f32[2,8,128]{2,1,0:T(8,128)S(1)}, u32[]{:S(2)}, u32[]{:S(2)}) collective-permute-start(f32[2,8,128]{2,1,0:T(8,128)S(1)} %add.6), channel_id=1, source_target_pairs={{0,2},{1,3},{2,0},{3,1},{4,6},{5,7},{6,4},{7,5},{8,10},{9,11},{10,... | collective-permute-start | bytes 24584 | tf_op jit(solution)/shard_map/ppermute | solution.py:377
  54.6 4.5 %collective-permute-start.9 = (f32[2,8,128]{2,1,0:T(8,128)S(1)}, f32[2,8,128]{2,1,0:T(8,128)S(1)}, u32[]{:S(2)}, u32[]{:S(2)}) collective-permute-start(f32[2,8,128]{2,1,0:T(8,128)S(1)} %add.14), channel_id=1, source_target_pairs={{0,4},{1,5},{2,6},{3,7},{4,0},{5,1},{6,2},{7,3},{8,12},{9,13},{10,... | collective-permute-start | bytes 24584 | tf_op jit(solution)/shard_map/ppermute | solution.py:377

commit v2 on v0

v2 whole, which is shorter than its diff:
```python
import functools

import jax
import jax.numpy as jnp
from jax import lax
from jax.experimental import pallas as pl
from jax.experimental.pallas import tpu as pltpu
from jax.sharding import PartitionSpec as P

STEPS_EACH = 2
TIME_STEP = 0.15
DIFFUSION = 0.2
MIXING = 0.1
CORIOLIS = 0.5
BUOYANCY_GAIN = 0.3
STRATIFICATION = 0.3
SATURATION = 0.5
LATENT = 0.5

LANES = 128
TILE = 8
REACH = 2
SHALLOW = 2 * REACH

INTERIOR_LIMIT = 16 * 1024 * 1024
RIM_LIMIT = 16 * 1024 * 1024

KEEP = 1.0 - TIME_STEP * (4.0 * DIFFUSION + 2.0 * MIXING)
SPREAD = TIME_STEP * DIFFUSION
LIFT = TIME_STEP * MIXING
NEAR = TIME_STEP * 8.0 / 12.0
FAR = TIME_STEP / 12.0


def shifted(parts, by):
    lane = lax.broadcasted_iota(jnp.int32, parts[0].shape, 1)
    turned = [pltpu.roll(part, (-by) % LANES, 1) for part in parts]
    count = len(parts)
    if by > 0:
        return [jnp.where(lane >= LANES - by, turned[(h + 1) % count], turned[h]) for h in range(count)]
    return [jnp.where(lane < -by, turned[(h - 1) % count], turned[h]) for h in range(count)]


def advance_tile(load, levels, halves, store):
    for l in range(levels):
        up, down = min(l + 1, levels - 1), max(l - 1, 0)
        centre = [[load(f, l, h, 0) for h in range(halves)] for f in range(4)]
        winds = []
        for h in range(halves):
            e, n = centre[0][h], centre[1][h]
            en, nn = NEAR * e, NEAR * n
            winds.append((SPREAD - en, SPREAD + en, FAR * e, SPREAD - nn, SPREAD + nn, FAR * n))
        updated = []
        for f in range(4):
            c = centre[f]
            e1, w1, e2, w2 = shifted(c, 1), shifted(c, -1), shifted(c, 2), shifted(c, -2)
            row = []
            for h in range(halves):
                ae, aw, ax, an, as_, ay = winds[h]
                new = KEEP * c[h] + LIFT * (load(f, up, h, 0) + load(f, down, h, 0))
                new += ae * e1[h] + aw * w1[h] + ax * (e2[h] - w2[h])
                new += an * load(f, l, h, 1) + as_ * load(f, l, h, -1)
                new += ay * (load(f, l, h, 2) - load(f, l, h, -2))
                row.append(new)
            updated.append(row)
        for h in range(halves):
            e, n, b = centre[0][h], centre[1][h], centre[2][h]
            turn = (TIME_STEP * CORIOLIS) * n
            store(0, l, h, updated[0][h] + turn)
            store(1, l, h, updated[1][h] - (TIME_STEP * CORIOLIS) * e + (TIME_STEP * BUOYANCY_GAIN) * b)
            b_new = updated[2][h] - (TIME_STEP * STRATIFICATION) * n
            q_new = updated[3][h]
            excess = jnp.maximum(q_new - SATURATION * jnp.exp(0.1 * b_new), 0.0)
            store(2, l, h, b_new + LATENT * excess)
            store(3, l, h, q_new - excess)


def loader(ref, m, start):
    def load(f, l, h, shift):
        return ref[m, f, l, h, pl.ds(start + shift, TILE), :]

    return load


def latitude(first_row, total_rows):
    rows = first_row + lax.broadcasted_iota(jnp.int32, (TILE, LANES), 0)
    return 1.0 + (2.0 / (total_rows - 1)) * rows.astype(jnp.float32)


def half(h):
    return pl.ds(h * LANES, LANES)


def from_source(ancestors, members, slot, own, other, act):
    owner = lax.axis_index("member")
    source = ancestors[owner * members + slot]
    here = lax.div(source, members) == owner
    number = lax.rem(source, members)

    @pl.when(here)
    def _():
        act(own, number)

    @pl.when(jnp.logical_not(here))
    def _():
        act(other, number)


def interior_kernel(dims, ancestors, own, other, pert, sums, zero, one, two, three, noise, sems):
    members, levels, rows, halves, total_rows = dims
    tile = lax.axis_index("tile")

    def state_copies(m, source, number):
        return [
            pltpu.make_async_copy(
                source.at[number, :, :, :, half(h)], zero.at[m, :, :, h, pl.ds(TILE, rows), :], sems.at[0, m, h]
            )
            for h in range(halves)
        ]

    def pert_copies(m):
        return [
            pltpu.make_async_copy(
                pert.at[m, :, :, :, half(h)], noise.at[m, :, :, h, pl.ds(TILE, rows), :], sems.at[1, m, h]
            )
            for h in range(halves)
        ]

    def begin(m, source, number):
        for copy in state_copies(m, source, number):
            copy.start()

    for m in range(members):
        from_source(ancestors, members, m, own, other, functools.partial(begin, m))
    for m in range(members):
        for copy in pert_copies(m):
            copy.start()

    def sweep(source, target, m, start, tiles, post=None):
        for r in range(start, start + tiles * TILE, TILE):

            def store(f, l, h, value):
                if post is not None:
                    value = post(f, l, h, r, value)
                target[m, f, l, h, pl.ds(r, TILE), :] = value

            advance_tile(loader(source, m, r), levels, halves, store)

    for m in range(members):
        for copy in state_copies(m, own, 0):
            copy.wait()
        sweep(zero, one, m, TILE + REACH, rows // TILE)
        for copy in pert_copies(m):
            copy.wait()

        def perturbed(f, l, h, r, value):
            return value + noise[m, f, l, h, pl.ds(r, TILE), :]

        sweep(one, two, m, TILE + 2 * REACH, rows // TILE - 1, perturbed)
        sweep(two, three, m, TILE + 3 * REACH, rows // TILE - 1)
        parts = []

        def counted(f, l, h, r, value):
            if f == 2:
                parts.append(latitude(tile * rows + r - TILE, total_rows) * (value * value))
            return value

        sweep(three, zero, m, 2 * TILE, rows // TILE - 2, counted)
        sums[m] = sum(parts)


def surround(dims, buffer, m, width, near, far):
    members, levels, rows, halves, total_rows = dims
    tile = lax.axis_index("tile")
    odd = lax.rem(tile, 2) == 1
    first, last = tile == 0, tile == lax.axis_size("tile") - 1
    end = TILE + rows
    for f in range(4):
        for l in range(levels):
            for h in range(halves):
                index = (f, l, slice(None), half(h))
                a, b = near(index), far(index)
                buffer[m, f, l, h, TILE - width : TILE, :] = jnp.where(first, 0.0, jnp.where(odd, a, b))
                buffer[m, f, l, h, end : end + width, :] = jnp.where(last, 0.0, jnp.where(odd, b, a))


def pert_rows_kernel(dims, pair, cross, held, noise):
    for m in range(dims[0]):
        surround(dims, noise, m, SHALLOW, lambda index: pair[(m, *index)], lambda index: cross[(m, *index)])


def rim_kernel(
    dims, ancestors, pair, cross, other_pair, other_cross, sums, zero, one, two, three, noise, fields, total, *rest
):
    zero, one, two, three, noise, sems = rest
    members, levels, rows, halves, total_rows = dims
    tile = lax.axis_index("tile")
    outside = (tile == 0, tile == lax.axis_size("tile") - 1)
    end = TILE + rows

    def result_copies(part, start, size):
        return [
            pltpu.make_async_copy(
                zero.at[m, :, :, h, pl.ds(start, size), :],
                fields.at[m, :, :, pl.ds(start - TILE, size), half(h)],
                sems.at[part, m, h],
            )
            for m in range(members)
            for h in range(halves)
        ]

    middle = result_copies(0, 2 * TILE, rows - 2 * TILE)
    for copy in middle:
        copy.start()

    owner = lax.axis_index("member")
    for m in range(members):
        source = ancestors[owner * members + m]
        here = lax.div(source, members) == owner
        number = lax.rem(source, members)

        def chosen(own, other):
            return lambda index: jnp.where(here, own[(number, *index)], other[(number, *index)])

        surround(dims, zero, m, TILE, chosen(pair, other_pair), chosen(cross, other_cross))

    row = lax.broadcasted_iota(jnp.int32, (TILE, LANES), 0)

    def rim_step(source, target, shift, post=None):
        for m in range(members):
            for side, start in enumerate((shift, end - shift)):
                inner = TILE - shift
                beyond = jnp.logical_and(outside[side], row < inner if side == 0 else row >= TILE - inner)

                def store(f, l, h, value):
                    if post is not None:
                        value = post(m, f, l, h, start, value)
                    if inner:
                        value = jnp.where(beyond, 0.0, value)
                    target[m, f, l, h, pl.ds(start, TILE), :] = value

                advance_tile(loader(source, m, start), levels, halves, store)

    def perturbed(m, f, l, h, start, value):
        return value + noise[m, f, l, h, pl.ds(start, TILE), :]

    parts = [[sums[m]] for m in range(members)]

    def counted(m, f, l, h, start, value):
        if f == 2:
            parts[m].append(latitude(tile * rows + start - TILE, total_rows) * (value * value))
        return value

    rim_step(zero, one, REACH)
    rim_step(one, two, 2 * REACH, perturbed)
    rim_step(two, three, 3 * REACH)
    rim_step(three, zero, TILE, counted)
    rims = result_copies(1, TILE, TILE) + result_copies(2, end - TILE, TILE)
    for copy in rims:
        copy.start()
    for m in range(members):
        share = jnp.sum(sum(parts[m])) / (levels * total_rows * halves * LANES)
        total[m] = jnp.full((TILE, LANES), share, jnp.float32)
    for copy in middle + rims:
        copy.wait()


def tile_sum(value, count):
    if count & (count - 1):
        return lax.psum(value, "tile")
    reach = 1
    while reach < count:
        value = value + lax.ppermute(value, "tile", [(i, i ^ reach) for i in range(count)])
        reach *= 2
    return value


def body(state, perturbation, ancestors):
    members, _, levels, rows, columns = state.shape
    halves = columns // LANES
    count, groups = lax.axis_size("tile"), lax.axis_size("groups")
    dims = (members, levels, rows, halves, rows * count)
    odd = lax.rem(lax.axis_index("tile"), 2) == 1
    f32 = jnp.float32

    def to_pair(array):
        return lax.ppermute(array, "tile", [(i, i ^ 1) for i in range(count)])

    def to_cross(array):
        def partner(group, i):
            if i in (0, count - 1):
                return (group ^ 1) * count + i if groups % 2 == 0 else group * count + count - 1 - i
            return group * count + (i + 1 if i % 2 else i - 1)

        pairs = [(group * count + i, partner(group, i)) for group in range(groups) for i in range(count)]
        return lax.ppermute(array, ("groups", "tile"), pairs)

    def edge(array, width, low):
        return lax.dynamic_slice_in_dim(array, jnp.where(low, 0, rows - width), width, axis=3)

    def to_member(array):
        return lax.ppermute(array, "member", [(0, 1), (1, 0)])

    def spec(space):
        return pl.BlockSpec(memory_space=space)

    other = to_member(state)
    pair, cross = to_pair(edge(state, TILE, odd)), to_cross(edge(state, TILE, ~odd))
    near, far = edge(perturbation, SHALLOW, odd), edge(perturbation, SHALLOW, ~odd)
    ancestors, near, far = lax.optimization_barrier((ancestors, near, far))
    pert_pair, pert_cross = to_pair(near), to_cross(far)

    cells = state.size
    buffer = jax.ShapeDtypeStruct((members, 4, levels, halves, rows + 2 * TILE, LANES), f32)
    sums_shape = jax.ShapeDtypeStruct((members, TILE, LANES), f32)
    sums, *buffers = pl.pallas_call(
        functools.partial(interior_kernel, dims),
        out_shape=(sums_shape,) + (buffer,) * 5,
        in_specs=[spec(pltpu.SMEM), spec(pl.ANY), spec(pl.ANY), spec(pl.ANY)],
        out_specs=(spec(pltpu.VMEM),) * 6,
        scratch_shapes=[pltpu.SemaphoreType.DMA((2, members, halves))],
        compiler_params=pltpu.CompilerParams(vmem_limit_bytes=INTERIOR_LIMIT),
        cost_estimate=pl.CostEstimate(flops=cells * 100, bytes_accessed=cells * 16, transcendentals=cells),
        name="interior",
    )(ancestors, state, other, perturbation)

    pair, cross, pert_pair, pert_cross, sums = lax.optimization_barrier((pair, cross, pert_pair, pert_cross, sums))
    other_pair, other_cross = to_member(pair), to_member(cross)
    buffers[4] = pl.pallas_call(
        functools.partial(pert_rows_kernel, dims),
        out_shape=buffer,
        in_specs=[spec(pltpu.VMEM)] * 3,
        out_specs=spec(pltpu.VMEM),
        input_output_aliases={2: 0},
        compiler_params=pltpu.CompilerParams(vmem_limit_bytes=RIM_LIMIT),
        cost_estimate=pl.CostEstimate(flops=0, bytes_accessed=cells * 100, transcendentals=0),
        name="pert_rows",
    )(pert_pair, pert_cross, buffers[4])
    evolved, total, *_ = pl.pallas_call(
        functools.partial(rim_kernel, dims),
        out_shape=(jax.ShapeDtypeStruct(state.shape, f32), sums_shape) + (buffer,) * 5,
        in_specs=[spec(pltpu.SMEM)] + [spec(pltpu.VMEM)] * 10,
        out_specs=(spec(pl.ANY),) + (spec(pltpu.VMEM),) * 6,
        scratch_shapes=[pltpu.SemaphoreType.DMA((3, members, halves))],
        input_output_aliases={6: 2, 7: 3, 8: 4, 9: 5, 10: 6},
        compiler_params=pltpu.CompilerParams(vmem_limit_bytes=RIM_LIMIT),
        cost_estimate=pl.CostEstimate(flops=cells * 30, bytes_accessed=cells * 8, transcendentals=cells),
        name="rim",
    )(ancestors, pair, cross, other_pair, other_cross, sums, *buffers)

    observable = tile_sum(total, count)[:, 0, 0]
    return evolved, observable


def solution(mesh):
    return jax.shard_map(
        body,
        mesh=mesh,
        in_specs=(
            P(("groups", "member"), None, None, "tile", None),
            P(("groups", "member"), None, None, "tile", None),
            P("groups"),
        ),
        out_specs=(P(("groups", "member"), None, None, "tile", None), P(("groups", "member"))),
        check_vma=False,
    )
```

time: 147 us -> 42.4 us (0.29)
  other arithmetic: 46.4 us -> 0.62 us
  blocking collectives: 32.5 us -> 0 us
  local copies, waits for them, and re-layouts: 35.6 us -> 5.99 us
  Pallas kernels: 0 us -> 12.7 us
  starting transfers between devices: 26.7 us -> 14.5 us
  waiting for transfers between devices: 3.75 us -> 7.68 us
    slice x32 -> x0, local copies, waits for them, and re-layouts: 29.9 us -> none  [the longest x8 10.6 us: advance_core(): west_two = jnp.roll(centre, 2, axis=4)]
    add x7 -> x2, other arithmetic: 29.1 us -> 0.01 us  [tile_sum(): value + lax.ppermute(value, 'tile', [(i, i ^ reach) for i in range(count)])]
    psum x1 -> x0, blocking collectives: 24.4 us -> none  [body(): total = lax.psum(partial_total, 'tile')]
    pallas_call x0 -> x3, Pallas kernels: none -> 12.7 us  [the longest x1 8.8 us: body(): pl.pallas_call(functools.partial(interior_kernel, dims), out_shape=(sums_...]
    ppermute x8 -> x10, starting transfers between devices: 26.7 us -> 14.5 us  [the longest x3 7.66 us: tile_sum(): lax.ppermute(value, 'tile', [(i, i ^ reach) for i in range(count)])]
    all_to_all x1 -> x0, blocking collectives: 8.18 us -> none  [body(): lax.all_to_all(outgoing, 'member', split_axis=0, concat_axis=0, tiled=True)]
    mul x4 -> x0, other arithmetic: 7.68 us -> none  [advance_core(): east_wind * slope_x + north_wind * slope_y]
    ppermute x8 -> x10, waiting for transfers between devices: 3.75 us -> 7.68 us  [the longest x3 4.89 us: tile_sum(): lax.ppermute(value, 'tile', [(i, i ^ reach) for i in range(count)])]
  transfers between devices with their start and end apart: 8 -> 10, of which waited for: 3 -> 6; matrix products, arithmetic and copies ran while one was open for 14% -> 5% of each run, Pallas kernels for 0% -> 21%
where the time goes in v2:
time: 42.4 us; the launch traced here: 42.2 us
  starting transfers between devices  14.5 us (34%)
  Pallas kernels  12.7 us (30%)
  waiting for transfers between devices  7.68 us (18%)
  local copies, waits for them, and re-layouts  5.99 us (14%)
  between operations  0.68 us (2%)
  other arithmetic  0.62 us (1%)
    pallas_call x1, Pallas kernels, body(): pl.pallas_call(functools.partial(interior_kernel, dims), out_shape=(sums_...  8.8 us
    ppermute x3, starting transfers between devices, tile_sum(): lax.ppermute(value, 'tile', [(i, i ^ reach) for i in range(count)])  7.66 us
    ppermute x3, waiting for transfers between devices, tile_sum(): lax.ppermute(value, 'tile', [(i, i ^ reach) for i in range(count)])  4.89 us
    pallas_call x1, Pallas kernels, body(): pl.pallas_call(functools.partial(rim_kernel, dims), out_shape=(jax.ShapeD...  3.87 us
    unnamed x6, local copies, waits for them, and re-layouts  3.84 us
    ppermute x2, starting transfers between devices, to_cross(): return lax.ppermute(array, ('groups', 'tile'), pairs)  3.67 us
    dynamic_slice x2, local copies, waits for them, and re-layouts, edge(): lax.dynamic_slice_in_dim(array, jnp.where(low, 0, rows - width), width, a...  2.15 us
    ppermute x2, starting transfers between devices, to_pair(): return lax.ppermute(array, 'tile', [(i, i ^ 1) for i in range(count)])  2.09 us
  transfers between devices with their start and end apart: 10, of which 6 were waited for; matrix products, arithmetic and copies ran while one was open for 5% of the time, Pallas kernels for 21%

profile of v2, /device:TPU:0, one launch (start us, length us, event | category | flops | bytes accessed | tf_op | source)
XLA Modules:
  0.0 42.2 jit_solution(14740273855379528707)
XLA Ops:
  0.6 0.5 %collective-permute-start.4 = (f32[2,4,4,64,256]{4,3,2,1,0:T(8,128)}, f32[2,4,4,64,256]{4,3,2,1,0:T(8,128)S(1)}, u32[]{:S(2)}, u32[]{:S(2)}) collective-permute-start(f32[2,4,4,64,256]{4,3,2,1,0:T(8,128)} %own.1), channel_id=1, source_target_pairs={{0,8},{8,0},{1,9},{9,1},{2,10},{10,2},{3,11},{11,3},{4,12},{12,4},... | collective-permute-start | bytes 6291464 | tf_op jit(solution)/shard_map/ppermute | solution.py:302
  1.1 1.1 %constant_dynamic-slice_fusion = (f32[2,4,4,8,256]{4,3,2,1,0:T(8,128)S(1)}, f32[2,4,4,8,256]{4,3,2,1,0:T(8,128)S(1)}) fusion(f32[2,4,4,64,256]{4,3,2,1,0:T(8,128)} %own.1, s32[]{:T(128)S(6)} %select_n.20, s32[]{:T(128)S(6)} %select_n.19), kind=kLoop, calls=%fused_computation.1 | loop fusion | bytes 1048584 | tf_op jit(solution)/shard_map/dynamic_slice | solution.py:299
  2.2 2.6 %collective-permute-start.1 = (f32[2,4,4,8,256]{4,3,2,1,0:T(8,128)S(1)}, f32[2,4,4,8,256]{4,3,2,1,0:T(8,128)S(1)}, u32[]{:S(2)}, u32[]{:S(2)}) collective-permute-start(f32[2,4,4,8,256]{4,3,2,1,0:T(8,128)S(1)} %get-tuple-element.34), channel_id=1, source_target_pairs={{0,16},{1,2},{2,1},{3,4},{4,3},{5,6},{6,5},{7,23},{16,0},{17,18},{... | collective-permute-start | bytes 786440 | tf_op jit(solution)/shard_map/ppermute | solution.py:296
  4.8 1.5 %collective-permute-start = (f32[2,4,4,8,256]{4,3,2,1,0:T(8,128)S(1)}, f32[2,4,4,8,256]{4,3,2,1,0:T(8,128)S(1)}, u32[]{:S(2)}, u32[]{:S(2)}) collective-permute-start(f32[2,4,4,8,256]{4,3,2,1,0:T(8,128)S(1)} %get-tuple-element.35), channel_id=1, source_target_pairs={{0,1},{1,0},{2,3},{3,2},{4,5},{5,4},{6,7},{7,6},{8,9},{9,8},{10,11... | collective-permute-start | bytes 786440 | tf_op jit(solution)/shard_map/ppermute | solution.py:287
  6.4 1.1 %constant_dynamic-slice_fusion.2 = (f32[2,4,4,4,256]{4,3,2,1,0:T(4,128)S(1)}, f32[2,4,4,4,256]{4,3,2,1,0:T(4,128)S(1)}) fusion(f32[2,4,4,64,256]{4,3,2,1,0:T(8,128)} %pert.1, s32[]{:T(128)S(6)} %select_n.18, s32[]{:T(128)S(6)} %select_n.17), kind=kLoop, calls=%fused_computation.3 | loop fusion | bytes 524296 | tf_op jit(solution)/shard_map/dynamic_slice | solution.py:299
  7.4 0.5 %collective-permute-start.2 = (f32[2,4,4,4,256]{4,3,2,1,0:T(4,128)S(1)}, f32[2,4,4,4,256]{4,3,2,1,0:T(4,128)S(1)}, u32[]{:S(2)}, u32[]{:S(2)}) collective-permute-start(f32[2,4,4,4,256]{4,3,2,1,0:T(4,128)S(1)} %get-tuple-element.19), channel_id=1, source_target_pairs={{0,1},{1,0},{2,3},{3,2},{4,5},{5,4},{6,7},{7,6},{8,9},{9,8},{10,11... | collective-permute-start | bytes 393224 | tf_op jit(solution)/shard_map/ppermute | solution.py:287
  8.0 1.1 %collective-permute-start.3 = (f32[2,4,4,4,256]{4,3,2,1,0:T(4,128)S(1)}, f32[2,4,4,4,256]{4,3,2,1,0:T(4,128)S(1)}, u32[]{:S(2)}, u32[]{:S(2)}) collective-permute-start(f32[2,4,4,4,256]{4,3,2,1,0:T(4,128)S(1)} %get-tuple-element.20), channel_id=1, source_target_pairs={{0,16},{1,2},{2,1},{3,4},{4,3},{5,6},{6,5},{7,23},{16,0},{17,18},{... | collective-permute-start | bytes 393224 | tf_op jit(solution)/shard_map/ppermute | solution.py:296
  9.1 0.0 collective-permute-done.4.other
  9.1 0.0 copy-start
  9.1 1.6 %copy-done = f32[2,4,4,64,256]{4,3,2,1,0:T(8,128)S(1)} copy-done((f32[2,4,4,64,256]{4,3,2,1,0:T(8,128)S(1)}, f32[2,4,4,64,256]{4,3,2,1,0:T(8,128)}, u32[]{:S(2)}) %copy-start) | copy-done | bytes 2097176
  10.7 0.0 copy-start.1
  10.7 1.6 %copy-done.1 = f32[2,4,4,64,256]{4,3,2,1,0:T(8,128)S(1)} copy-done((f32[2,4,4,64,256]{4,3,2,1,0:T(8,128)S(1)}, f32[2,4,4,64,256]{4,3,2,1,0:T(8,128)}, u32[]{:S(2)}) %copy-start.1) | copy-done | bytes 2097176
  12.3 0.0 copy-start.2
  12.3 0.7 %copy-done.2 = s32[4]{0:T(128)S(1)} copy-done((s32[4]{0:T(128)S(1)}, s32[4]{0:T(128)}, u32[]{:S(2)}) %copy-start.2) | copy-done | bytes 40
  12.9 8.8 %interior.1 = (f32[2,8,128]{2,1,0:T(8,128)S(1)}, f32[2,4,4,2,80,128]{5,4,3,2,1,0:T(8,128)S(1)}, f32[2,4,4,2,80,128]{5,4,3,2,1,0:T(8,128)S(1)}, f32[2,4,4,2,80,12...) custom-call(s32[4]{0:T(128)S(1)} %copy-done.2, ...), custom_call_target="tpu_custom_call" | custom-call | flops 52428800 | bytes 8388608 | tf_op jit(solution)/shard_map/interior/pallas_call | solution.py:316
  21.7 1.4 %collective-permute-done.2.pair = f32[2,4,4,4,256]{4,3,2,1,0:T(4,128)S(1)} collective-permute-done((f32[2,4,4,4,256]{4,3,2,1,0:T(4,128)S(1)}, f32[2,4,4,4,256]{4,3,2,1,0:T(4,128)S(1)}, u32[]{:S(2)}, u32[]{:S(2)}) %collective-permute-start.2) | collective-permute-done | bytes 131104 | tf_op jit(solution)/shard_map/ppermute | solution.py:287
  23.2 0.0 collective-permute-done.3.cross
  23.2 0.0 collective-permute-done.1.cross
  23.2 0.0 collective-permute-done.pair
  23.2 0.1 collective-permute-start.5
  23.3 0.5 %collective-permute-start.6 = (f32[2,4,4,8,256]{4,3,2,1,0:T(8,128)S(1)}, f32[2,4,4,8,256]{4,3,2,1,0:T(8,128)S(1)}, u32[]{:S(2)}, u32[]{:S(2)}) collective-permute-start(f32[2,4,4,8,256]{4,3,2,1,0:T(8,128)S(1)} %collective-permute-done.1.cross), channel_id=1, source_target_pairs={{0,8},{8,0},{1,9},{9,1},{2,10},{10,2},{3,11},{11,3},{4,12},{12,4},... | collective-permute-start | bytes 786440 | tf_op jit(solution)/shard_map/ppermute | solution.py:302
  23.8 0.1 pert_rows.1.noise
  23.8 1.0 %collective-permute-done.5.other_pair = f32[2,4,4,8,256]{4,3,2,1,0:T(8,128)S(1)} collective-permute-done((f32[2,4,4,8,256]{4,3,2,1,0:T(8,128)S(1)}, f32[2,4,4,8,256]{4,3,2,1,0:T(8,128)S(1)}, u32[]{:S(2)}, u32[]{:S(2)}) %collective-permute-start.5) | collective-permute-done | bytes 262176 | tf_op jit(solution)/shard_map/ppermute | solution.py:302
  24.8 0.4 collective-permute-done.6.other_cross
  25.2 3.9 %rim.1 = (f32[2,4,4,64,256]{4,3,2,1,0:T(8,128)}, f32[2,8,128]{2,1,0:T(8,128)S(1)}, f32[2,4,4,2,80,128]{5,4,3,2,1,0:T(8,128)S(1)}, f32[2,4,4,2,80,128]{5,4,3,2,1,...) custom-call(s32[4]{0:T(128)S(1)} %copy-done.2, ...), custom_call_target="tpu_custom_call", output_to_operand_aliasing={{2}: (6, {}), {3}: (7, {}), {4}: (8, {}), {5}: (9, {}), {6}... | custom-call | flops 15728640 | bytes 4194304 | tf_op jit(solution)/shard_map/rim/pallas_call | solution.py:339
  29.0 2.5 %collective-permute-start.7 = (f32[2,8,128]{2,1,0:T(8,128)S(1)}, f32[2,8,128]{2,1,0:T(8,128)S(1)}, u32[]{:S(2)}, u32[]{:S(2)}) collective-permute-start(f32[2,8,128]{2,1,0:T(8,128)S(1)} %get-tuple-element.33), channel_id=1, source_target_pairs={{0,1},{1,0},{2,3},{3,2},{4,5},{5,4},{6,7},{7,6},{8,9},{9,8},{10,11... | collective-permute-start | bytes 24584 | tf_op jit(solution)/shard_map/ppermute | solution.py:273
  31.6 1.6 %collective-permute-done.7 = f32[2,8,128]{2,1,0:T(8,128)S(1)} collective-permute-done((f32[2,8,128]{2,1,0:T(8,128)S(1)}, f32[2,8,128]{2,1,0:T(8,128)S(1)}, u32[]{:S(2)}, u32[]{:S(2)}) %collective-permute-start.7) | collective-permute-done | bytes 8224 | tf_op jit(solution)/shard_map/ppermute | solution.py:273
  33.2 2.1 %collective-permute-start.8 = (f32[2,8,128]{2,1,0:T(8,128)S(1)}, f32[2,8,128]{2,1,0:T(8,128)S(1)}, u32[]{:S(2)}, u32[]{:S(2)}) collective-permute-start(f32[2,8,128]{2,1,0:T(8,128)S(1)} %add.6), channel_id=1, source_target_pairs={{0,2},{1,3},{2,0},{3,1},{4,6},{5,7},{6,4},{7,5},{8,10},{9,11},{10,... | collective-permute-start | bytes 24584 | tf_op jit(solution)/shard_map/ppermute | solution.py:273
  35.3 1.6 %collective-permute-done.8 = f32[2,8,128]{2,1,0:T(8,128)S(1)} collective-permute-done((f32[2,8,128]{2,1,0:T(8,128)S(1)}, f32[2,8,128]{2,1,0:T(8,128)S(1)}, u32[]{:S(2)}, u32[]{:S(2)}) %collective-permute-start.8) | collective-permute-done | bytes 8224 | tf_op jit(solution)/shard_map/ppermute | solution.py:273
  36.9 3.0 %collective-permute-start.9 = (f32[2,8,128]{2,1,0:T(8,128)S(1)}, f32[2,8,128]{2,1,0:T(8,128)S(1)}, u32[]{:S(2)}, u32[]{:S(2)}) collective-permute-start(f32[2,8,128]{2,1,0:T(8,128)S(1)} %add.14), channel_id=1, source_target_pairs={{0,4},{1,5},{2,6},{3,7},{4,0},{5,1},{6,2},{7,3},{8,12},{9,13},{10,... | collective-permute-start | bytes 24584 | tf_op jit(solution)/shard_map/ppermute | solution.py:273
  40.0 1.6 %collective-permute-done.9 = f32[2,8,128]{2,1,0:T(8,128)S(1)} collective-permute-done((f32[2,8,128]{2,1,0:T(8,128)S(1)}, f32[2,8,128]{2,1,0:T(8,128)S(1)}, u32[]{:S(2)}, u32[]{:S(2)}) %collective-permute-start.9) | collective-permute-done | bytes 8224 | tf_op jit(solution)/shard_map/ppermute | solution.py:273
  41.6 0.6 %fusion = f32[2]{0:T(128)} fusion(f32[2,8,128]{2,1,0:T(8,128)S(1)} %collective-permute-done.9, f32[2,8,128]{2,1,0:T(8,128)S(1)} %add.14), kind=kLoop, calls=%fused_computation.5 | loop fusion | flops 2 | bytes 24 | tf_op jit(solution)/shard_map/slice | solution.py:351
  (2 shorter events, 0.0 us)
Async XLA Ops:
  0.6 8.5 %collective-permute-start.4 = (f32[2,4,4,64,256]{4,3,2,1,0:T(8,128)}, f32[2,4,4,64,256]{4,3,2,1,0:T(8,128)S(1)}, u32[]{:S(2)}, u32[]{:S(2)}) collective-permute-start(f32[2,4,4,64,256]{4,3,2,1,0:T(8,128)} %own.1), channel_id=1, source_target_pairs={{0,8},{8,0},{1,9},{9,1},{2,10},{10,2},{3,11},{11,3},{4,12},{12,4},... | collective-permute-start | bytes 6291464 | tf_op jit(solution)/shard_map/ppermute | solution.py:302
  2.2 21.0 %collective-permute-start.1 = (f32[2,4,4,8,256]{4,3,2,1,0:T(8,128)S(1)}, f32[2,4,4,8,256]{4,3,2,1,0:T(8,128)S(1)}, u32[]{:S(2)}, u32[]{:S(2)}) collective-permute-start(f32[2,4,4,8,256]{4,3,2,1,0:T(8,128)S(1)} %get-tuple-element.34), channel_id=1, source_target_pairs={{0,16},{1,2},{2,1},{3,4},{4,3},{5,6},{6,5},{7,23},{16,0},{17,18},{... | collective-permute-start | bytes 786440 | tf_op jit(solution)/shard_map/ppermute | solution.py:296
  4.8 18.4 %collective-permute-start = (f32[2,4,4,8,256]{4,3,2,1,0:T(8,128)S(1)}, f32[2,4,4,8,256]{4,3,2,1,0:T(8,128)S(1)}, u32[]{:S(2)}, u32[]{:S(2)}) collective-permute-start(f32[2,4,4,8,256]{4,3,2,1,0:T(8,128)S(1)} %get-tuple-element.35), channel_id=1, source_target_pairs={{0,1},{1,0},{2,3},{3,2},{4,5},{5,4},{6,7},{7,6},{8,9},{9,8},{10,11... | collective-permute-start | bytes 786440 | tf_op jit(solution)/shard_map/ppermute | solution.py:287
  7.4 15.7 %collective-permute-start.2 = (f32[2,4,4,4,256]{4,3,2,1,0:T(4,128)S(1)}, f32[2,4,4,4,256]{4,3,2,1,0:T(4,128)S(1)}, u32[]{:S(2)}, u32[]{:S(2)}) collective-permute-start(f32[2,4,4,4,256]{4,3,2,1,0:T(4,128)S(1)} %get-tuple-element.19), channel_id=1, source_target_pairs={{0,1},{1,0},{2,3},{3,2},{4,5},{5,4},{6,7},{7,6},{8,9},{9,8},{10,11... | collective-permute-start | bytes 393224 | tf_op jit(solution)/shard_map/ppermute | solution.py:287
  8.0 15.2 %collective-permute-start.3 = (f32[2,4,4,4,256]{4,3,2,1,0:T(4,128)S(1)}, f32[2,4,4,4,256]{4,3,2,1,0:T(4,128)S(1)}, u32[]{:S(2)}, u32[]{:S(2)}) collective-permute-start(f32[2,4,4,4,256]{4,3,2,1,0:T(4,128)S(1)} %get-tuple-element.20), channel_id=1, source_target_pairs={{0,16},{1,2},{2,1},{3,4},{4,3},{5,6},{6,5},{7,23},{16,0},{17,18},{... | collective-permute-start | bytes 393224 | tf_op jit(solution)/shard_map/ppermute | solution.py:296
  9.1 1.6 %copy-start = (f32[2,4,4,64,256]{4,3,2,1,0:T(8,128)S(1)}, f32[2,4,4,64,256]{4,3,2,1,0:T(8,128)}, u32[]{:S(2)}) copy-start(f32[2,4,4,64,256]{4,3,2,1,0:T(8,128)} %own.1) | copy-start | bytes 6291460
  10.7 1.6 %copy-start.1 = (f32[2,4,4,64,256]{4,3,2,1,0:T(8,128)S(1)}, f32[2,4,4,64,256]{4,3,2,1,0:T(8,128)}, u32[]{:S(2)}) copy-start(f32[2,4,4,64,256]{4,3,2,1,0:T(8,128)} %pert.1) | copy-start | bytes 6291460
  12.3 0.7 %copy-start.2 = (s32[4]{0:T(128)S(1)}, s32[4]{0:T(128)}, u32[]{:S(2)}) copy-start(s32[4]{0:T(128)} %ancestors.1) | copy-start | bytes 52
  23.2 1.6 %collective-permute-start.5 = (f32[2,4,4,8,256]{4,3,2,1,0:T(8,128)S(1)}, f32[2,4,4,8,256]{4,3,2,1,0:T(8,128)S(1)}, u32[]{:S(2)}, u32[]{:S(2)}) collective-permute-start(f32[2,4,4,8,256]{4,3,2,1,0:T(8,128)S(1)} %collective-permute-done.pair), channel_id=1, source_target_pairs={{0,8},{8,0},{1,9},{9,1},{2,10},{10,2},{3,11},{11,3},{4,12},{12,4},... | collective-permute-start | bytes 786440 | tf_op jit(solution)/shard_map/ppermute | solution.py:302
  23.3 1.9 %collective-permute-start.6 = (f32[2,4,4,8,256]{4,3,2,1,0:T(8,128)S(1)}, f32[2,4,4,8,256]{4,3,2,1,0:T(8,128)S(1)}, u32[]{:S(2)}, u32[]{:S(2)}) collective-permute-start(f32[2,4,4,8,256]{4,3,2,1,0:T(8,128)S(1)} %collective-permute-done.1.cross), channel_id=1, source_target_pairs={{0,8},{8,0},{1,9},{9,1},{2,10},{10,2},{3,11},{11,3},{4,12},{12,4},... | collective-permute-start | bytes 786440 | tf_op jit(solution)/shard_map/ppermute | solution.py:302
  29.0 4.2 %collective-permute-start.7 = (f32[2,8,128]{2,1,0:T(8,128)S(1)}, f32[2,8,128]{2,1,0:T(8,128)S(1)}, u32[]{:S(2)}, u32[]{:S(2)}) collective-permute-start(f32[2,8,128]{2,1,0:T(8,128)S(1)} %get-tuple-element.33), channel_id=1, source_target_pairs={{0,1},{1,0},{2,3},{3,2},{4,5},{5,4},{6,7},{7,6},{8,9},{9,8},{10,11... | collective-permute-start | bytes 24584 | tf_op jit(solution)/shard_map/ppermute | solution.py:273
  33.2 3.7 %collective-permute-start.8 = (f32[2,8,128]{2,1,0:T(8,128)S(1)}, f32[2,8,128]{2,1,0:T(8,128)S(1)}, u32[]{:S(2)}, u32[]{:S(2)}) collective-permute-start(f32[2,8,128]{2,1,0:T(8,128)S(1)} %add.6), channel_id=1, source_target_pairs={{0,2},{1,3},{2,0},{3,1},{4,6},{5,7},{6,4},{7,5},{8,10},{9,11},{10,... | collective-permute-start | bytes 24584 | tf_op jit(solution)/shard_map/ppermute | solution.py:273
  36.9 4.7 %collective-permute-start.9 = (f32[2,8,128]{2,1,0:T(8,128)S(1)}, f32[2,8,128]{2,1,0:T(8,128)S(1)}, u32[]{:S(2)}, u32[]{:S(2)}) collective-permute-start(f32[2,8,128]{2,1,0:T(8,128)S(1)} %add.14), channel_id=1, source_target_pairs={{0,4},{1,5},{2,6},{3,7},{4,0},{5,1},{6,2},{7,3},{8,12},{9,13},{10,... | collective-permute-start | bytes 24584 | tf_op jit(solution)/shard_map/ppermute | solution.py:273

commit v3 on v2

v3 whole, which is shorter than its diff:
```python
import functools

import jax
import jax.numpy as jnp
from jax import lax
from jax.experimental import pallas as pl
from jax.experimental.pallas import tpu as pltpu
from jax.sharding import PartitionSpec as P

STEPS_EACH = 2
TIME_STEP = 0.15
DIFFUSION = 0.2
MIXING = 0.1
CORIOLIS = 0.5
BUOYANCY_GAIN = 0.3
STRATIFICATION = 0.3
SATURATION = 0.5
LATENT = 0.5

LANES = 128
TILE = 8
REACH = 2
WIDTH = 2 * REACH

VMEM_LIMIT = 16 * 1024 * 1024
WIDE_LIMIT = 16 * 1024 * 1024

KEEP = 1.0 - TIME_STEP * (4.0 * DIFFUSION + 2.0 * MIXING)
SPREAD = TIME_STEP * DIFFUSION
LIFT = TIME_STEP * MIXING
NEAR = TIME_STEP * 8.0 / 12.0
FAR = TIME_STEP / 12.0


def shifted(parts, by):
    lane = lax.broadcasted_iota(jnp.int32, parts[0].shape, 1)
    turned = [pltpu.roll(part, (-by) % LANES, 1) for part in parts]
    count = len(parts)
    if by > 0:
        return [jnp.where(lane >= LANES - by, turned[(h + 1) % count], turned[h]) for h in range(count)]
    return [jnp.where(lane < -by, turned[(h - 1) % count], turned[h]) for h in range(count)]


def advance_tile(load, levels, halves, store):
    for l in range(levels):
        up, down = min(l + 1, levels - 1), max(l - 1, 0)
        centre = [[load(f, l, h, 0) for h in range(halves)] for f in range(4)]
        winds = []
        for h in range(halves):
            e, n = centre[0][h], centre[1][h]
            en, nn = NEAR * e, NEAR * n
            winds.append((SPREAD - en, SPREAD + en, FAR * e, SPREAD - nn, SPREAD + nn, FAR * n))
        updated = []
        for f in range(4):
            c = centre[f]
            e1, w1, e2, w2 = shifted(c, 1), shifted(c, -1), shifted(c, 2), shifted(c, -2)
            row = []
            for h in range(halves):
                ae, aw, ax, an, as_, ay = winds[h]
                new = KEEP * c[h] + LIFT * (load(f, up, h, 0) + load(f, down, h, 0))
                new += ae * e1[h] + aw * w1[h] + ax * (e2[h] - w2[h])
                new += an * load(f, l, h, 1) + as_ * load(f, l, h, -1)
                new += ay * (load(f, l, h, 2) - load(f, l, h, -2))
                row.append(new)
            updated.append(row)
        for h in range(halves):
            e, n, b = centre[0][h], centre[1][h], centre[2][h]
            turn = (TIME_STEP * CORIOLIS) * n
            store(0, l, h, updated[0][h] + turn)
            store(1, l, h, updated[1][h] - (TIME_STEP * CORIOLIS) * e + (TIME_STEP * BUOYANCY_GAIN) * b)
            b_new = updated[2][h] - (TIME_STEP * STRATIFICATION) * n
            q_new = updated[3][h]
            excess = jnp.maximum(q_new - SATURATION * jnp.exp(0.1 * b_new), 0.0)
            store(2, l, h, b_new + LATENT * excess)
            store(3, l, h, q_new - excess)


def loader(ref, m, start):
    def load(f, l, h, shift):
        return ref[m, f, l, h, pl.ds(start + shift, TILE), :]

    return load


def latitude(first_row, total_rows):
    rows = first_row + lax.broadcasted_iota(jnp.int32, (TILE, LANES), 0)
    return 1.0 + (2.0 / (total_rows - 1)) * rows.astype(jnp.float32)


def half(h):
    return pl.ds(h * LANES, LANES)


def from_source(ancestors, members, slot, own, other, act):
    owner = lax.axis_index("member")
    source = ancestors[owner * members + slot]
    here = lax.div(source, members) == owner
    number = lax.rem(source, members)

    @pl.when(here)
    def _():
        act(own, number)

    @pl.when(jnp.logical_not(here))
    def _():
        act(other, number)


def sweep(dims, source, target, m, starts, post=None):
    members, levels, rows, halves, total_rows = dims
    for start in starts:

        def store(f, l, h, value):
            if post is not None:
                value = post(f, l, h, start, value)
            target[m, f, l, h, pl.ds(start, TILE), :] = value

        advance_tile(loader(source, m, start), levels, halves, store)


def inner_starts(rows):
    first = range(2 * TILE - REACH, rows + REACH, TILE)
    second = range(2 * TILE, rows, TILE)
    return first, second


def perturbed(noise, m):
    def post(f, l, h, start, value):
        return value + noise[m, f, l, h, pl.ds(start, TILE), :]

    return post


def weighed(dims, parts):
    members, levels, rows, halves, total_rows = dims
    offset = lax.axis_index("tile") * rows - TILE

    def post(f, l, h, start, value):
        if f == 2:
            parts.append(latitude(offset + start, total_rows) * (value * value))
        return value

    return post


def split_edges(dims, low, high, to_pair, to_cross):
    members, levels, rows, halves, total_rows = dims
    odd = lax.rem(lax.axis_index("tile"), 2) == 1
    for m in range(members):
        for f in range(4):
            for l in range(levels):
                for h in range(halves):
                    a, b = low(m, f, l, h), high(m, f, l, h)
                    to_pair[m, f, l, :, half(h)] = jnp.where(odd, a, b)
                    to_cross[m, f, l, :, half(h)] = jnp.where(odd, b, a)


def edge_kernel(dims, low, high, to_pair, to_cross):
    split_edges(
        dims, lambda m, f, l, h: low[m, f, l, :, half(h)], lambda m, f, l, h: high[m, f, l, :, half(h)], to_pair, to_cross
    )


def inner_early_kernel(dims, ancestors_in, own, other, pert, mark, zero, one, two, noise, ancestors, sems, sem):
    members, levels, rows, halves, total_rows = dims
    first, second = inner_starts(rows)
    owner = lax.axis_index("member")

    def copies(source, number, target, part, m):
        return [
            pltpu.make_async_copy(
                source.at[number, :, :, :, half(h)], target.at[m, :, :, h, pl.ds(TILE, rows), :], sems.at[part, m, h]
            )
            for h in range(halves)
        ]

    def begin(source, number, m):
        for copy in copies(source, number, zero, 0, m):
            copy.start()

    bring = pltpu.make_async_copy(ancestors_in, ancestors, sem)
    bring.start()
    bring.wait()
    for m in range(members):
        source = ancestors[owner * members + m]
        here = lax.div(source, members) == owner
        number = lax.rem(source, members)
        mark[m] = jnp.full((TILE, LANES), jnp.where(here, number, number + members), jnp.int32)
        pl.when(here)(functools.partial(begin, own, number, m))
        pl.when(jnp.logical_not(here))(functools.partial(begin, other, number, m))
    for m in range(members):
        for copy in copies(pert, m, noise, 1, m):
            copy.start()
    for m in range(members):
        for copy in copies(own, 0, zero, 0, m):
            copy.wait()
        sweep(dims, zero, one, m, first)
        for copy in copies(pert, m, noise, 1, m):
            copy.wait()
        sweep(dims, one, two, m, second, perturbed(noise, m))


def inner_late_kernel(dims, two, sums, three, zero):
    members, levels, rows, halves, total_rows = dims
    first, second = inner_starts(rows)
    for m in range(members):
        parts = []
        sweep(dims, two, three, m, first)
        sweep(dims, three, zero, m, second, weighed(dims, parts))
        sums[m] = sum(parts)


def surround(dims, buffer, m, near, far):
    members, levels, rows, halves, total_rows = dims
    tile = lax.axis_index("tile")
    odd = lax.rem(tile, 2) == 1
    first, last = tile == 0, tile == lax.axis_size("tile") - 1
    end = TILE + rows
    for f in range(4):
        for l in range(levels):
            for h in range(halves):
                index = (f, l, slice(None), half(h))
                a, b = near(index), far(index)
                buffer[m, f, l, h, TILE - WIDTH : TILE, :] = jnp.where(first, 0.0, jnp.where(odd, a, b))
                buffer[m, f, l, h, end : end + WIDTH, :] = jnp.where(last, 0.0, jnp.where(odd, b, a))


def outer_step(dims, source, target, m):
    members, levels, rows, halves, total_rows = dims
    tile = lax.axis_index("tile")
    row = lax.broadcasted_iota(jnp.int32, (TILE, LANES), 0)
    below = jnp.logical_and(tile == 0, row < REACH)
    above = jnp.logical_and(tile == lax.axis_size("tile") - 1, row >= TILE - REACH)
    for start, beyond in ((TILE - REACH, below), (rows + REACH, above)):
        sweep(dims, source, target, m, (start,), lambda f, l, h, start, value: jnp.where(beyond, 0.0, value))


def outer_early_kernel(dims, pair, cross, other_pair, other_cross, mark, noise, zero_in, one_in, two_in,
                       to_pair, to_cross, zero, one, two):
    members, levels, rows, halves, total_rows = dims
    for m in range(members):
        place = mark[m, :WIDTH, :]

        def chosen(own, other):
            def read(index):
                value = own[(0, *index)]
                for k in range(1, 2 * members):
                    array = own if k < members else other
                    value = jnp.where(place == k, array[(k % members, *index)], value)
                return value

            return read

        surround(dims, zero, m, chosen(pair, other_pair), chosen(cross, other_cross))
        outer_step(dims, zero, one, m)
        sweep(dims, one, two, m, (TILE, rows), perturbed(noise, m))
    split_edges(
        dims,
        lambda m, f, l, h: two[m, f, l, h, TILE : TILE + WIDTH, :],
        lambda m, f, l, h: two[m, f, l, h, TILE + rows - WIDTH : TILE + rows, :],
        to_pair,
        to_cross,
    )


def outer_late_kernel(dims, pair, cross, sums, two_in, three_in, zero_in, fields, total, two, three, zero, sems):
    members, levels, rows, halves, total_rows = dims

    def copies(part, m, start, size):
        return [
            pltpu.make_async_copy(
                zero.at[m, :, :, h, pl.ds(start, size), :],
                fields.at[m, :, :, pl.ds(start - TILE, size), half(h)],
                sems.at[part, m, h],
            )
            for h in range(halves)
        ]

    started = []
    for m in range(members):
        started += copies(0, m, 2 * TILE, rows - 2 * TILE)
    for copy in started:
        copy.start()
    for m in range(members):
        surround(dims, two, m, lambda index: pair[(m, *index)], lambda index: cross[(m, *index)])
        outer_step(dims, two, three, m)
        parts = [sums[m]]
        for part, start in ((1, TILE), (2, rows)):
            sweep(dims, three, zero, m, (start,), weighed(dims, parts))
            for copy in copies(part, m, start, TILE):
                copy.start()
                started.append(copy)
        total[m] = sum(parts)
    for copy in started:
        copy.wait()


def tile_sum(value, count):
    if count & (count - 1):
        return lax.psum(value, "tile")
    reach = 1
    while reach < count:
        value = value + lax.ppermute(value, "tile", [(i, i ^ reach) for i in range(count)])
        reach *= 2
    return value


def body(state, perturbation, ancestors):
    members, _, levels, rows, columns = state.shape
    halves = columns // LANES
    count, groups = lax.axis_size("tile"), lax.axis_size("groups")
    dims = (members, levels, rows, halves, rows * count)
    f32 = jnp.float32

    def to_pair(array):
        return lax.ppermute(array, "tile", [(i, i ^ 1) for i in range(count)])

    def to_cross(array):
        def partner(group, i):
            if i in (0, count - 1):
                return (group ^ 1) * count + i if groups % 2 == 0 else group * count + count - 1 - i
            return group * count + (i + 1 if i % 2 else i - 1)

        pairs = [(group * count + i, partner(group, i)) for group in range(groups) for i in range(count)]
        return lax.ppermute(array, ("groups", "tile"), pairs)

    def to_member(array):
        return lax.ppermute(array, "member", [(0, 1), (1, 0)])

    def in_hbm(array):
        return pltpu.with_memory_space_constraint(array, pltpu.HBM)

    def spec(space):
        return pl.BlockSpec(memory_space=space)

    vmem, anywhere = spec(pltpu.VMEM), spec(pl.ANY)
    params = pltpu.CompilerParams(vmem_limit_bytes=VMEM_LIMIT)
    cells = state.size

    def cost(part):
        return pl.CostEstimate(flops=cells * part, bytes_accessed=cells * part, transcendentals=0)

    buffer = jax.ShapeDtypeStruct((members, 4, levels, halves, rows + 2 * TILE, LANES), f32)
    tile = jax.ShapeDtypeStruct((members, TILE, LANES), f32)
    strip = jax.ShapeDtypeStruct((members, 4, levels, WIDTH, columns), f32)

    other = to_member(state)
    edge_pair, edge_cross = pl.pallas_call(
        functools.partial(edge_kernel, dims),
        out_shape=(strip, strip),
        in_specs=[vmem, vmem],
        out_specs=(vmem, vmem),
        compiler_params=params,
        cost_estimate=cost(0),
        name="edge",
    )(state[:, :, :, :WIDTH], state[:, :, :, rows - WIDTH :])
    pair, cross = to_pair(edge_pair), to_cross(edge_cross)
    mark, zero, one, two, noise = pl.pallas_call(
        functools.partial(inner_early_kernel, dims),
        out_shape=(jax.ShapeDtypeStruct(tile.shape, jnp.int32),) + (buffer,) * 4,
        in_specs=[anywhere] * 4,
        out_specs=(vmem,) * 5,
        scratch_shapes=[
            pltpu.SMEM(ancestors.shape, jnp.int32),
            pltpu.SemaphoreType.DMA((2, members, halves)),
            pltpu.SemaphoreType.DMA,
        ],
        compiler_params=pltpu.CompilerParams(vmem_limit_bytes=WIDE_LIMIT),
        cost_estimate=cost(20),
        name="inner_early",
    )(in_hbm(ancestors), in_hbm(state), other, in_hbm(perturbation))
    pair, cross, mark = lax.optimization_barrier((pair, cross, mark))
    other_pair, other_cross = to_member(pair), to_member(cross)
    edge_pair, edge_cross, zero, one, two = pl.pallas_call(
        functools.partial(outer_early_kernel, dims),
        out_shape=(strip, strip) + (buffer,) * 3,
        in_specs=[vmem] * 9,
        out_specs=(vmem,) * 5,
        input_output_aliases={6: 2, 7: 3, 8: 4},
        compiler_params=params,
        cost_estimate=cost(5),
        name="outer_early",
    )(pair, cross, other_pair, other_cross, mark, noise, zero, one, two)

    pair, cross = to_pair(edge_pair), to_cross(edge_cross)
    sums, three, zero = pl.pallas_call(
        functools.partial(inner_late_kernel, dims),
        out_shape=(tile, buffer, buffer),
        in_specs=[vmem],
        out_specs=(vmem,) * 3,
        compiler_params=params,
        cost_estimate=cost(20),
        name="inner_late",
    )(two)
    pair, cross, sums = lax.optimization_barrier((pair, cross, sums))
    evolved, total, *_ = pl.pallas_call(
        functools.partial(outer_late_kernel, dims),
        out_shape=(jax.ShapeDtypeStruct(state.shape, f32), tile) + (buffer,) * 3,
        in_specs=[vmem] * 6,
        out_specs=(anywhere,) + (vmem,) * 4,
        scratch_shapes=[pltpu.SemaphoreType.DMA((3, members, halves))],
        input_output_aliases={3: 2, 4: 3, 5: 4},
        compiler_params=params,
        cost_estimate=cost(5),
        name="outer_late",
    )(pair, cross, sums, two, three, zero)

    observable = jnp.sum(tile_sum(total, count), axis=(1, 2)) / (levels * rows * count * columns)
    return evolved, observable


def solution(mesh):
    return jax.shard_map(
        body,
        mesh=mesh,
        in_specs=(
            P(("groups", "member"), None, None, "tile", None),
            P(("groups", "member"), None, None, "tile", None),
            P("groups"),
        ),
        out_specs=(P(("groups", "member"), None, None, "tile", None), P(("groups", "member"))),
        check_vma=False,
    )
```

time: 42.4 us -> 38.2 us (0.901)
  local copies, waits for them, and re-layouts: 5.99 us -> 1.08 us
  starting transfers between devices: 14.5 us -> 16 us
  waiting for transfers between devices: 7.68 us -> 6.94 us
    unnamed x6 -> x0, local copies, waits for them, and re-layouts: 3.84 us -> none
    ppermute x2, starting transfers between devices: 2.09 us -> 4.3 us  [to_pair(): return lax.ppermute(array, 'tile', [(i, i ^ 1) for i in range(count)])]
    dynamic_slice x2 -> x0, local copies, waits for them, and re-layouts: 2.15 us -> none  [edge(): lax.dynamic_slice_in_dim(array, jnp.where(low, 0, rows - width), width, a...]
    slice x0 -> x1, local copies, waits for them, and re-layouts: none -> 1.08 us  [body(): state[:, :, :, rows - WIDTH:]]
    ppermute x2, starting transfers between devices: 3.67 us -> 2.93 us  [to_cross(): return lax.ppermute(array, ('groups', 'tile'), pairs)]
    slice x1 -> x0, other arithmetic: 0.61 us -> none  [body(): observable = tile_sum(total, count)[:, 0, 0]]
    div x0 -> x1, other arithmetic: none -> 0.52 us  [body(): jnp.sum(tile_sum(total, count), axis=(1, 2))]
    ppermute x2, waiting for transfers between devices: 1.45 us -> 1.02 us  [to_pair(): return lax.ppermute(array, 'tile', [(i, i ^ 1) for i in range(count)])]
  transfers between devices with their start and end apart: 10 -> 10, of which waited for: 6 -> 6; matrix products, arithmetic and copies ran while one was open for 5% -> 3% of each run, Pallas kernels for 21% -> 25%
where the time goes in v3:
time: 38.2 us; the launch traced here: 38.1 us
  starting transfers between devices  16 us (42%)
  Pallas kernels  12.8 us (34%)
  waiting for transfers between devices  6.94 us (18%)
  local copies, waits for them, and re-layouts  1.08 us (3%)
  between operations  0.7 us (2%)
  other arithmetic  0.62 us (2%)
    ppermute x3, starting transfers between devices, tile_sum(): lax.ppermute(value, 'tile', [(i, i ^ reach) for i in range(count)])  7.66 us
    pallas_call x1, Pallas kernels, body(): pl.pallas_call(functools.partial(inner_early_kernel, dims), out_shape=(ja...  5.8 us
    ppermute x3, waiting for transfers between devices, tile_sum(): lax.ppermute(value, 'tile', [(i, i ^ reach) for i in range(count)])  4.89 us
    ppermute x2, starting transfers between devices, to_pair(): return lax.ppermute(array, 'tile', [(i, i ^ 1) for i in range(count)])  4.3 us
    pallas_call x1, Pallas kernels, body(): pl.pallas_call(functools.partial(inner_late_kernel, dims), out_shape=(til...  3.59 us
    ppermute x2, starting transfers between devices, to_cross(): return lax.ppermute(array, ('groups', 'tile'), pairs)  2.93 us
    pallas_call x1, Pallas kernels, body(): pl.pallas_call(functools.partial(outer_late_kernel, dims), out_shape=(jax...  1.97 us
    pallas_call x1, Pallas kernels, body(): pl.pallas_call(functools.partial(outer_early_kernel, dims), out_shape=(st...  1.35 us
  transfers between devices with their start and end apart: 10, of which 6 were waited for; matrix products, arithmetic and copies ran while one was open for 3% of the time, Pallas kernels for 25%

profile of v3, /device:TPU:0, one launch (start us, length us, event | category | flops | bytes accessed | tf_op | source)
XLA Modules:
  0.0 38.1 jit_solution(15395826717025451391)
XLA Ops:
  0.6 0.5 %collective-permute-start.2 = (f32[2,4,4,64,256]{4,3,2,1,0:T(8,128)}, f32[2,4,4,64,256]{4,3,2,1,0:T(8,128)S(1)}, u32[]{:S(2)}, u32[]{:S(2)}) collective-permute-start(f32[2,4,4,64,256]{4,3,2,1,0:T(8,128)} %own.1), channel_id=1, source_target_pairs={{0,8},{8,0},{1,9},{9,1},{2,10},{10,2},{3,11},{11,3},{4,12},{12,4},... | collective-permute-start | bytes 6291464 | tf_op jit(solution)/shard_map/ppermute | solution.py:328
  1.1 1.1 %fusion = (f32[2,4,4,4,256]{4,3,2,1,0:T(4,128)S(1)}, f32[2,4,4,4,256]{4,3,2,1,0:T(4,128)S(1)}) fusion(f32[2,4,4,64,256]{4,3,2,1,0:T(8,128)} %own.1), kind=kLoop, calls=%fused_computation.2 | loop fusion | bytes 524288 | tf_op jit(solution)/shard_map/slice | solution.py:356
  2.2 0.1 edge.1
  2.3 2.6 %collective-permute-start = (f32[2,4,4,4,256]{4,3,2,1,0:T(4,128)S(1)}, f32[2,4,4,4,256]{4,3,2,1,0:T(4,128)S(1)}, u32[]{:S(2)}, u32[]{:S(2)}) collective-permute-start(f32[2,4,4,4,256]{4,3,2,1,0:T(4,128)S(1)} %get-tuple-element.23), channel_id=1, source_target_pairs={{0,1},{1,0},{2,3},{3,2},{4,5},{5,4},{6,7},{7,6},{8,9},{9,8},{10,11... | collective-permute-start | bytes 393224 | tf_op jit(solution)/shard_map/ppermute | solution.py:316
  4.9 1.5 %collective-permute-start.1 = (f32[2,4,4,4,256]{4,3,2,1,0:T(4,128)S(1)}, f32[2,4,4,4,256]{4,3,2,1,0:T(4,128)S(1)}, u32[]{:S(2)}, u32[]{:S(2)}) collective-permute-start(f32[2,4,4,4,256]{4,3,2,1,0:T(4,128)S(1)} %get-tuple-element.24), channel_id=1, source_target_pairs={{0,16},{1,2},{2,1},{3,4},{4,3},{5,6},{6,5},{7,23},{16,0},{17,18},{... | collective-permute-start | bytes 393224 | tf_op jit(solution)/shard_map/ppermute | solution.py:325
  6.4 0.0 collective-permute-done.2.other
  6.4 5.8 %inner_early.1 = (s32[2,8,128]{2,1,0:T(8,128)S(1)}, f32[2,4,4,2,80,128]{5,4,3,2,1,0:T(8,128)S(1)}, f32[2,4,4,2,80,128]{5,4,3,2,1,0:T(8,128)S(1)}, f32[2,4,4,2,80...) custom-call(s32[4]{0:T(128)} %ancestors_in.1, f32[2,4,4,64,256]{4,3,2,1,0:T(8,128)} %own.1, ...), custom_call_target="tpu_custom_call" | custom-call | flops 10485760 | bytes 10485760 | tf_op jit(solution)/shard_map/inner_early/pallas_call | solution.py:358
  12.2 0.0 collective-permute-done.pair
  12.2 0.0 collective-permute-done.1.cross
  12.2 0.1 collective-permute-start.3
  12.3 0.5 %collective-permute-start.4 = (f32[2,4,4,4,256]{4,3,2,1,0:T(4,128)S(1)}, f32[2,4,4,4,256]{4,3,2,1,0:T(4,128)S(1)}, u32[]{:S(2)}, u32[]{:S(2)}) collective-permute-start(f32[2,4,4,4,256]{4,3,2,1,0:T(4,128)S(1)} %collective-permute-done.1.cross), channel_id=1, source_target_pairs={{0,8},{8,0},{1,9},{9,1},{2,10},{10,2},{3,11},{11,3},{4,12},{12,4},... | collective-permute-start | bytes 393224 | tf_op jit(solution)/shard_map/ppermute | solution.py:328
  12.8 0.8 %collective-permute-done.3.other_pair = f32[2,4,4,4,256]{4,3,2,1,0:T(4,128)S(1)} collective-permute-done((f32[2,4,4,4,256]{4,3,2,1,0:T(4,128)S(1)}, f32[2,4,4,4,256]{4,3,2,1,0:T(4,128)S(1)}, u32[]{:S(2)}, u32[]{:S(2)}) %collective-permute-start.3) | collective-permute-done | bytes 131104 | tf_op jit(solution)/shard_map/ppermute | solution.py:328
  13.6 0.2 collective-permute-done.4.other_cross
  13.8 1.4 %outer_early.1 = (f32[2,4,4,4,256]{4,3,2,1,0:T(4,128)S(1)}, f32[2,4,4,4,256]{4,3,2,1,0:T(4,128)S(1)}, f32[2,4,4,2,80,128]{5,4,3,2,1,0:T(8,128)S(1)}, f32[2,4,4,2...) custom-call(f32[2,4,4,4,256]{4,3,2,1,0:T(4,128)S(1)} %collective-per, ...), custom_call_target="tpu_custom_call", output_to_operand_aliasing={{2}: (6, {}), {3}: (7, {}), {4}: (8, {})} | custom-call | flops 2621440 | bytes 2621440 | tf_op jit(solution)/shard_map/outer_early/pallas_call | solution.py:374
  15.2 1.7 %collective-permute-start.5 = (f32[2,4,4,4,256]{4,3,2,1,0:T(4,128)S(1)}, f32[2,4,4,4,256]{4,3,2,1,0:T(4,128)S(1)}, u32[]{:S(2)}, u32[]{:S(2)}) collective-permute-start(f32[2,4,4,4,256]{4,3,2,1,0:T(4,128)S(1)} %get-tuple-element.33), channel_id=1, source_target_pairs={{0,1},{1,0},{2,3},{3,2},{4,5},{5,4},{6,7},{7,6},{8,9},{9,8},{10,11... | collective-permute-start | bytes 393224 | tf_op jit(solution)/shard_map/ppermute | solution.py:316
  16.9 1.4 %collective-permute-start.6 = (f32[2,4,4,4,256]{4,3,2,1,0:T(4,128)S(1)}, f32[2,4,4,4,256]{4,3,2,1,0:T(4,128)S(1)}, u32[]{:S(2)}, u32[]{:S(2)}) collective-permute-start(f32[2,4,4,4,256]{4,3,2,1,0:T(4,128)S(1)} %get-tuple-element.34), channel_id=1, source_target_pairs={{0,16},{1,2},{2,1},{3,4},{4,3},{5,6},{6,5},{7,23},{16,0},{17,18},{... | collective-permute-start | bytes 393224 | tf_op jit(solution)/shard_map/ppermute | solution.py:325
  18.3 3.6 %inner_late.1 = (f32[2,8,128]{2,1,0:T(8,128)S(1)}, f32[2,4,4,2,80,128]{5,4,3,2,1,0:T(8,128)S(1)}, f32[2,4,4,2,80,128]{5,4,3,2,1,0:T(8,128)S(1)}) custom-call(f32[2,4,4,2,80,128]{5,4,3,2,1,0:T(8,128)S(1)} %get-tuple-element.35.two.two_in), custom_call_target="tpu_custom_call" | custom-call | flops 10485760 | bytes 10485760 | tf_op jit(solution)/shard_map/inner_late/pallas_call | solution.py:386
  21.9 1.0 %collective-permute-done.5.pair = f32[2,4,4,4,256]{4,3,2,1,0:T(4,128)S(1)} collective-permute-done((f32[2,4,4,4,256]{4,3,2,1,0:T(4,128)S(1)}, f32[2,4,4,4,256]{4,3,2,1,0:T(4,128)S(1)}, u32[]{:S(2)}, u32[]{:S(2)}) %collective-permute-start.5) | collective-permute-done | bytes 131104 | tf_op jit(solution)/shard_map/ppermute | solution.py:316
  22.9 0.0 collective-permute-done.6.cross
  22.9 2.0 %outer_late.1 = (f32[2,4,4,64,256]{4,3,2,1,0:T(8,128)}, f32[2,8,128]{2,1,0:T(8,128)S(1)}, f32[2,4,4,2,80,128]{5,4,3,2,1,0:T(8,128)S(1)}, f32[2,4,4,2,80,128]{5,4...) custom-call(f32[2,4,4,4,256]{4,3,2,1,0:T(4,128)S(1)} %collective-permute-do, ...), custom_call_target="tpu_custom_call", output_to_operand_aliasing={{2}: (3, {}), {3}: (4, {}), {4}: (5, {})} | custom-call | flops 2621440 | bytes 2621440 | tf_op jit(solution)/shard_map/outer_late/pallas_call | solution.py:396
  24.9 2.5 %collective-permute-start.7 = (f32[2,8,128]{2,1,0:T(8,128)S(1)}, f32[2,8,128]{2,1,0:T(8,128)S(1)}, u32[]{:S(2)}, u32[]{:S(2)}) collective-permute-start(f32[2,8,128]{2,1,0:T(8,128)S(1)} %get-tuple-element.43), channel_id=1, source_target_pairs={{0,1},{1,0},{2,3},{3,2},{4,5},{5,4},{6,7},{7,6},{8,9},{9,8},{10,11... | collective-permute-start | bytes 24584 | tf_op jit(solution)/shard_map/ppermute | solution.py:303
  27.5 1.6 %collective-permute-done.7 = f32[2,8,128]{2,1,0:T(8,128)S(1)} collective-permute-done((f32[2,8,128]{2,1,0:T(8,128)S(1)}, f32[2,8,128]{2,1,0:T(8,128)S(1)}, u32[]{:S(2)}, u32[]{:S(2)}) %collective-permute-start.7) | collective-permute-done | bytes 8224 | tf_op jit(solution)/shard_map/ppermute | solution.py:303
  29.1 2.1 %collective-permute-start.8 = (f32[2,8,128]{2,1,0:T(8,128)S(1)}, f32[2,8,128]{2,1,0:T(8,128)S(1)}, u32[]{:S(2)}, u32[]{:S(2)}) collective-permute-start(f32[2,8,128]{2,1,0:T(8,128)S(1)} %add.9), channel_id=1, source_target_pairs={{0,2},{1,3},{2,0},{3,1},{4,6},{5,7},{6,4},{7,5},{8,10},{9,11},{10,... | collective-permute-start | bytes 24584 | tf_op jit(solution)/shard_map/ppermute | solution.py:303
  31.2 1.6 %collective-permute-done.8 = f32[2,8,128]{2,1,0:T(8,128)S(1)} collective-permute-done((f32[2,8,128]{2,1,0:T(8,128)S(1)}, f32[2,8,128]{2,1,0:T(8,128)S(1)}, u32[]{:S(2)}, u32[]{:S(2)}) %collective-permute-start.8) | collective-permute-done | bytes 8224 | tf_op jit(solution)/shard_map/ppermute | solution.py:303
  32.8 3.0 %collective-permute-start.9 = (f32[2,8,128]{2,1,0:T(8,128)S(1)}, f32[2,8,128]{2,1,0:T(8,128)S(1)}, u32[]{:S(2)}, u32[]{:S(2)}) collective-permute-start(f32[2,8,128]{2,1,0:T(8,128)S(1)} %add.10), channel_id=1, source_target_pairs={{0,4},{1,5},{2,6},{3,7},{4,0},{5,1},{6,2},{7,3},{8,12},{9,13},{10,... | collective-permute-start | bytes 24584 | tf_op jit(solution)/shard_map/ppermute | solution.py:303
  35.8 1.6 %collective-permute-done.9 = f32[2,8,128]{2,1,0:T(8,128)S(1)} collective-permute-done((f32[2,8,128]{2,1,0:T(8,128)S(1)}, f32[2,8,128]{2,1,0:T(8,128)S(1)}, u32[]{:S(2)}, u32[]{:S(2)}) %collective-permute-start.9) | collective-permute-done | bytes 8224 | tf_op jit(solution)/shard_map/ppermute | solution.py:303
  37.5 0.1 add_reduce_fusion
  37.6 0.5 %broadcast_multiply_fusion = f32[2]{0:T(128)} fusion(f32[2]{0:T(128)S(1)} %add_reduce_fusion), kind=kLoop, calls=%fused_computation.1 | loop fusion | flops 2 | bytes 16 | tf_op jit(solution)/shard_map/div | solution.py:408
  (2 shorter events, 0.0 us)
Async XLA Ops:
  0.6 5.8 %collective-permute-start.2 = (f32[2,4,4,64,256]{4,3,2,1,0:T(8,128)}, f32[2,4,4,64,256]{4,3,2,1,0:T(8,128)S(1)}, u32[]{:S(2)}, u32[]{:S(2)}) collective-permute-start(f32[2,4,4,64,256]{4,3,2,1,0:T(8,128)} %own.1), channel_id=1, source_target_pairs={{0,8},{8,0},{1,9},{9,1},{2,10},{10,2},{3,11},{11,3},{4,12},{12,4},... | collective-permute-start | bytes 6291464 | tf_op jit(solution)/shard_map/ppermute | solution.py:328
  2.3 9.9 %collective-permute-start = (f32[2,4,4,4,256]{4,3,2,1,0:T(4,128)S(1)}, f32[2,4,4,4,256]{4,3,2,1,0:T(4,128)S(1)}, u32[]{:S(2)}, u32[]{:S(2)}) collective-permute-start(f32[2,4,4,4,256]{4,3,2,1,0:T(4,128)S(1)} %get-tuple-element.23), channel_id=1, source_target_pairs={{0,1},{1,0},{2,3},{3,2},{4,5},{5,4},{6,7},{7,6},{8,9},{9,8},{10,11... | collective-permute-start | bytes 393224 | tf_op jit(solution)/shard_map/ppermute | solution.py:316
  4.9 7.3 %collective-permute-start.1 = (f32[2,4,4,4,256]{4,3,2,1,0:T(4,128)S(1)}, f32[2,4,4,4,256]{4,3,2,1,0:T(4,128)S(1)}, u32[]{:S(2)}, u32[]{:S(2)}) collective-permute-start(f32[2,4,4,4,256]{4,3,2,1,0:T(4,128)S(1)} %get-tuple-element.24), channel_id=1, source_target_pairs={{0,16},{1,2},{2,1},{3,4},{4,3},{5,6},{6,5},{7,23},{16,0},{17,18},{... | collective-permute-start | bytes 393224 | tf_op jit(solution)/shard_map/ppermute | solution.py:325
  12.2 1.4 %collective-permute-start.3 = (f32[2,4,4,4,256]{4,3,2,1,0:T(4,128)S(1)}, f32[2,4,4,4,256]{4,3,2,1,0:T(4,128)S(1)}, u32[]{:S(2)}, u32[]{:S(2)}) collective-permute-start(f32[2,4,4,4,256]{4,3,2,1,0:T(4,128)S(1)} %collective-permute-done.pair), channel_id=1, source_target_pairs={{0,8},{8,0},{1,9},{9,1},{2,10},{10,2},{3,11},{11,3},{4,12},{12,4},... | collective-permute-start | bytes 393224 | tf_op jit(solution)/shard_map/ppermute | solution.py:328
  12.3 1.5 %collective-permute-start.4 = (f32[2,4,4,4,256]{4,3,2,1,0:T(4,128)S(1)}, f32[2,4,4,4,256]{4,3,2,1,0:T(4,128)S(1)}, u32[]{:S(2)}, u32[]{:S(2)}) collective-permute-start(f32[2,4,4,4,256]{4,3,2,1,0:T(4,128)S(1)} %collective-permute-done.1.cross), channel_id=1, source_target_pairs={{0,8},{8,0},{1,9},{9,1},{2,10},{10,2},{3,11},{11,3},{4,12},{12,4},... | collective-permute-start | bytes 393224 | tf_op jit(solution)/shard_map/ppermute | solution.py:328
  15.2 7.8 %collective-permute-start.5 = (f32[2,4,4,4,256]{4,3,2,1,0:T(4,128)S(1)}, f32[2,4,4,4,256]{4,3,2,1,0:T(4,128)S(1)}, u32[]{:S(2)}, u32[]{:S(2)}) collective-permute-start(f32[2,4,4,4,256]{4,3,2,1,0:T(4,128)S(1)} %get-tuple-element.33), channel_id=1, source_target_pairs={{0,1},{1,0},{2,3},{3,2},{4,5},{5,4},{6,7},{7,6},{8,9},{9,8},{10,11... | collective-permute-start | bytes 393224 | tf_op jit(solution)/shard_map/ppermute | solution.py:316
  16.9 6.1 %collective-permute-start.6 = (f32[2,4,4,4,256]{4,3,2,1,0:T(4,128)S(1)}, f32[2,4,4,4,256]{4,3,2,1,0:T(4,128)S(1)}, u32[]{:S(2)}, u32[]{:S(2)}) collective-permute-start(f32[2,4,4,4,256]{4,3,2,1,0:T(4,128)S(1)} %get-tuple-element.34), channel_id=1, source_target_pairs={{0,16},{1,2},{2,1},{3,4},{4,3},{5,6},{6,5},{7,23},{16,0},{17,18},{... | collective-permute-start | bytes 393224 | tf_op jit(solution)/shard_map/ppermute | solution.py:325
  24.9 4.2 %collective-permute-start.7 = (f32[2,8,128]{2,1,0:T(8,128)S(1)}, f32[2,8,128]{2,1,0:T(8,128)S(1)}, u32[]{:S(2)}, u32[]{:S(2)}) collective-permute-start(f32[2,8,128]{2,1,0:T(8,128)S(1)} %get-tuple-element.43), channel_id=1, source_target_pairs={{0,1},{1,0},{2,3},{3,2},{4,5},{5,4},{6,7},{7,6},{8,9},{9,8},{10,11... | collective-permute-start | bytes 24584 | tf_op jit(solution)/shard_map/ppermute | solution.py:303
  29.1 3.7 %collective-permute-start.8 = (f32[2,8,128]{2,1,0:T(8,128)S(1)}, f32[2,8,128]{2,1,0:T(8,128)S(1)}, u32[]{:S(2)}, u32[]{:S(2)}) collective-permute-start(f32[2,8,128]{2,1,0:T(8,128)S(1)} %add.9), channel_id=1, source_target_pairs={{0,2},{1,3},{2,0},{3,1},{4,6},{5,7},{6,4},{7,5},{8,10},{9,11},{10,... | collective-permute-start | bytes 24584 | tf_op jit(solution)/shard_map/ppermute | solution.py:303
  32.8 4.7 %collective-permute-start.9 = (f32[2,8,128]{2,1,0:T(8,128)S(1)}, f32[2,8,128]{2,1,0:T(8,128)S(1)}, u32[]{:S(2)}, u32[]{:S(2)}) collective-permute-start(f32[2,8,128]{2,1,0:T(8,128)S(1)} %add.10), channel_id=1, source_target_pairs={{0,4},{1,5},{2,6},{3,7},{4,0},{5,1},{6,2},{7,3},{8,12},{9,13},{10,... | collective-permute-start | bytes 24584 | tf_op jit(solution)/shard_map/ppermute | solution.py:303

commit v4 on v3

--- a/solution.py
+++ b/solution.py
@@ -200,14 +200,34 @@
         sweep(dims, one, two, m, second, perturbed(noise, m))
 
 
-def inner_late_kernel(dims, two, sums, three, zero):
+def result_copies(dims, buffer, fields, sems, part, m, start, size):
+    members, levels, rows, halves, total_rows = dims
+    return [
+        pltpu.make_async_copy(
+            buffer.at[m, :, :, h, pl.ds(start, size), :],
+            fields.at[m, :, :, pl.ds(start - TILE, size), half(h)],
+            sems.at[part, m, h],
+        )
+        for h in range(halves)
+    ]
+
+
+def inner_late_kernel(dims, two, sums, three, zero, fields, sems):
     members, levels, rows, halves, total_rows = dims
     first, second = inner_starts(rows)
+    middle = len(second) // 2
+    started = []
     for m in range(members):
         parts = []
         sweep(dims, two, three, m, first)
-        sweep(dims, three, zero, m, second, weighed(dims, parts))
+        for part, starts in enumerate((second[:middle], second[middle:])):
+            sweep(dims, three, zero, m, starts, weighed(dims, parts))
+            for copy in result_copies(dims, zero, fields, sems, part, m, starts[0], len(starts) * TILE):
+                copy.start()
+                started.append(copy)
         sums[m] = sum(parts)
+    for copy in started:
+        copy.wait()
 
 
 def surround(dims, buffer, m, near, far):
@@ -263,34 +283,29 @@
     )
 
 
-def outer_late_kernel(dims, pair, cross, sums, two_in, three_in, zero_in, fields, total, two, three, zero, sems):
-    members, levels, rows, halves, total_rows = dims
-
-    def copies(part, m, start, size):
-        return [
-            pltpu.make_async_copy(
-                zero.at[m, :, :, h, pl.ds(start, size), :],
-                fields.at[m, :, :, pl.ds(start - TILE, size), half(h)],
-                sems.at[part, m, h],
-            )
-            for h in range(halves)
-        ]
-
+def outer_late_kernel(dims, pair, cross, sums, two_in, three_in, zero_in, total, two, three, zero):
+    members, levels, rows, halves, total_rows = dims
+    sublane = lax.broadcasted_iota(jnp.int32, (TILE, LANES), 0)
+    held = jnp.zeros((TILE, LANES), jnp.float32)
+    for m in range(members):
+        surround(dims, two, m, lambda index: pair[(m, *index)], lambda index: cross[(m, *index)])
+    for m in range(members):
+        outer_step(dims, two, three, m)
+        parts = [sums[m]]
+        sweep(dims, three, zero, m, (TILE, rows), weighed(dims, parts))
+        column_sums = jnp.sum(sum(parts), axis=0, keepdims=True) * (1.0 / (levels * total_rows * halves * LANES))
+        held = jnp.where(sublane == m, column_sums, held)
+    total[...] = held
+
+
+def place_kernel(dims, zero, inner, fields, sems):
+    members, levels, rows, halves, total_rows = dims
     started = []
     for m in range(members):
-        started += copies(0, m, 2 * TILE, rows - 2 * TILE)
+        for part, start in enumerate((TILE, rows)):
+            started += result_copies(dims, zero, fields, sems, part, m, start, TILE)
     for copy in started:
         copy.start()
-    for m in range(members):
-        surround(dims, two, m, lambda index: pair[(m, *index)], lambda index: cross[(m, *index)])
-        outer_step(dims, two, three, m)
-        parts = [sums[m]]
-        for part, start in ((1, TILE), (2, rows)):
-            sweep(dims, three, zero, m, (start,), weighed(dims, parts))
-            for copy in copies(part, m, start, TILE):
-                copy.start()
-                started.append(copy)
-        total[m] = sum(parts)
     for copy in started:
         copy.wait()
 
@@ -383,29 +398,40 @@
     )(pair, cross, other_pair, other_cross, mark, noise, zero, one, two)
 
     pair, cross = to_pair(edge_pair), to_cross(edge_cross)
-    sums, three, zero = pl.pallas_call(
+    result = jax.ShapeDtypeStruct(state.shape, f32)
+    sums, three, zero, inner = pl.pallas_call(
         functools.partial(inner_late_kernel, dims),
-        out_shape=(tile, buffer, buffer),
+        out_shape=(tile, buffer, buffer, result),
         in_specs=[vmem],
-        out_specs=(vmem,) * 3,
+        out_specs=(vmem,) * 3 + (anywhere,),
+        scratch_shapes=[pltpu.SemaphoreType.DMA((2, members, halves))],
         compiler_params=params,
         cost_estimate=cost(20),
         name="inner_late",
     )(two)
     pair, cross, sums = lax.optimization_barrier((pair, cross, sums))
-    evolved, total, *_ = pl.pallas_call(
+    total, _, _, zero = pl.pallas_call(
         functools.partial(outer_late_kernel, dims),
-        out_shape=(jax.ShapeDtypeStruct(state.shape, f32), tile) + (buffer,) * 3,
+        out_shape=(jax.ShapeDtypeStruct((TILE, LANES), f32),) + (buffer,) * 3,
         in_specs=[vmem] * 6,
-        out_specs=(anywhere,) + (vmem,) * 4,
-        scratch_shapes=[pltpu.SemaphoreType.DMA((3, members, halves))],
-        input_output_aliases={3: 2, 4: 3, 5: 4},
+        out_specs=(vmem,) * 4,
+        input_output_aliases={3: 1, 4: 2, 5: 3},
         compiler_params=params,
         cost_estimate=cost(5),
         name="outer_late",
     )(pair, cross, sums, two, three, zero)
-
-    observable = jnp.sum(tile_sum(total, count), axis=(1, 2)) / (levels * rows * count * columns)
+    evolved = pl.pallas_call(
+        functools.partial(place_kernel, dims),
+        out_shape=result,
+        in_specs=[vmem, anywhere],
+        out_specs=anywhere,
+        scratch_shapes=[pltpu.SemaphoreType.DMA((2, members, halves))],
+        input_output_aliases={1: 0},
+        compiler_params=params,
+        cost_estimate=cost(5),
+        name="place",
+    )(zero, inner)
+    observable = jnp.sum(tile_sum(total, count), axis=1)[:members]
     return evolved, observable
 
 

time: 38.2 us -> 37.3 us (0.976)
  waiting for transfers between devices: 6.94 us -> 4.94 us
  Pallas kernels: 12.8 us -> 13.9 us
    pallas_call x1, Pallas kernels: 3.59 us -> 4.65 us  [body(): pl.pallas_call(functools.partial(inner_late_kernel, dims), out_shape=(til...]
    ppermute x2, waiting for transfers between devices: 1.02 us -> 0.01 us  [to_pair(): return lax.ppermute(array, 'tile', [(i, i ^ 1) for i in range(count)])]
    ppermute x3, waiting for transfers between devices: 4.89 us -> 3.9 us  [tile_sum(): lax.ppermute(value, 'tile', [(i, i ^ reach) for i in range(count)])]
    pallas_call x0 -> x1, Pallas kernels: none -> 0.85 us  [body(): pl.pallas_call(functools.partial(place_kernel, dims), out_shape=result, i...]
    pallas_call x1, Pallas kernels: 1.97 us -> 1.2 us  [body(): pl.pallas_call(functools.partial(outer_late_kernel, dims), out_shape=(jax...]
    reduce_sum x1, other arithmetic: 0.1 us -> 0.62 us  [body(): observable = jnp.sum(tile_sum(total, count), axis=1)[:members]]
    div x1 -> x0, other arithmetic: 0.52 us -> none  [body(): jnp.sum(tile_sum(total, count), axis=(1, 2))]
  transfers between devices with their start and end apart: 10 -> 10, of which waited for: 6 -> 5; matrix products, arithmetic and copies ran while one was open for 3% -> 3% of each run, Pallas kernels for 25% -> 30%
where the time goes in v4:
time: 37.3 us; the launch traced here: 37.2 us
  starting transfers between devices  15.9 us (43%)
  Pallas kernels  13.9 us (37%)
  waiting for transfers between devices  4.94 us (13%)
  local copies, waits for them, and re-layouts  1.08 us (3%)
  between operations  0.72 us (2%)
  other arithmetic  0.63 us (2%)
    ppermute x3, starting transfers between devices, tile_sum(): lax.ppermute(value, 'tile', [(i, i ^ reach) for i in range(count)])  7.59 us
    pallas_call x1, Pallas kernels, body(): pl.pallas_call(functools.partial(inner_early_kernel, dims), out_shape=(ja...  5.8 us
    pallas_call x1, Pallas kernels, body(): pl.pallas_call(functools.partial(inner_late_kernel, dims), out_shape=(til...  4.65 us
    ppermute x2, starting transfers between devices, to_pair(): return lax.ppermute(array, 'tile', [(i, i ^ 1) for i in range(count)])  4.3 us
    ppermute x3, waiting for transfers between devices, tile_sum(): lax.ppermute(value, 'tile', [(i, i ^ reach) for i in range(count)])  3.9 us
    ppermute x2, starting transfers between devices, to_cross(): return lax.ppermute(array, ('groups', 'tile'), pairs)  2.93 us
    pallas_call x1, Pallas kernels, body(): pl.pallas_call(functools.partial(outer_early_kernel, dims), out_shape=(st...  1.35 us
    pallas_call x1, Pallas kernels, body(): pl.pallas_call(functools.partial(outer_late_kernel, dims), out_shape=(jax...  1.2 us
  transfers between devices with their start and end apart: 10, of which 5 were waited for; matrix products, arithmetic and copies ran while one was open for 3% of the time, Pallas kernels for 30%

profile of v4, /device:TPU:0, one launch (start us, length us, event | category | flops | bytes accessed | tf_op | source)
XLA Modules:
  0.0 37.2 jit_solution(9262150915088113446)
XLA Ops:
  0.6 0.5 %collective-permute-start.2 = (f32[2,4,4,64,256]{4,3,2,1,0:T(8,128)}, f32[2,4,4,64,256]{4,3,2,1,0:T(8,128)S(1)}, u32[]{:S(2)}, u32[]{:S(2)}) collective-permute-start(f32[2,4,4,64,256]{4,3,2,1,0:T(8,128)} %own.1), channel_id=1, source_target_pairs={{0,8},{8,0},{1,9},{9,1},{2,10},{10,2},{3,11},{11,3},{4,12},{12,4},... | collective-permute-start | bytes 6291464 | tf_op jit(solution)/shard_map/ppermute | solution.py:343
  1.1 1.1 %fusion = (f32[2,4,4,4,256]{4,3,2,1,0:T(4,128)S(1)}, f32[2,4,4,4,256]{4,3,2,1,0:T(4,128)S(1)}) fusion(f32[2,4,4,64,256]{4,3,2,1,0:T(8,128)} %own.1), kind=kLoop, calls=%fused_computation.1 | loop fusion | bytes 524288 | tf_op jit(solution)/shard_map/slice | solution.py:371
  2.2 0.1 edge.1
  2.3 2.6 %collective-permute-start = (f32[2,4,4,4,256]{4,3,2,1,0:T(4,128)S(1)}, f32[2,4,4,4,256]{4,3,2,1,0:T(4,128)S(1)}, u32[]{:S(2)}, u32[]{:S(2)}) collective-permute-start(f32[2,4,4,4,256]{4,3,2,1,0:T(4,128)S(1)} %get-tuple-element.24), channel_id=1, source_target_pairs={{0,1},{1,0},{2,3},{3,2},{4,5},{5,4},{6,7},{7,6},{8,9},{9,8},{10,11... | collective-permute-start | bytes 393224 | tf_op jit(solution)/shard_map/ppermute | solution.py:331
  4.9 1.5 %collective-permute-start.1 = (f32[2,4,4,4,256]{4,3,2,1,0:T(4,128)S(1)}, f32[2,4,4,4,256]{4,3,2,1,0:T(4,128)S(1)}, u32[]{:S(2)}, u32[]{:S(2)}) collective-permute-start(f32[2,4,4,4,256]{4,3,2,1,0:T(4,128)S(1)} %get-tuple-element.25), channel_id=1, source_target_pairs={{0,16},{1,2},{2,1},{3,4},{4,3},{5,6},{6,5},{7,23},{16,0},{17,18},{... | collective-permute-start | bytes 393224 | tf_op jit(solution)/shard_map/ppermute | solution.py:340
  6.4 0.0 collective-permute-done.2.other
  6.4 5.8 %inner_early.1 = (s32[2,8,128]{2,1,0:T(8,128)S(1)}, f32[2,4,4,2,80,128]{5,4,3,2,1,0:T(8,128)S(1)}, f32[2,4,4,2,80,128]{5,4,3,2,1,0:T(8,128)S(1)}, f32[2,4,4,2,80...) custom-call(s32[4]{0:T(128)} %ancestors_in.1, f32[2,4,4,64,256]{4,3,2,1,0:T(8,128)} %own.1, ...), custom_call_target="tpu_custom_call" | custom-call | flops 10485760 | bytes 10485760 | tf_op jit(solution)/shard_map/inner_early/pallas_call | solution.py:373
  12.2 0.0 collective-permute-done.pair
  12.2 0.0 collective-permute-done.1.cross
  12.2 0.1 collective-permute-start.3
  12.3 0.5 %collective-permute-start.4 = (f32[2,4,4,4,256]{4,3,2,1,0:T(4,128)S(1)}, f32[2,4,4,4,256]{4,3,2,1,0:T(4,128)S(1)}, u32[]{:S(2)}, u32[]{:S(2)}) collective-permute-start(f32[2,4,4,4,256]{4,3,2,1,0:T(4,128)S(1)} %collective-permute-done.1.cross), channel_id=1, source_target_pairs={{0,8},{8,0},{1,9},{9,1},{2,10},{10,2},{3,11},{11,3},{4,12},{12,4},... | collective-permute-start | bytes 393224 | tf_op jit(solution)/shard_map/ppermute | solution.py:343
  12.8 0.8 %collective-permute-done.3.other_pair = f32[2,4,4,4,256]{4,3,2,1,0:T(4,128)S(1)} collective-permute-done((f32[2,4,4,4,256]{4,3,2,1,0:T(4,128)S(1)}, f32[2,4,4,4,256]{4,3,2,1,0:T(4,128)S(1)}, u32[]{:S(2)}, u32[]{:S(2)}) %collective-permute-start.3) | collective-permute-done | bytes 131104 | tf_op jit(solution)/shard_map/ppermute | solution.py:343
  13.6 0.2 collective-permute-done.4.other_cross
  13.8 1.4 %outer_early.1 = (f32[2,4,4,4,256]{4,3,2,1,0:T(4,128)S(1)}, f32[2,4,4,4,256]{4,3,2,1,0:T(4,128)S(1)}, f32[2,4,4,2,80,128]{5,4,3,2,1,0:T(8,128)S(1)}, f32[2,4,4,2...) custom-call(f32[2,4,4,4,256]{4,3,2,1,0:T(4,128)S(1)} %collective-per, ...), custom_call_target="tpu_custom_call", output_to_operand_aliasing={{2}: (6, {}), {3}: (7, {}), {4}: (8, {})} | custom-call | flops 2621440 | bytes 2621440 | tf_op jit(solution)/shard_map/outer_early/pallas_call | solution.py:389
  15.2 1.7 %collective-permute-start.5 = (f32[2,4,4,4,256]{4,3,2,1,0:T(4,128)S(1)}, f32[2,4,4,4,256]{4,3,2,1,0:T(4,128)S(1)}, u32[]{:S(2)}, u32[]{:S(2)}) collective-permute-start(f32[2,4,4,4,256]{4,3,2,1,0:T(4,128)S(1)} %get-tuple-element.34), channel_id=1, source_target_pairs={{0,1},{1,0},{2,3},{3,2},{4,5},{5,4},{6,7},{7,6},{8,9},{9,8},{10,11... | collective-permute-start | bytes 393224 | tf_op jit(solution)/shard_map/ppermute | solution.py:331
  16.9 1.4 %collective-permute-start.6 = (f32[2,4,4,4,256]{4,3,2,1,0:T(4,128)S(1)}, f32[2,4,4,4,256]{4,3,2,1,0:T(4,128)S(1)}, u32[]{:S(2)}, u32[]{:S(2)}) collective-permute-start(f32[2,4,4,4,256]{4,3,2,1,0:T(4,128)S(1)} %get-tuple-element.35), channel_id=1, source_target_pairs={{0,16},{1,2},{2,1},{3,4},{4,3},{5,6},{6,5},{7,23},{16,0},{17,18},{... | collective-permute-start | bytes 393224 | tf_op jit(solution)/shard_map/ppermute | solution.py:340
  18.3 4.6 %inner_late.1 = (f32[2,8,128]{2,1,0:T(8,128)S(1)}, f32[2,4,4,2,80,128]{5,4,3,2,1,0:T(8,128)S(1)}, f32[2,4,4,2,80,128]{5,4,3,2,1,0:T(8,128)S(1)}, f32[2,4,4,64,256]{4,3,2,1,0:T(8,128)}) custom-call(f32[2,4,4,2,80,128]{5,4,3,2,1,0:T(8,128)S(1)} %get-tuple-element.36.two.two_in), custom_call_target="tpu_custom_call" | custom-call | flops 10485760 | bytes 10485760 | tf_op jit(solution)/shard_map/inner_late/pallas_call | solution.py:402
  23.0 0.0 collective-permute-done.5.pair
  23.0 0.0 collective-permute-done.6.cross
  23.0 1.2 %outer_late.1 = (f32[8,128]{1,0:T(8,128)S(1)}, f32[2,4,4,2,80,128]{5,4,3,2,1,0:T(8,128)S(1)}, f32[2,4,4,2,80,128]{5,4,3,2,1,0:T(8,128)S(1)}, f32[2,4,4,2,80,128]{5,4,3,2,1,0:T(8,128)S(1)}) custom-call(f32[2,4,4,4,256]{4,3,2,1,0:T(4,128)S(1)} %collective-permute-done.5.pair, ...), custom_call_target="tpu_custom_call", output_to_operand_aliasing={{1}: (3, {}), {2}: (4, {}), {3}: (5, {})} | custom-call | flops 2621440 | bytes 2621440 | tf_op jit(solution)/shard_map/outer_late/pallas_call | solution.py:413
  24.2 2.5 %collective-permute-start.7 = (f32[8,128]{1,0:T(8,128)S(1)}, f32[8,128]{1,0:T(8,128)S(1)}, u32[]{:S(2)}, u32[]{:S(2)}) collective-permute-start(f32[8,128]{1,0:T(8,128)S(1)} %get-tuple-element.45), channel_id=1, source_target_pairs={{0,1},{1,0},{2,3},{3,2},{4,5},{5,4},{6,7},{7,6},{8,9},{9,8},{10,11... | collective-permute-start | bytes 12296 | tf_op jit(solution)/shard_map/ppermute | solution.py:318
  26.7 1.6 %collective-permute-done.7 = f32[8,128]{1,0:T(8,128)S(1)} collective-permute-done((f32[8,128]{1,0:T(8,128)S(1)}, f32[8,128]{1,0:T(8,128)S(1)}, u32[]{:S(2)}, u32[]{:S(2)}) %collective-permute-start.7) | collective-permute-done | bytes 4128 | tf_op jit(solution)/shard_map/ppermute | solution.py:318
  28.3 2.1 %collective-permute-start.8 = (f32[8,128]{1,0:T(8,128)S(1)}, f32[8,128]{1,0:T(8,128)S(1)}, u32[]{:S(2)}, u32[]{:S(2)}) collective-permute-start(f32[8,128]{1,0:T(8,128)S(1)} %add.9), channel_id=1, source_target_pairs={{0,2},{1,3},{2,0},{3,1},{4,6},{5,7},{6,4},{7,5},{8,10},{9,11},{10,... | collective-permute-start | bytes 12296 | tf_op jit(solution)/shard_map/ppermute | solution.py:318
  30.3 1.6 %collective-permute-done.8 = f32[8,128]{1,0:T(8,128)S(1)} collective-permute-done((f32[8,128]{1,0:T(8,128)S(1)}, f32[8,128]{1,0:T(8,128)S(1)}, u32[]{:S(2)}, u32[]{:S(2)}) %collective-permute-start.8) | collective-permute-done | bytes 4128 | tf_op jit(solution)/shard_map/ppermute | solution.py:318
  31.9 3.0 %collective-permute-start.9 = (f32[8,128]{1,0:T(8,128)S(1)}, f32[8,128]{1,0:T(8,128)S(1)}, u32[]{:S(2)}, u32[]{:S(2)}) collective-permute-start(f32[8,128]{1,0:T(8,128)S(1)} %add.10), channel_id=1, source_target_pairs={{0,4},{1,5},{2,6},{3,7},{4,0},{5,1},{6,2},{7,3},{8,12},{9,13},{10,... | collective-permute-start | bytes 12296 | tf_op jit(solution)/shard_map/ppermute | solution.py:318
  35.0 0.8 %place.1 = f32[2,4,4,64,256]{4,3,2,1,0:T(8,128)} custom-call(f32[2,4,4,2,80,128]{5,4,3,2,1,0:T(8,128)S(1)} %get-tuple-element.43.zero, f32[2,4,4,64,256]{4,3,2,1,0:T(8,128)} %get-tuple-element.44.inner), custom_call_target="tpu_custom_call", output_to_operand_aliasing={{}: (1, {})} | custom-call | flops 2621440 | bytes 2621440 | tf_op jit(solution)/shard_map/place/pallas_call | solution.py:423
  35.8 0.7 %collective-permute-done.9 = f32[8,128]{1,0:T(8,128)S(1)} collective-permute-done((f32[8,128]{1,0:T(8,128)S(1)}, f32[8,128]{1,0:T(8,128)S(1)}, u32[]{:S(2)}, u32[]{:S(2)}) %collective-permute-start.9) | collective-permute-done | bytes 4128 | tf_op jit(solution)/shard_map/ppermute | solution.py:318
  36.6 0.6 %add_reduce_fusion = f32[8]{0:T(128)} fusion(f32[8,128]{1,0:T(8,128)S(1)} %add.10, f32[8,128]{1,0:T(8,128)S(1)} %collective-permute-done.9), kind=kLoop, calls=%fused_computation | loop fusion | flops 2040 | bytes 8224 | tf_op jit(solution)/shard_map/reduce_sum | solution.py:434
  (2 shorter events, 0.0 us)
Async XLA Ops:
  0.6 5.8 %collective-permute-start.2 = (f32[2,4,4,64,256]{4,3,2,1,0:T(8,128)}, f32[2,4,4,64,256]{4,3,2,1,0:T(8,128)S(1)}, u32[]{:S(2)}, u32[]{:S(2)}) collective-permute-start(f32[2,4,4,64,256]{4,3,2,1,0:T(8,128)} %own.1), channel_id=1, source_target_pairs={{0,8},{8,0},{1,9},{9,1},{2,10},{10,2},{3,11},{11,3},{4,12},{12,4},... | collective-permute-start | bytes 6291464 | tf_op jit(solution)/shard_map/ppermute | solution.py:343
  2.3 9.9 %collective-permute-start = (f32[2,4,4,4,256]{4,3,2,1,0:T(4,128)S(1)}, f32[2,4,4,4,256]{4,3,2,1,0:T(4,128)S(1)}, u32[]{:S(2)}, u32[]{:S(2)}) collective-permute-start(f32[2,4,4,4,256]{4,3,2,1,0:T(4,128)S(1)} %get-tuple-element.24), channel_id=1, source_target_pairs={{0,1},{1,0},{2,3},{3,2},{4,5},{5,4},{6,7},{7,6},{8,9},{9,8},{10,11... | collective-permute-start | bytes 393224 | tf_op jit(solution)/shard_map/ppermute | solution.py:331
  4.9 7.3 %collective-permute-start.1 = (f32[2,4,4,4,256]{4,3,2,1,0:T(4,128)S(1)}, f32[2,4,4,4,256]{4,3,2,1,0:T(4,128)S(1)}, u32[]{:S(2)}, u32[]{:S(2)}) collective-permute-start(f32[2,4,4,4,256]{4,3,2,1,0:T(4,128)S(1)} %get-tuple-element.25), channel_id=1, source_target_pairs={{0,16},{1,2},{2,1},{3,4},{4,3},{5,6},{6,5},{7,23},{16,0},{17,18},{... | collective-permute-start | bytes 393224 | tf_op jit(solution)/shard_map/ppermute | solution.py:340
  12.2 1.4 %collective-permute-start.3 = (f32[2,4,4,4,256]{4,3,2,1,0:T(4,128)S(1)}, f32[2,4,4,4,256]{4,3,2,1,0:T(4,128)S(1)}, u32[]{:S(2)}, u32[]{:S(2)}) collective-permute-start(f32[2,4,4,4,256]{4,3,2,1,0:T(4,128)S(1)} %collective-permute-done.pair), channel_id=1, source_target_pairs={{0,8},{8,0},{1,9},{9,1},{2,10},{10,2},{3,11},{11,3},{4,12},{12,4},... | collective-permute-start | bytes 393224 | tf_op jit(solution)/shard_map/ppermute | solution.py:343
  12.3 1.5 %collective-permute-start.4 = (f32[2,4,4,4,256]{4,3,2,1,0:T(4,128)S(1)}, f32[2,4,4,4,256]{4,3,2,1,0:T(4,128)S(1)}, u32[]{:S(2)}, u32[]{:S(2)}) collective-permute-start(f32[2,4,4,4,256]{4,3,2,1,0:T(4,128)S(1)} %collective-permute-done.1.cross), channel_id=1, source_target_pairs={{0,8},{8,0},{1,9},{9,1},{2,10},{10,2},{3,11},{11,3},{4,12},{12,4},... | collective-permute-start | bytes 393224 | tf_op jit(solution)/shard_map/ppermute | solution.py:343
  15.2 7.8 %collective-permute-start.5 = (f32[2,4,4,4,256]{4,3,2,1,0:T(4,128)S(1)}, f32[2,4,4,4,256]{4,3,2,1,0:T(4,128)S(1)}, u32[]{:S(2)}, u32[]{:S(2)}) collective-permute-start(f32[2,4,4,4,256]{4,3,2,1,0:T(4,128)S(1)} %get-tuple-element.34), channel_id=1, source_target_pairs={{0,1},{1,0},{2,3},{3,2},{4,5},{5,4},{6,7},{7,6},{8,9},{9,8},{10,11... | collective-permute-start | bytes 393224 | tf_op jit(solution)/shard_map/ppermute | solution.py:331
  16.9 6.1 %collective-permute-start.6 = (f32[2,4,4,4,256]{4,3,2,1,0:T(4,128)S(1)}, f32[2,4,4,4,256]{4,3,2,1,0:T(4,128)S(1)}, u32[]{:S(2)}, u32[]{:S(2)}) collective-permute-start(f32[2,4,4,4,256]{4,3,2,1,0:T(4,128)S(1)} %get-tuple-element.35), channel_id=1, source_target_pairs={{0,16},{1,2},{2,1},{3,4},{4,3},{5,6},{6,5},{7,23},{16,0},{17,18},{... | collective-permute-start | bytes 393224 | tf_op jit(solution)/shard_map/ppermute | solution.py:340
  24.2 4.1 %collective-permute-start.7 = (f32[8,128]{1,0:T(8,128)S(1)}, f32[8,128]{1,0:T(8,128)S(1)}, u32[]{:S(2)}, u32[]{:S(2)}) collective-permute-start(f32[8,128]{1,0:T(8,128)S(1)} %get-tuple-element.45), channel_id=1, source_target_pairs={{0,1},{1,0},{2,3},{3,2},{4,5},{5,4},{6,7},{7,6},{8,9},{9,8},{10,11... | collective-permute-start | bytes 12296 | tf_op jit(solution)/shard_map/ppermute | solution.py:318
  28.3 3.7 %collective-permute-start.8 = (f32[8,128]{1,0:T(8,128)S(1)}, f32[8,128]{1,0:T(8,128)S(1)}, u32[]{:S(2)}, u32[]{:S(2)}) collective-permute-start(f32[8,128]{1,0:T(8,128)S(1)} %add.9), channel_id=1, source_target_pairs={{0,2},{1,3},{2,0},{3,1},{4,6},{5,7},{6,4},{7,5},{8,10},{9,11},{10,... | collective-permute-start | bytes 12296 | tf_op jit(solution)/shard_map/ppermute | solution.py:318
  31.9 4.6 %collective-permute-start.9 = (f32[8,128]{1,0:T(8,128)S(1)}, f32[8,128]{1,0:T(8,128)S(1)}, u32[]{:S(2)}, u32[]{:S(2)}) collective-permute-start(f32[8,128]{1,0:T(8,128)S(1)} %add.10), channel_id=1, source_target_pairs={{0,4},{1,5},{2,6},{3,7},{4,0},{5,1},{6,2},{7,3},{8,12},{9,13},{10,... | collective-permute-start | bytes 12296 | tf_op jit(solution)/shard_map/ppermute | solution.py:318

commit v5 on v4

--- a/solution.py
+++ b/solution.py
@@ -212,22 +212,14 @@
     ]
 
 
-def inner_late_kernel(dims, two, sums, three, zero, fields, sems):
+def inner_late_kernel(dims, two, sums, three, zero):
     members, levels, rows, halves, total_rows = dims
     first, second = inner_starts(rows)
-    middle = len(second) // 2
-    started = []
     for m in range(members):
         parts = []
         sweep(dims, two, three, m, first)
-        for part, starts in enumerate((second[:middle], second[middle:])):
-            sweep(dims, three, zero, m, starts, weighed(dims, parts))
-            for copy in result_copies(dims, zero, fields, sems, part, m, starts[0], len(starts) * TILE):
-                copy.start()
-                started.append(copy)
+        sweep(dims, three, zero, m, second, weighed(dims, parts))
         sums[m] = sum(parts)
-    for copy in started:
-        copy.wait()
 
 
 def surround(dims, buffer, m, near, far):
@@ -255,32 +247,37 @@
         sweep(dims, source, target, m, (start,), lambda f, l, h, start, value: jnp.where(beyond, 0.0, value))
 
 
-def outer_early_kernel(dims, pair, cross, other_pair, other_cross, mark, noise, zero_in, one_in, two_in,
-                       to_pair, to_cross, zero, one, two):
-    members, levels, rows, halves, total_rows = dims
+def outer_early_kernel(dims, facing, halo, other_halo, mark, noise, zero_in, one_in, two_in, to_next, zero, one, two):
+    members, levels, rows, halves, total_rows = dims
+    tile = lax.axis_index("tile")
+    low = lax.rem(tile, 2) == facing
+    limit = jnp.where(low, 0, lax.axis_size("tile") - 1)
+    row = lax.broadcasted_iota(jnp.int32, (TILE, LANES), 0)
+    side = jnp.where(low, row, TILE - 1 - row)
+    beyond = jnp.logical_and(tile == limit, side < REACH)
+
+    def at(below, above):
+        return jnp.where(low, below, above)
+
     for m in range(members):
         place = mark[m, :WIDTH, :]
-
-        def chosen(own, other):
-            def read(index):
-                value = own[(0, *index)]
-                for k in range(1, 2 * members):
-                    array = own if k < members else other
-                    value = jnp.where(place == k, array[(k % members, *index)], value)
-                return value
-
-            return read
-
-        surround(dims, zero, m, chosen(pair, other_pair), chosen(cross, other_cross))
-        outer_step(dims, zero, one, m)
-        sweep(dims, one, two, m, (TILE, rows), perturbed(noise, m))
-    split_edges(
-        dims,
-        lambda m, f, l, h: two[m, f, l, h, TILE : TILE + WIDTH, :],
-        lambda m, f, l, h: two[m, f, l, h, TILE + rows - WIDTH : TILE + rows, :],
-        to_pair,
-        to_cross,
-    )
+        for f in range(4):
+            for l in range(levels):
+                for h in range(halves):
+                    value = halo[0, f, l, :, half(h)]
+                    for k in range(1, 2 * members):
+                        array = halo if k < members else other_halo
+                        value = jnp.where(place == k, array[k % members, f, l, :, half(h)], value)
+                    value = jnp.where(tile == limit, 0.0, value)
+                    zero[m, f, l, h, pl.ds(at(TILE - WIDTH, TILE + rows), WIDTH), :] = value
+    for m in range(members):
+        sweep(dims, zero, one, m, (at(TILE - REACH, rows + REACH),),
+              lambda f, l, h, start, value: jnp.where(beyond, 0.0, value))
+        sweep(dims, one, two, m, (at(TILE, rows),), perturbed(noise, m))
+        for f in range(4):
+            for l in range(levels):
+                for h in range(halves):
+                    to_next[m, f, l, :, half(h)] = two[m, f, l, h, pl.ds(at(TILE, TILE + rows - WIDTH), WIDTH), :]
 
 
 def outer_late_kernel(dims, pair, cross, sums, two_in, three_in, zero_in, total, two, three, zero):
@@ -298,12 +295,11 @@
     total[...] = held
 
 
-def place_kernel(dims, zero, inner, fields, sems):
+def place_kernel(dims, zero, fields, sems):
     members, levels, rows, halves, total_rows = dims
     started = []
     for m in range(members):
-        for part, start in enumerate((TILE, rows)):
-            started += result_copies(dims, zero, fields, sems, part, m, start, TILE)
+        started += result_copies(dims, zero, fields, sems, 0, m, TILE, rows)
     for copy in started:
         copy.start()
     for copy in started:
@@ -313,10 +309,10 @@
 def tile_sum(value, count):
     if count & (count - 1):
         return lax.psum(value, "tile")
-    reach = 1
-    while reach < count:
+    reach = count // 2
+    while reach:
         value = value + lax.ppermute(value, "tile", [(i, i ^ reach) for i in range(count)])
-        reach *= 2
+        reach //= 2
     return value
 
 
@@ -386,25 +382,29 @@
     )(in_hbm(ancestors), in_hbm(state), other, in_hbm(perturbation))
     pair, cross, mark = lax.optimization_barrier((pair, cross, mark))
     other_pair, other_cross = to_member(pair), to_member(cross)
-    edge_pair, edge_cross, zero, one, two = pl.pallas_call(
-        functools.partial(outer_early_kernel, dims),
-        out_shape=(strip, strip) + (buffer,) * 3,
-        in_specs=[vmem] * 9,
-        out_specs=(vmem,) * 5,
-        input_output_aliases={6: 2, 7: 3, 8: 4},
-        compiler_params=params,
-        cost_estimate=cost(5),
-        name="outer_early",
-    )(pair, cross, other_pair, other_cross, mark, noise, zero, one, two)
-
-    pair, cross = to_pair(edge_pair), to_cross(edge_cross)
+
+    def outer_early(facing, halo, other_halo, zero, one, two):
+        return pl.pallas_call(
+            functools.partial(outer_early_kernel, dims, facing),
+            out_shape=(strip,) + (buffer,) * 3,
+            in_specs=[vmem] * 7,
+            out_specs=(vmem,) * 4,
+            input_output_aliases={4: 1, 5: 2, 6: 3},
+            compiler_params=params,
+            cost_estimate=cost(5),
+            name="outer_early",
+        )(halo, other_halo, mark, noise, zero, one, two)
+
+    edge_pair, zero, one, two = outer_early(1, pair, other_pair, zero, one, two)
+    pair = to_pair(edge_pair)
+    edge_cross, zero, one, two = outer_early(0, cross, other_cross, zero, one, two)
+    cross = to_cross(edge_cross)
     result = jax.ShapeDtypeStruct(state.shape, f32)
-    sums, three, zero, inner = pl.pallas_call(
+    sums, three, zero = pl.pallas_call(
         functools.partial(inner_late_kernel, dims),
-        out_shape=(tile, buffer, buffer, result),
+        out_shape=(tile, buffer, buffer),
         in_specs=[vmem],
-        out_specs=(vmem,) * 3 + (anywhere,),
-        scratch_shapes=[pltpu.SemaphoreType.DMA((2, members, halves))],
+        out_specs=(vmem,) * 3,
         compiler_params=params,
         cost_estimate=cost(20),
         name="inner_late",
@@ -423,14 +423,13 @@
     evolved = pl.pallas_call(
         functools.partial(place_kernel, dims),
         out_shape=result,
-        in_specs=[vmem, anywhere],
+        in_specs=[vmem],
         out_specs=anywhere,
-        scratch_shapes=[pltpu.SemaphoreType.DMA((2, members, halves))],
-        input_output_aliases={1: 0},
+        scratch_shapes=[pltpu.SemaphoreType.DMA((1, members, halves))],
         compiler_params=params,
         cost_estimate=cost(5),
         name="place",
-    )(zero, inner)
+    )(zero)
     observable = jnp.sum(tile_sum(total, count), axis=1)[:members]
     return evolved, observable
 

time: 37.3 us -> 36.5 us (0.979)
  Pallas kernels: 13.9 us -> 13.4 us
    pallas_call x1, Pallas kernels: 4.65 us -> 3.59 us  [body(): pl.pallas_call(functools.partial(inner_late_kernel, dims), out_shape=(til...]
    pallas_call x1, Pallas kernels: 0.85 us -> 1.34 us  [body(): pl.pallas_call(functools.partial(place_kernel, dims), out_shape=result, i...]
    ppermute x3, starting transfers between devices: 7.59 us -> 7.18 us  [tile_sum(): lax.ppermute(value, 'tile', [(i, i ^ reach) for i in range(count)])]
    pallas_call x1 -> x2, Pallas kernels: 1.35 us -> 1.46 us  [outer_early(): pl.pallas_call(functools.partial(outer_early_kernel, dims, facing), out_s...]
  transfers between devices with their start and end apart: 10 -> 10, of which waited for: 5 -> 5; matrix products, arithmetic and copies ran while one was open for 3% -> 3% of each run, Pallas kernels for 30% -> 34%
where the time goes in v5:
time: 36.5 us; the launch traced here: 36.3 us
  starting transfers between devices  15.6 us (43%)
  Pallas kernels  13.4 us (37%)
  waiting for transfers between devices  4.85 us (13%)
  local copies, waits for them, and re-layouts  1.08 us (3%)
  between operations  0.71 us (2%)
  other arithmetic  0.63 us (2%)
    ppermute x3, starting transfers between devices, tile_sum(): lax.ppermute(value, 'tile', [(i, i ^ reach) for i in range(count)])  7.18 us
    pallas_call x1, Pallas kernels, body(): pl.pallas_call(functools.partial(inner_early_kernel, dims), out_shape=(ja...  5.8 us
    ppermute x2, starting transfers between devices, to_pair(): return lax.ppermute(array, 'tile', [(i, i ^ 1) for i in range(count)])  4.31 us
    ppermute x3, waiting for transfers between devices, tile_sum(): lax.ppermute(value, 'tile', [(i, i ^ reach) for i in range(count)])  3.82 us
    pallas_call x1, Pallas kernels, body(): pl.pallas_call(functools.partial(inner_late_kernel, dims), out_shape=(til...  3.59 us
    ppermute x2, starting transfers between devices, to_cross(): return lax.ppermute(array, ('groups', 'tile'), pairs)  3.05 us
    pallas_call x2, Pallas kernels, outer_early(): pl.pallas_call(functools.partial(outer_early_kernel, dims, facing), out_s...  1.46 us
    pallas_call x1, Pallas kernels, body(): pl.pallas_call(functools.partial(place_kernel, dims), out_shape=result, i...  1.34 us
  transfers between devices with their start and end apart: 10, of which 5 were waited for; matrix products, arithmetic and copies ran while one was open for 3% of the time, Pallas kernels for 34%

profile of v5, /device:TPU:0, one launch (start us, length us, event | category | flops | bytes accessed | tf_op | source)
XLA Modules:
  0.0 36.3 jit_solution(8201092074626066904)
XLA Ops:
  0.6 0.5 %collective-permute-start.2 = (f32[2,4,4,64,256]{4,3,2,1,0:T(8,128)}, f32[2,4,4,64,256]{4,3,2,1,0:T(8,128)S(1)}, u32[]{:S(2)}, u32[]{:S(2)}) collective-permute-start(f32[2,4,4,64,256]{4,3,2,1,0:T(8,128)} %own.1), channel_id=1, source_target_pairs={{0,8},{8,0},{1,9},{9,1},{2,10},{10,2},{3,11},{11,3},{4,12},{12,4},... | collective-permute-start | bytes 6291464 | tf_op jit(solution)/shard_map/ppermute | solution.py:339
  1.1 1.1 %fusion = (f32[2,4,4,4,256]{4,3,2,1,0:T(4,128)S(1)}, f32[2,4,4,4,256]{4,3,2,1,0:T(4,128)S(1)}) fusion(f32[2,4,4,64,256]{4,3,2,1,0:T(8,128)} %own.1), kind=kLoop, calls=%fused_computation.1 | loop fusion | bytes 524288 | tf_op jit(solution)/shard_map/slice | solution.py:367
  2.2 0.1 edge.1
  2.3 2.6 %collective-permute-start = (f32[2,4,4,4,256]{4,3,2,1,0:T(4,128)S(1)}, f32[2,4,4,4,256]{4,3,2,1,0:T(4,128)S(1)}, u32[]{:S(2)}, u32[]{:S(2)}) collective-permute-start(f32[2,4,4,4,256]{4,3,2,1,0:T(4,128)S(1)} %get-tuple-element.26), channel_id=1, source_target_pairs={{0,1},{1,0},{2,3},{3,2},{4,5},{5,4},{6,7},{7,6},{8,9},{9,8},{10,11... | collective-permute-start | bytes 393224 | tf_op jit(solution)/shard_map/ppermute | solution.py:327
  4.9 1.5 %collective-permute-start.1 = (f32[2,4,4,4,256]{4,3,2,1,0:T(4,128)S(1)}, f32[2,4,4,4,256]{4,3,2,1,0:T(4,128)S(1)}, u32[]{:S(2)}, u32[]{:S(2)}) collective-permute-start(f32[2,4,4,4,256]{4,3,2,1,0:T(4,128)S(1)} %get-tuple-element.27), channel_id=1, source_target_pairs={{0,16},{1,2},{2,1},{3,4},{4,3},{5,6},{6,5},{7,23},{16,0},{17,18},{... | collective-permute-start | bytes 393224 | tf_op jit(solution)/shard_map/ppermute | solution.py:336
  6.4 0.0 collective-permute-done.2.other
  6.4 5.8 %inner_early.1 = (s32[2,8,128]{2,1,0:T(8,128)S(1)}, f32[2,4,4,2,80,128]{5,4,3,2,1,0:T(8,128)S(1)}, f32[2,4,4,2,80,128]{5,4,3,2,1,0:T(8,128)S(1)}, f32[2,4,4,2,80...) custom-call(s32[4]{0:T(128)} %ancestors_in.1, f32[2,4,4,64,256]{4,3,2,1,0:T(8,128)} %own.1, ...), custom_call_target="tpu_custom_call" | custom-call | flops 10485760 | bytes 10485760 | tf_op jit(solution)/shard_map/inner_early/pallas_call | solution.py:369
  12.2 0.0 collective-permute-done.halo
  12.2 0.0 collective-permute-done.1.halo
  12.2 0.1 collective-permute-start.3
  12.3 0.5 %collective-permute-start.5 = (f32[2,4,4,4,256]{4,3,2,1,0:T(4,128)S(1)}, f32[2,4,4,4,256]{4,3,2,1,0:T(4,128)S(1)}, u32[]{:S(2)}, u32[]{:S(2)}) collective-permute-start(f32[2,4,4,4,256]{4,3,2,1,0:T(4,128)S(1)} %collective-permute-done.1.halo), channel_id=1, source_target_pairs={{0,8},{8,0},{1,9},{9,1},{2,10},{10,2},{3,11},{11,3},{4,12},{12,4},... | collective-permute-start | bytes 393224 | tf_op jit(solution)/shard_map/ppermute | solution.py:339
  12.8 0.8 %collective-permute-done.3.other_halo = f32[2,4,4,4,256]{4,3,2,1,0:T(4,128)S(1)} collective-permute-done((f32[2,4,4,4,256]{4,3,2,1,0:T(4,128)S(1)}, f32[2,4,4,4,256]{4,3,2,1,0:T(4,128)S(1)}, u32[]{:S(2)}, u32[]{:S(2)}) %collective-permute-start.3) | collective-permute-done | bytes 131104 | tf_op jit(solution)/shard_map/ppermute | solution.py:339
  13.6 0.7 %outer_early.2 = (f32[2,4,4,4,256]{4,3,2,1,0:T(4,128)S(1)}, f32[2,4,4,2,80,128]{5,4,3,2,1,0:T(8,128)S(1)}, f32[2,4,4,2,80,128]{5,4,3,2,1,0:T(8,128)S(1)}, f32[2,4,4,2,80,128]{5,4,3,2,1,0:T(8,128)S(1)}) custom-call(f32[2,4,4,4,256]{4,3,2,1,0:T(4,128)S(1)} %collective-permute-done.halo, ...), custom_call_target="tpu_custom_call", output_to_operand_aliasing={{1}: (4, {}), {2}: (5, {}), {3}: (6, {})} | custom-call | flops 2621440 | bytes 2621440 | tf_op jit(solution)/shard_map/outer_early/pallas_call | solution.py:387
  14.4 1.7 %collective-permute-start.4 = (f32[2,4,4,4,256]{4,3,2,1,0:T(4,128)S(1)}, f32[2,4,4,4,256]{4,3,2,1,0:T(4,128)S(1)}, u32[]{:S(2)}, u32[]{:S(2)}) collective-permute-start(f32[2,4,4,4,256]{4,3,2,1,0:T(4,128)S(1)} %get-tuple-element.35), channel_id=1, source_target_pairs={{0,1},{1,0},{2,3},{3,2},{4,5},{5,4},{6,7},{7,6},{8,9},{9,8},{10,11... | collective-permute-start | bytes 393224 | tf_op jit(solution)/shard_map/ppermute | solution.py:327
  16.1 0.0 collective-permute-done.5.other_halo
  16.1 0.7 %outer_early.3 = (f32[2,4,4,4,256]{4,3,2,1,0:T(4,128)S(1)}, f32[2,4,4,2,80,128]{5,4,3,2,1,0:T(8,128)S(1)}, f32[2,4,4,2,80,128]{5,4,3,2,1,0:T(8,128)S(1)}, f32[2,4,4,2,80,128]{5,4,3,2,1,0:T(8,128)S(1)}) custom-call(f32[2,4,4,4,256]{4,3,2,1,0:T(4,128)S(1)} %collective-permute-done.1.halo, ...), custom_call_target="tpu_custom_call", output_to_operand_aliasing={{1}: (4, {}), {2}: (5, {}), {3}: (6, {})} | custom-call | flops 2621440 | bytes 2621440 | tf_op jit(solution)/shard_map/outer_early/pallas_call | solution.py:387
  16.8 1.6 %collective-permute-start.6 = (f32[2,4,4,4,256]{4,3,2,1,0:T(4,128)S(1)}, f32[2,4,4,4,256]{4,3,2,1,0:T(4,128)S(1)}, u32[]{:S(2)}, u32[]{:S(2)}) collective-permute-start(f32[2,4,4,4,256]{4,3,2,1,0:T(4,128)S(1)} %get-tuple-element.40), channel_id=1, source_target_pairs={{0,16},{1,2},{2,1},{3,4},{4,3},{5,6},{6,5},{7,23},{16,0},{17,18},{... | collective-permute-start | bytes 393224 | tf_op jit(solution)/shard_map/ppermute | solution.py:336
  18.4 3.6 %inner_late.1 = (f32[2,8,128]{2,1,0:T(8,128)S(1)}, f32[2,4,4,2,80,128]{5,4,3,2,1,0:T(8,128)S(1)}, f32[2,4,4,2,80,128]{5,4,3,2,1,0:T(8,128)S(1)}) custom-call(f32[2,4,4,2,80,128]{5,4,3,2,1,0:T(8,128)S(1)} %get-tuple-element.41.two.two_in), custom_call_target="tpu_custom_call" | custom-call | flops 10485760 | bytes 10485760 | tf_op jit(solution)/shard_map/inner_late/pallas_call | solution.py:403
  22.0 0.0 collective-permute-done.4.pair
  22.0 0.2 collective-permute-done.6.cross
  22.1 1.2 %outer_late.1 = (f32[8,128]{1,0:T(8,128)S(1)}, f32[2,4,4,2,80,128]{5,4,3,2,1,0:T(8,128)S(1)}, f32[2,4,4,2,80,128]{5,4,3,2,1,0:T(8,128)S(1)}, f32[2,4,4,2,80,128]{5,4,3,2,1,0:T(8,128)S(1)}) custom-call(f32[2,4,4,4,256]{4,3,2,1,0:T(4,128)S(1)} %collective-permute-done.4.pair, ...), custom_call_target="tpu_custom_call", output_to_operand_aliasing={{1}: (3, {}), {2}: (4, {}), {3}: (5, {})} | custom-call | flops 2621440 | bytes 2621440 | tf_op jit(solution)/shard_map/outer_late/pallas_call | solution.py:413
  23.3 3.6 %collective-permute-start.7 = (f32[8,128]{1,0:T(8,128)S(1)}, f32[8,128]{1,0:T(8,128)S(1)}, u32[]{:S(2)}, u32[]{:S(2)}) collective-permute-start(f32[8,128]{1,0:T(8,128)S(1)} %get-tuple-element.49), channel_id=1, source_target_pairs={{0,4},{1,5},{2,6},{3,7},{4,0},{5,1},{6,2},{7,3},{8,12},{9,13},{10,... | collective-permute-start | bytes 12296 | tf_op jit(solution)/shard_map/ppermute | solution.py:314
  26.9 1.6 %collective-permute-done.7 = f32[8,128]{1,0:T(8,128)S(1)} collective-permute-done((f32[8,128]{1,0:T(8,128)S(1)}, f32[8,128]{1,0:T(8,128)S(1)}, u32[]{:S(2)}, u32[]{:S(2)}) %collective-permute-start.7) | collective-permute-done | bytes 4128 | tf_op jit(solution)/shard_map/ppermute | solution.py:314
  28.5 1.9 %collective-permute-start.8 = (f32[8,128]{1,0:T(8,128)S(1)}, f32[8,128]{1,0:T(8,128)S(1)}, u32[]{:S(2)}, u32[]{:S(2)}) collective-permute-start(f32[8,128]{1,0:T(8,128)S(1)} %add.9), channel_id=1, source_target_pairs={{0,2},{1,3},{2,0},{3,1},{4,6},{5,7},{6,4},{7,5},{8,10},{9,11},{10,... | collective-permute-start | bytes 12296 | tf_op jit(solution)/shard_map/ppermute | solution.py:314
  30.4 1.7 %collective-permute-done.8 = f32[8,128]{1,0:T(8,128)S(1)} collective-permute-done((f32[8,128]{1,0:T(8,128)S(1)}, f32[8,128]{1,0:T(8,128)S(1)}, u32[]{:S(2)}, u32[]{:S(2)}) %collective-permute-start.8) | collective-permute-done | bytes 4128 | tf_op jit(solution)/shard_map/ppermute | solution.py:314
  32.1 1.7 %collective-permute-start.9 = (f32[8,128]{1,0:T(8,128)S(1)}, f32[8,128]{1,0:T(8,128)S(1)}, u32[]{:S(2)}, u32[]{:S(2)}) collective-permute-start(f32[8,128]{1,0:T(8,128)S(1)} %add.10), channel_id=1, source_target_pairs={{0,1},{1,0},{2,3},{3,2},{4,5},{5,4},{6,7},{7,6},{8,9},{9,8},{10,11... | collective-permute-start | bytes 12296 | tf_op jit(solution)/shard_map/ppermute | solution.py:314
  33.8 1.3 %place.1 = f32[2,4,4,64,256]{4,3,2,1,0:T(8,128)} custom-call(f32[2,4,4,2,80,128]{5,4,3,2,1,0:T(8,128)S(1)} %get-tuple-element.48.zero), custom_call_target="tpu_custom_call" | custom-call | flops 2621440 | bytes 2621440 | tf_op jit(solution)/shard_map/place/pallas_call | solution.py:423
  35.2 0.5 %collective-permute-done.9 = f32[8,128]{1,0:T(8,128)S(1)} collective-permute-done((f32[8,128]{1,0:T(8,128)S(1)}, f32[8,128]{1,0:T(8,128)S(1)}, u32[]{:S(2)}, u32[]{:S(2)}) %collective-permute-start.9) | collective-permute-done | bytes 4128 | tf_op jit(solution)/shard_map/ppermute | solution.py:314
  35.7 0.6 %add_reduce_fusion = f32[8]{0:T(128)} fusion(f32[8,128]{1,0:T(8,128)S(1)} %add.10, f32[8,128]{1,0:T(8,128)S(1)} %collective-permute-done.9), kind=kLoop, calls=%fused_computation | loop fusion | flops 2040 | bytes 8224 | tf_op jit(solution)/shard_map/reduce_sum | solution.py:433
  (2 shorter events, 0.0 us)
Async XLA Ops:
  0.6 5.8 %collective-permute-start.2 = (f32[2,4,4,64,256]{4,3,2,1,0:T(8,128)}, f32[2,4,4,64,256]{4,3,2,1,0:T(8,128)S(1)}, u32[]{:S(2)}, u32[]{:S(2)}) collective-permute-start(f32[2,4,4,64,256]{4,3,2,1,0:T(8,128)} %own.1), channel_id=1, source_target_pairs={{0,8},{8,0},{1,9},{9,1},{2,10},{10,2},{3,11},{11,3},{4,12},{12,4},... | collective-permute-start | bytes 6291464 | tf_op jit(solution)/shard_map/ppermute | solution.py:339
  2.3 9.9 %collective-permute-start = (f32[2,4,4,4,256]{4,3,2,1,0:T(4,128)S(1)}, f32[2,4,4,4,256]{4,3,2,1,0:T(4,128)S(1)}, u32[]{:S(2)}, u32[]{:S(2)}) collective-permute-start(f32[2,4,4,4,256]{4,3,2,1,0:T(4,128)S(1)} %get-tuple-element.26), channel_id=1, source_target_pairs={{0,1},{1,0},{2,3},{3,2},{4,5},{5,4},{6,7},{7,6},{8,9},{9,8},{10,11... | collective-permute-start | bytes 393224 | tf_op jit(solution)/shard_map/ppermute | solution.py:327
  4.9 7.3 %collective-permute-start.1 = (f32[2,4,4,4,256]{4,3,2,1,0:T(4,128)S(1)}, f32[2,4,4,4,256]{4,3,2,1,0:T(4,128)S(1)}, u32[]{:S(2)}, u32[]{:S(2)}) collective-permute-start(f32[2,4,4,4,256]{4,3,2,1,0:T(4,128)S(1)} %get-tuple-element.27), channel_id=1, source_target_pairs={{0,16},{1,2},{2,1},{3,4},{4,3},{5,6},{6,5},{7,23},{16,0},{17,18},{... | collective-permute-start | bytes 393224 | tf_op jit(solution)/shard_map/ppermute | solution.py:336
  12.2 1.4 %collective-permute-start.3 = (f32[2,4,4,4,256]{4,3,2,1,0:T(4,128)S(1)}, f32[2,4,4,4,256]{4,3,2,1,0:T(4,128)S(1)}, u32[]{:S(2)}, u32[]{:S(2)}) collective-permute-start(f32[2,4,4,4,256]{4,3,2,1,0:T(4,128)S(1)} %collective-permute-done.halo), channel_id=1, source_target_pairs={{0,8},{8,0},{1,9},{9,1},{2,10},{10,2},{3,11},{11,3},{4,12},{12,4},... | collective-permute-start | bytes 393224 | tf_op jit(solution)/shard_map/ppermute | solution.py:339
  12.3 3.8 %collective-permute-start.5 = (f32[2,4,4,4,256]{4,3,2,1,0:T(4,128)S(1)}, f32[2,4,4,4,256]{4,3,2,1,0:T(4,128)S(1)}, u32[]{:S(2)}, u32[]{:S(2)}) collective-permute-start(f32[2,4,4,4,256]{4,3,2,1,0:T(4,128)S(1)} %collective-permute-done.1.halo), channel_id=1, source_target_pairs={{0,8},{8,0},{1,9},{9,1},{2,10},{10,2},{3,11},{11,3},{4,12},{12,4},... | collective-permute-start | bytes 393224 | tf_op jit(solution)/shard_map/ppermute | solution.py:339
  14.4 7.6 %collective-permute-start.4 = (f32[2,4,4,4,256]{4,3,2,1,0:T(4,128)S(1)}, f32[2,4,4,4,256]{4,3,2,1,0:T(4,128)S(1)}, u32[]{:S(2)}, u32[]{:S(2)}) collective-permute-start(f32[2,4,4,4,256]{4,3,2,1,0:T(4,128)S(1)} %get-tuple-element.35), channel_id=1, source_target_pairs={{0,1},{1,0},{2,3},{3,2},{4,5},{5,4},{6,7},{7,6},{8,9},{9,8},{10,11... | collective-permute-start | bytes 393224 | tf_op jit(solution)/shard_map/ppermute | solution.py:327
  16.8 5.3 %collective-permute-start.6 = (f32[2,4,4,4,256]{4,3,2,1,0:T(4,128)S(1)}, f32[2,4,4,4,256]{4,3,2,1,0:T(4,128)S(1)}, u32[]{:S(2)}, u32[]{:S(2)}) collective-permute-start(f32[2,4,4,4,256]{4,3,2,1,0:T(4,128)S(1)} %get-tuple-element.40), channel_id=1, source_target_pairs={{0,16},{1,2},{2,1},{3,4},{4,3},{5,6},{6,5},{7,23},{16,0},{17,18},{... | collective-permute-start | bytes 393224 | tf_op jit(solution)/shard_map/ppermute | solution.py:336
  23.3 5.1 %collective-permute-start.7 = (f32[8,128]{1,0:T(8,128)S(1)}, f32[8,128]{1,0:T(8,128)S(1)}, u32[]{:S(2)}, u32[]{:S(2)}) collective-permute-start(f32[8,128]{1,0:T(8,128)S(1)} %get-tuple-element.49), channel_id=1, source_target_pairs={{0,4},{1,5},{2,6},{3,7},{4,0},{5,1},{6,2},{7,3},{8,12},{9,13},{10,... | collective-permute-start | bytes 12296 | tf_op jit(solution)/shard_map/ppermute | solution.py:314
  28.5 3.6 %collective-permute-start.8 = (f32[8,128]{1,0:T(8,128)S(1)}, f32[8,128]{1,0:T(8,128)S(1)}, u32[]{:S(2)}, u32[]{:S(2)}) collective-permute-start(f32[8,128]{1,0:T(8,128)S(1)} %add.9), channel_id=1, source_target_pairs={{0,2},{1,3},{2,0},{3,1},{4,6},{5,7},{6,4},{7,5},{8,10},{9,11},{10,... | collective-permute-start | bytes 12296 | tf_op jit(solution)/shard_map/ppermute | solution.py:314
  32.1 3.6 %collective-permute-start.9 = (f32[8,128]{1,0:T(8,128)S(1)}, f32[8,128]{1,0:T(8,128)S(1)}, u32[]{:S(2)}, u32[]{:S(2)}) collective-permute-start(f32[8,128]{1,0:T(8,128)S(1)} %add.10), channel_id=1, source_target_pairs={{0,1},{1,0},{2,3},{3,2},{4,5},{5,4},{6,7},{7,6},{8,9},{9,8},{10,11... | collective-permute-start | bytes 12296 | tf_op jit(solution)/shard_map/ppermute | solution.py:314
